TPU v7x, 128 devices: a whole 4x4x4 slice. The times are simulated.
128 devices in a mesh: mx: 8 (over x, core), my: 16 (over y, z).
Axes of the slice: x: 4, y: 4, z: 4, core: 2. Of those that a mesh axis runs over, the one named last changes fastest.
Arguments:
- lanczos_block: float32 [16, 64, 2048], P(None, 'mx', 'my'), may hold values from -6 to 6
- previous_block: float32 [16, 64, 2048], P(None, 'mx', 'my'), may hold values from -6 to 6
- previous_beta: float32 [16, 16], replicated, may hold values from -2 to 2
- prior_reaction: float32 [64, 2048], P('mx', 'my'), may hold values from 0.02 to 0.5
- vert_coupling: float32 [15, 64, 2048], P(None, 'mx', 'my'), may hold values from 2 to 20
- horiz_coupling: float32 [16, 64, 2048], P(None, 'mx', 'my'), may hold values from 0.05 to 0.25
- friction: float32 [64, 2048], P('mx', 'my'), may hold values from 0.5 to 2
- base_velocity: float32 [2, 64, 2048], P(None, 'mx', 'my'), may hold values from -4 to 4
- layers: int32 [64, 2048], P('mx', 'my'), may hold values from 1 to 16
- obs_dest: int32 [32768, 1], P(('mx', 'my')), may hold values from 0 to 127; in each aligned block of 256 rows (0 to 255, 256 to 511, ...) at most 4 rows name the same one
- obs_cell: int32 [32768], P(('mx', 'my')), may hold values from 0 to 1023
- obs_weight: float32 [32768, 2], P(('mx', 'my')), may hold values from 40 to 400
Outputs:
- next_block: float32 [16, 64, 2048], P(None, 'mx', 'my')
- block_alpha: float32 [16, 16], replicated
- block_beta: float32 [16, 16], replicated
Inputs may be any that keep to these rules, and one draw needn't show every extreme that they name: `obs_dest`: within the rows of one device, no device index appears more than 4 times, and some index appears exactly 4 times.
All inputs are finite; a program needn't handle non-finite values.
Results may differ from a plain program's by a relative error of at most 0.0002.
Values sent between devices are 32-bit elements; how exact they have to be, the bound alone decides.
No kernel may reach another device: no remote copies, remote signals or barrier semaphores. Data moves between devices by JAX's collectives and lax.ppermute only.
A program may use at most 64 MiB of HBM per device.

v0:
```python
import jax
import jax.numpy as jnp
from jax import lax
from jax.sharding import PartitionSpec as P

SWEEPS = 3
PRIOR_ITERS = 3


base_damping = 0.02
highest = lax.Precision.HIGHEST


def with_halo(cells, sides, width):
    for axis, dim in sides:
        count = lax.axis_size(axis)
        ends = count - 1
        head = lax.slice_in_dim(cells, 0, width, axis=dim)
        tail = lax.slice_in_dim(cells, cells.shape[dim] - width, cells.shape[dim], axis=dim)
        cells = jnp.concatenate(
            [
                lax.ppermute(tail, axis, [(i, (i + 1) % count) for i in range(ends)]),
                cells,
                lax.ppermute(head, axis, [((i + 1) % count, i) for i in range(ends)]),
            ],
            axis=dim,
        )
    return cells


def neighbour_sum(padded):
    return (
        padded[..., 2:, 1:-1]
        + padded[..., :-2, 1:-1]
        + padded[..., 1:-1, 2:]
        + padded[..., 1:-1, :-2]
    )


def column_neighbours(grid_field):
    return neighbour_sum(with_halo(grid_field, (("mx", 3), ("my", 4)), 1))


def prior_neighbours(grid_field):
    return neighbour_sum(with_halo(grid_field, (("mx", 1), ("my", 2)), 1))


def cell_sums(values):
    return lax.psum(jnp.sum(values, axis=(1, 2)), ("mx", "my"))


def top_layer(active):
    return active - jnp.concatenate([active[1:], jnp.zeros_like(active[:1])], axis=0)


def column_factors(vert_coupling, horiz_coupling, friction, active):
    coupling_up = vert_coupling * active[1:]
    lateral = horiz_coupling * active
    zero_row = jnp.zeros_like(coupling_up[:1])
    from_below = jnp.concatenate([zero_row, coupling_up], axis=0)
    from_above = jnp.concatenate([coupling_up, zero_row], axis=0)
    bed_drag = jnp.concatenate([friction[None], jnp.zeros_like(lateral[1:])], axis=0)
    diagonal = (base_damping + lateral + from_below + from_above + bed_drag) * active + (
        1.0 - active
    )
    pivot_list = [diagonal[0]]
    for layer_idx in range(1, diagonal.shape[0]):
        pivot_list.append(
            diagonal[layer_idx]
            - coupling_up[layer_idx - 1] * coupling_up[layer_idx - 1] / pivot_list[layer_idx - 1]
        )
    pivots = jnp.stack(pivot_list, axis=0)
    ratios = coupling_up / pivots[:-1]
    return (coupling_up, lateral, ratios, pivots)


def column_solve(source, coupling_up, ratios, pivots):
    layer_count = pivots.shape[0]
    carried = [source[..., 0, :, :]]
    for layer_idx in range(1, layer_count):
        carried.append(
            source[..., layer_idx, :, :] + ratios[layer_idx - 1] * carried[layer_idx - 1]
        )
    solved = [carried[layer_count - 1] / pivots[layer_count - 1]]
    for layer_idx in range(layer_count - 2, -1, -1):
        solved.append(
            (carried[layer_idx] + coupling_up[layer_idx] * solved[-1]) / pivots[layer_idx]
        )
    return jnp.stack(solved[::-1], axis=-3)


def column_map(source, factors, neighbours):
    coupling_up, lateral, ratios, pivots = factors
    iterate = column_solve(source, coupling_up, ratios, pivots)
    for sweep_idx in range(SWEEPS):
        iterate = column_solve(
            source + lateral * neighbours(lateral * iterate), coupling_up, ratios, pivots
        )
    return iterate


def prior_solve(right_side, reaction):
    solution = jnp.zeros_like(right_side)
    residual = right_side
    search = right_side
    norm_now = cell_sums(residual * residual)
    for iter_idx in range(PRIOR_ITERS):
        applied_dir = (reaction + 4.0) * search - prior_neighbours(search)
        step_size = norm_now / cell_sums(search * applied_dir)
        solution = solution + step_size[:, None, None] * search
        residual = residual - step_size[:, None, None] * applied_dir
        if iter_idx + 1 < PRIOR_ITERS:
            norm_next = cell_sums(residual * residual)
            search = residual + (norm_next / norm_now)[:, None, None] * search
            norm_now = norm_next
    return solution


def shards(
    lanczos_block,
    previous_block,
    previous_beta,
    prior_reaction,
    vert_coupling,
    horiz_coupling,
    friction,
    base_velocity,
    layers,
    obs_dest,
    obs_cell,
    obs_weight,
):
    block_size, tile_x, tile_y = lanczos_block.shape
    layer_total = horiz_coupling.shape[0]
    cell_count = tile_x * tile_y
    devices = lax.axis_size("mx") * lax.axis_size("my")
    cell_total = cell_count * devices
    layer_ids = jnp.arange(layer_total, dtype=jnp.int32)[:, None, None]
    active = (layer_ids < layers[None]).astype(jnp.float32)
    obs_rows = obs_cell.shape[0]
    capacity = (2 * obs_rows + devices - 1) // devices
    target = obs_dest[:, 0]
    onehot = (target[:, None] == jnp.arange(devices, dtype=jnp.int32)[None, :]).astype(jnp.float32)
    row_ids = jnp.arange(obs_rows, dtype=jnp.int32)
    lower_ones = (row_ids[:, None] >= row_ids[None, :]).astype(jnp.float32)
    running = jnp.dot(lower_ones, onehot, precision=highest)
    slot_rank = jnp.sum(running * onehot, axis=1).astype(jnp.int32) - 1
    slot_index = target * capacity + slot_rank
    request = jnp.full((devices * capacity,), cell_count, jnp.int32).at[slot_index].set(obs_cell)
    received = lax.all_to_all(
        request.reshape(devices, capacity), ("mx", "my"), split_axis=0, concat_axis=0, tiled=True
    ).reshape(devices * capacity)
    slot_weight = (
        jnp.zeros((2, devices * capacity), jnp.float32)
        .at[:, slot_index]
        .set(jnp.transpose(obs_weight))
    )
    smoothed = prior_solve(lanczos_block, prior_reaction)
    factors = column_factors(vert_coupling, horiz_coupling, friction, active)
    bed_factor = friction * base_velocity
    bed_onehot = (layer_ids == 0).astype(jnp.float32)
    bed_source = (bed_factor * smoothed[:, None])[:, :, None] * bed_onehot
    velocity = column_map(bed_source, factors, column_neighbours)
    surface = jnp.sum(velocity * top_layer(active)[None, None], axis=2)
    flat_surface = surface.reshape(block_size * 2, cell_count)
    with_blank = jnp.concatenate(
        [flat_surface, jnp.zeros((block_size * 2, 1), jnp.float32)], axis=1
    )
    picked = jnp.take(with_blank, received, axis=1)
    returned = lax.all_to_all(
        picked.reshape(block_size * 2, devices, capacity),
        ("mx", "my"),
        split_axis=1,
        concat_axis=1,
        tiled=True,
    )
    weighted = returned.reshape(block_size, 2, devices * capacity) * slot_weight[None]
    misfit_sent = lax.all_to_all(
        weighted.reshape(block_size * 2, devices, capacity),
        ("mx", "my"),
        split_axis=1,
        concat_axis=1,
        tiled=True,
    )
    misfit_table = (
        jnp.zeros((block_size * 2, cell_count + 1), jnp.float32)
        .at[:, received]
        .add(misfit_sent.reshape(block_size * 2, devices * capacity))
    )
    misfit = misfit_table[:, :cell_count].reshape(block_size, 2, tile_x, tile_y)
    adjoint = column_map(
        misfit[:, :, None] * top_layer(active)[None, None], factors, column_neighbours
    )
    pulled = jnp.sum(bed_factor * adjoint[:, :, 0], axis=1)
    applied = prior_solve(pulled, prior_reaction)
    applied_rows = applied.reshape(block_size, cell_count)
    basis_rows = lanczos_block.reshape(block_size, cell_count)
    prior_rows = previous_block.reshape(block_size, cell_count)
    residual_rows = applied_rows - jnp.dot(previous_beta, prior_rows, precision=highest)
    block_alpha = (
        lax.psum(jnp.dot(basis_rows, jnp.transpose(residual_rows), precision=highest), ("mx", "my"))
        / cell_total
    )
    projected = residual_rows - jnp.dot(jnp.transpose(block_alpha), basis_rows, precision=highest)
    gram_matrix = (
        lax.psum(jnp.dot(projected, jnp.transpose(projected), precision=highest), ("mx", "my"))
        / cell_total
    )
    factor = jnp.linalg.cholesky(gram_matrix)
    next_rows = jax.scipy.linalg.solve_triangular(factor, projected, lower=True)
    return (next_rows.reshape(block_size, tile_x, tile_y), block_alpha, jnp.transpose(factor))


def solution(mesh):
    in_specs = (
        P(None, "mx", "my"),
        P(None, "mx", "my"),
        P(),
        P("mx", "my"),
        P(None, "mx", "my"),
        P(None, "mx", "my"),
        P("mx", "my"),
        P(None, "mx", "my"),
        P("mx", "my"),
        P(("mx", "my"), None),
        P(("mx", "my")),
        P(("mx", "my"), None),
    )
    out_specs = (P(None, "mx", "my"), P(), P())
    return jax.shard_map(shards, mesh=mesh, in_specs=in_specs, out_specs=out_specs, check_vma=False)
```

profile of v0, /device:TPU:0, one launch (start us, length us, event | category | flops | bytes accessed | tf_op | source)
XLA Modules:
  0.0 1249.2 jit_solution(694511709183301746)
XLA Ops:
  20.7 72.0 %all-reduce.6 = (f32[16]{0:T(128)S(1)}, f32[16]{0:T(128)S(1)}) all-reduce(f32[16]{0:T(128)S(1)} %get-tuple-element.24, f32[16]{0:T(128)S(1)} %get-tuple-element.23), channel_id=1, replica_groups=mesh['mx'=8,'my'=16] {'mx','my'}, use_global_device_ids=true, to_apply=%region_3.0 | all-reduce | flops 32 | bytes 256 | tf_op jit(solution)/shard_map/psum | solution.py:49
  93.0 62.5 %psum.100 = f32[16]{0:T(128)S(1)} all-reduce(f32[16]{0:T(128)S(1)} %get-tuple-element.164), channel_id=1, replica_groups=mesh['mx'=8,'my'=16] {'mx','my'}, use_global_device_ids=true, to_apply=%region_7.0 | all-reduce | flops 16 | bytes 128 | tf_op jit(solution)/shard_map/psum | solution.py:49
  170.8 67.9 %psum.101 = f32[16]{0:T(128)S(1)} all-reduce(f32[16]{0:T(128)S(1)} %get-tuple-element.162), channel_id=1, replica_groups=mesh['mx'=8,'my'=16] {'mx','my'}, use_global_device_ids=true, to_apply=%region_9.0 | all-reduce | flops 16 | bytes 128 | tf_op jit(solution)/shard_map/psum | solution.py:49
  239.1 62.3 %psum.102 = f32[16]{0:T(128)S(1)} all-reduce(f32[16]{0:T(128)S(1)} %multiply_reduce_fusion.7), channel_id=1, replica_groups=mesh['mx'=8,'my'=16] {'mx','my'}, use_global_device_ids=true, to_apply=%region_11.0 | all-reduce | flops 16 | bytes 128 | tf_op jit(solution)/shard_map/psum | solution.py:49
  316.8 68.1 %psum.103 = f32[16]{0:T(128)S(1)} all-reduce(f32[16]{0:T(128)S(1)} %fusion.79), channel_id=1, replica_groups=mesh['mx'=8,'my'=16] {'mx','my'}, use_global_device_ids=true, to_apply=%region_13.0 | all-reduce | flops 16 | bytes 128 | tf_op jit(solution)/shard_map/psum | solution.py:49
  412.4 5.6 copy.123
  418.0 5.6 copy.125
  423.6 5.8 multiply_add_fusion.5
  460.2 24.1 %all_to_all.19 = s32[128,1,4]{2,1,0:T(1,128)S(1)} all-to-all(s32[128,1,4]{2,1,0:T(1,128)S(1)} %bitcast.388), channel_id=1, replica_groups=mesh['mx'=8,'my'=16] {'mx','my'}, dimensions={0} | all-to-all | bytes 4096 | tf_op jit(solution)/shard_map/all_to_all | solution.py:150
  485.7 5.6 copy.127
  491.3 5.6 copy.129
  496.9 5.8 multiply_add_fusion.4
  529.8 5.6 copy.131
  535.4 5.6 copy.133
  541.0 5.8 multiply_add_fusion.3
  550.2 10.5 all-to-all-start.1
  572.1 14.4 %all_to_all.20 = f32[128,1,128]{2,1,0:T(1,128)S(1)} all-to-all(f32[128,1,128]{2,1,0:T(1,128)S(1)} %reshape.1058), channel_id=1, replica_groups=mesh['mx'=8,'my'=16] {'mx','my'}, dimensions={0} | all-to-all | bytes 131072 | tf_op jit(solution)/shard_map/all_to_all | solution.py:178
  617.6 5.6 copy.142
  628.7 5.8 multiply_add_fusion.2
  663.8 5.6 copy.146
  675.0 5.8 multiply_add_fusion.1
  683.6 7.2 collective-permute-start.33
  712.3 5.6 copy.150
  723.5 5.8 multiply_add_fusion
  731.1 7.2 collective-permute-start.37
  748.0 73.8 %all-reduce.5 = (f32[16]{0:T(128)S(1)}, f32[16]{0:T(128)S(1)}) all-reduce(f32[16]{0:T(128)S(1)} %get-tuple-element.22, f32[16]{0:T(128)S(1)} %get-tuple-element.21), channel_id=1, replica_groups=mesh['mx'=8,'my'=16] {'mx','my'}, use_global_device_ids=true, to_apply=%region_19.20 | all-reduce | flops 32 | bytes 256 | tf_op jit(solution)/shard_map/psum | solution.py:49
  822.1 63.1 %psum.106 = f32[16]{0:T(128)S(1)} all-reduce(f32[16]{0:T(128)S(1)} %get-tuple-element.31), channel_id=1, replica_groups=mesh['mx'=8,'my'=16] {'mx','my'}, use_global_device_ids=true, to_apply=%region_23.24 | all-reduce | flops 16 | bytes 128 | tf_op jit(solution)/shard_map/psum | solution.py:49
  900.5 67.6 %psum.107 = f32[16]{0:T(128)S(1)} all-reduce(f32[16]{0:T(128)S(1)} %get-tuple-element.29), channel_id=1, replica_groups=mesh['mx'=8,'my'=16] {'mx','my'}, use_global_device_ids=true, to_apply=%region_25.26 | all-reduce | flops 16 | bytes 128 | tf_op jit(solution)/shard_map/psum | solution.py:49
  968.4 62.3 %psum.108 = f32[16]{0:T(128)S(1)} all-reduce(f32[16]{0:T(128)S(1)} %multiply_reduce_fusion.2), channel_id=1, replica_groups=mesh['mx'=8,'my'=16] {'mx','my'}, use_global_device_ids=true, to_apply=%region_27.28 | all-reduce | flops 16 | bytes 128 | tf_op jit(solution)/shard_map/psum | solution.py:49
  1046.1 68.4 %psum.109 = f32[16]{0:T(128)S(1)} all-reduce(f32[16]{0:T(128)S(1)} %fusion.65), channel_id=1, replica_groups=mesh['mx'=8,'my'=16] {'mx','my'}, use_global_device_ids=true, to_apply=%region_29.30 | all-reduce | flops 16 | bytes 128 | tf_op jit(solution)/shard_map/psum | solution.py:49
  1115.0 62.3 %psum.110 = f32[16,16]{0,1:T(8,128)S(1)} all-reduce(f32[16,16]{0,1:T(8,128)S(1)} %convolution_bitcast_fusion), channel_id=1, replica_groups=mesh['mx'=8,'my'=16] {'mx','my'}, use_global_device_ids=true, to_apply=%region_30.31 | all-reduce | flops 256 | bytes 2048 | tf_op jit(solution)/shard_map/psum | solution.py:201
  1177.7 64.7 %psum.111 = f32[16,16]{0,1:T(8,128)S(1)} all-reduce(f32[16,16]{0,1:T(8,128)S(1)} %fusion.149), channel_id=1, replica_groups=mesh['mx'=8,'my'=16] {'mx','my'}, use_global_device_ids=true, to_apply=%region_31.32 | all-reduce | flops 256 | bytes 2048 | tf_op jit(solution)/shard_map/psum | solution.py:206
  (387 shorter events, 302.5 us)
Async XLA Ops:
  1.6 7.0 collective-permute-start
  9.6 7.9 collective-permute-start.2
  10.9 8.3 collective-permute-start.3
  160.8 8.1 collective-permute-start.6
  162.1 8.3 collective-permute-start.7
  306.8 8.1 collective-permute-start.10
  308.1 8.3 collective-permute-start.11
  401.6 10.9 collective-permute-start.14
  407.2 10.8 collective-permute-start.15
  430.9 6.8 collective-permute-start.16
  447.6 38.1 %collective-permute-start.18 = (f32[16,2,16,10,1]{2,0,4,3,1:T(8,128)S(1)}, f32[16,2,16,10,1]{2,0,4,3,1:T(8,128)}, u32[]{:S(2)}, u32[]{:S(2)}) collective-permute-start(f32[16,2,16,10,1]{2,0,4,3,1:T(8,128)S(1)} %copy.126), channel_id=1, source_target_pairs={{1,0},{2,1},{3,2},{4,3},{5,4},{6,5},{7,6},{8,7},{9,8},{10,9},{11,1... | collective-permute-start | bytes 61448 | tf_op jit(solution)/shard_map/ppermute | solution.py:24
  453.3 38.0 %collective-permute-start.19 = (f32[16,2,16,10,1]{2,0,4,3,1:T(8,128)}, f32[16,2,16,10,1]{2,0,4,3,1:T(8,128)}, u32[]{:S(2)}, u32[]{:S(2)}) collective-permute-start(f32[16,2,16,10,1]{2,0,4,3,1:T(8,128)} %copy.128), channel_id=1, source_target_pairs={{0,1},{1,2},{2,3},{3,4},{4,5},{5,6},{6,7},{7,8},{8,9},{9,10},{10,1... | collective-permute-start | bytes 61448 | tf_op jit(solution)/shard_map/ppermute | solution.py:22
  518.9 10.9 collective-permute-start.22
  524.6 10.8 collective-permute-start.23
  550.2 19.9 %all-to-all-start.1 = ((f32[128,1,128]{2,1,0:T(1,128)}), f32[128,1,128]{2,1,0:T(1,128)S(1)}, u32[]{:S(2)}, u32[]{:S(2)}) async-start(f32[128,1,128]{2,1,0:T(1,128)} %reshape.1056), calls=%async_computation.1 | async-start | bytes 131072 | tf_op jit(solution)/shard_map/all_to_all | solution.py:170
  606.5 11.0 collective-permute-start.26
  612.2 11.0 collective-permute-start.27
  636.1 6.3 collective-permute-start.28
  652.8 11.1 collective-permute-start.30
  658.4 11.0 collective-permute-start.31
  682.3 8.5 collective-permute-start.32
  683.6 8.3 collective-permute-start.33
  701.2 11.1 collective-permute-start.34
  706.9 11.1 collective-permute-start.35
  729.8 8.5 collective-permute-start.36
  731.1 8.0 collective-permute-start.37
  739.2 6.9 collective-permute-start.38
  740.5 7.1 collective-permute-start.39
  890.6 8.2 collective-permute-start.42
  891.9 8.2 collective-permute-start.43
  1036.1 8.1 collective-permute-start.46
  1037.4 8.3 collective-permute-start.47
  (24 other events, 2285.3 us)
where the time goes:
time: 1260 us; the launch traced here: 1250 us
  blocking collectives  833 us (66%)
  local copies, waits for them, and re-layouts  162 us (13%)
  starting transfers between devices  150 us (12%)
  other arithmetic  64.7 us (5%)
  waiting for transfers between devices  34.6 us (3%)
    psum x10, blocking collectives, cell_sums(): return lax.psum(jnp.sum(values, axis=(1, 2)), ('mx', 'my'))  668 us
    ppermute x24, starting transfers between devices, with_halo(): lax.ppermute(tail, axis, [(i, (i + 1) % count) for i in range(ends)])  109 us
    psum x1, blocking collectives, shards(): lax.psum(jnp.dot(projected, jnp.transpose(projected), precision=highest),...  64.7 us
    psum x1, blocking collectives, shards(): lax.psum(jnp.dot(basis_rows, jnp.transpose(residual_rows), precision=high...  62.3 us
    slice x18, local copies, waits for them, and re-layouts, with_halo(): head = lax.slice_in_dim(cells, 0, width, axis=dim)  51.3 us
    add x6, other arithmetic, column_map(): source + lateral * neighbours(lateral * iterate)  34.9 us
    ppermute x6, local copies, waits for them, and re-layouts, with_halo(): lax.ppermute(head, axis, [((i + 1) % count, i) for i in range(ends)])  33.5 us
    ppermute x6, local copies, waits for them, and re-layouts, with_halo(): lax.ppermute(tail, axis, [(i, (i + 1) % count) for i in range(ends)])  33.4 us
  transfers between devices with their start and end apart: 49, of which 24 were waited for; matrix products, arithmetic and copies ran while one was open for 6% of the time, Pallas kernels for 0%

commit v1 on v0

v1 whole, which is shorter than its diff:
```python
import functools

import jax
import jax.numpy as jnp
from jax import lax
from jax.experimental import pallas as pl
from jax.experimental.pallas import tpu as pltpu
from jax.sharding import PartitionSpec as P

base_damping = 0.02
highest = lax.Precision.HIGHEST
SHIFT = 4.25
SCALE = 4.25
LANES = 128
HALO = 8
AXES = ("mx", "my")
VMEM_LIMIT = 56 * 1024 * 1024

F_RATIO = 0
F_PIVOT = 15
F_INV_LAT = 31
F_TOP = 32
F_LAYER = 33
F_BED = 34
F_REACT = 36
FIELDS = 37


def params():
    return pltpu.CompilerParams(vmem_limit_bytes=VMEM_LIMIT)


def lane_ids(shape):
    return lax.broadcasted_iota(jnp.int32, shape, len(shape) - 1)


def row_ids(shape):
    return lax.broadcasted_iota(jnp.int32, shape, len(shape) - 2)


def pack_kernel(
    block, previous, reaction, vert, horiz, friction, velocity, layers, out, prev_out, low, high, rows
):
    vectors, tile_x, tile_y = block.shape
    layer_count = horiz.shape[0]
    depth = layers[...]
    active = [(depth > k).astype(jnp.float32) for k in range(layer_count)]
    zero = jnp.zeros((tile_x, tile_y), jnp.float32)
    up = [vert[k] * active[k + 1] for k in range(layer_count - 1)] + [zero]
    lateral = [horiz[k] * active[k] for k in range(layer_count)]
    pivots = []
    for k in range(layer_count):
        drag = friction[...] if k == 0 else up[k - 1]
        diagonal = (base_damping + lateral[k] + drag + up[k]) * active[k] + (1.0 - active[k])
        if k > 0:
            diagonal = diagonal - up[k - 1] * up[k - 1] / pivots[k - 1]
        pivots.append(diagonal)
    top = zero
    for b in range(vectors):
        rows[pl.ds(b, tile_x, stride=vectors), :] = block[b]

    def put(field, value):
        rows[pl.ds(vectors * tile_x + field * tile_x, tile_x), :] = value

    for k in range(layer_count):
        put(F_PIVOT + k, lateral[k] * lateral[k] / pivots[k])
        is_top = depth == k + 1
        top = jnp.where(is_top, lateral[k] / pivots[k], top)
        if k + 1 < layer_count:
            below = jnp.where(depth > k + 1, lateral[k + 1], 1.0)
            put(F_RATIO + k, up[k] * lateral[k] / (pivots[k] * below))
    put(F_INV_LAT, 1.0 / lateral[0])
    put(F_TOP, top)
    put(F_LAYER, depth.astype(jnp.float32))
    put(F_BED, friction[...] * velocity[0])
    put(F_BED + 1, friction[...] * velocity[1])
    put(F_REACT, reaction[...])
    used = vectors * tile_x + FIELDS * tile_x
    rows[used:, :] = jnp.zeros((rows.shape[0] - used, tile_y), jnp.float32)
    for t in range(rows.shape[0] // LANES):
        out[t] = rows[t * LANES : (t + 1) * LANES, :].T
    low[...] = out[:, 0:HALO, :]
    high[...] = out[:, tile_y - HALO : tile_y, :]
    for b in range(vectors):
        rows[pl.ds(b, tile_x, stride=vectors), :] = previous[b]
    prev_out[...] = rows[0:LANES, :].T


def table_kernel(dest, cell, weight, out):
    count = dest.shape[0]
    devices = out.shape[0]
    onehot = dest[...] == lane_ids((count, devices))
    lower = row_ids((count, count)) >= lane_ids((count, count))
    running = jnp.dot(
        lower.astype(jnp.bfloat16), onehot.astype(jnp.bfloat16), preferred_element_type=jnp.float32
    )
    chosen = onehot.astype(jnp.float32)
    rank = jnp.sum(running * chosen, axis=1, keepdims=True).astype(jnp.int32) - 1
    lane = lane_ids((count, LANES))
    kind = lane // 4
    value = jnp.where(
        kind == 0,
        weight[:, 0:1],
        jnp.where(kind == 1, weight[:, 1:2], jnp.where(kind == 2, cell[...].astype(jnp.float32), 0.0)),
    )
    value = jnp.where(lane % 4 == rank, value, 0.0)
    out[...] = jnp.dot(chosen.T, value, precision=highest, preferred_element_type=jnp.float32)


def neighbour_sum(field, stride):
    rows, lanes = field.shape
    return (
        pltpu.roll(field, 1, 0)
        + pltpu.roll(field, rows - 1, 0)
        + pltpu.roll(field, stride, 1)
        + pltpu.roll(field, lanes - stride, 1)
    )


def shifted_prior(field, reaction, stride):
    image = (reaction - (SHIFT - 4.0)) * field - neighbour_sum(field, stride)
    return jnp.where(reaction > 0.0, image * (1.0 / SCALE), 0.0)


def expand(tiles, field, vectors, tile_x):
    place = field * tile_x
    tile, lane = place // LANES, place % LANES
    out = []
    for part in tiles:
        source = part[tile + 1]
        index = lane + lane_ids(source.shape) // vectors
        out.append(jnp.take_along_axis(source, index, axis=1))
    return jnp.concatenate(out, axis=1)


def fold(row, stride):
    shift = LANES // 2
    while shift >= stride:
        row = row + pltpu.roll(row, shift, 1)
        shift //= 2
    return row


def moment_kernel(vectors, flags, own, left, right, table, out, basis):
    tile_x = LANES // vectors
    rows = own.shape[1]
    weights = (flags[0], None, flags[1])

    def part_tile(t):
        result = []
        for ref, flag in zip((left, own, right), weights):
            value = ref[t]
            result.append(value if flag is None else value * flag)
        return result

    place = F_REACT * tile_x
    tile, lane = place // LANES, place % LANES
    index = lane + lane_ids((rows, LANES)) // vectors
    reaction = jnp.concatenate(
        [jnp.take_along_axis(part, index, axis=1) for part in part_tile(tile + 1)], axis=1
    )
    v0 = jnp.concatenate(part_tile(0), axis=1)
    v1 = shifted_prior(v0, reaction, vectors)
    v2 = shifted_prior(v1, reaction, vectors)
    v3 = shifted_prior(v2, reaction, vectors)
    for i, value in enumerate((v0, v1, v2)):
        for t in range(3):
            basis[i, t] = value[:, t * LANES : (t + 1) * LANES]
    own_of = [v[HALO : rows - HALO, LANES : 2 * LANES] for v in (v0, v1, v2, v3)]
    pairs = ((0, 0), (0, 1), (1, 1), (1, 2), (2, 2), (2, 3))
    group = lane_ids((1, LANES)) // vectors
    message = jnp.zeros((1, LANES), jnp.float32)
    for j, (a, b) in enumerate(pairs):
        total = fold(jnp.sum(own_of[a] * own_of[b], axis=0, keepdims=True), vectors)
        message = jnp.where(group == j + 1, total, message)
    out[...] = table[...] + message


def galerkin(moments):
    m = moments
    a = [SHIFT * m[i] + SCALE * m[i + 1] for i in range(5)]

    def over(top, pivot):
        return jnp.where(pivot > 0.0, top / jnp.where(pivot > 0.0, pivot, 1.0), 0.0)

    l10, l20 = over(a[1], a[0]), over(a[2], a[0])
    d1 = a[2] - l10 * a[1]
    e12 = a[3] - l20 * a[1]
    l21 = over(e12, d1)
    d2 = a[4] - l20 * a[2] - l21 * e12
    z1 = m[1] - l10 * m[0]
    z2 = m[2] - l20 * m[0] - l21 * z1
    y2 = over(z2, d2)
    y1 = over(z1, d1) - l21 * y2
    y0 = over(m[0], a[0]) - l10 * y1 - l20 * y2
    return y0, y1, y2


def split_rows(source, target, flag=None):
    count = target.shape[-3]
    for i in range(count):
        value = source[pl.ds(i, 8, stride=count), :]
        target[i] = value if flag is None else value * flag


def join_rows(source, target):
    count = source.shape[0]
    for t in range(target.shape[0]):
        for i in range(count):
            target[t, pl.ds(i, 8, stride=count), :] = source[i, :, t * LANES : (t + 1) * LANES]


def joined(flat):
    return jnp.concatenate([flat[t] for t in range(3)], axis=1)


def split_parts(own, left, right, flags, parts):
    for p, (ref, flag) in enumerate(((left, flags[0]), (own, None), (right, flags[1]))):
        for t in range(own.shape[0]):
            split_rows(ref.at[t], parts.at[p, t], flag)


def prepare_row(i, parts, ratio, pivot, bed_col, top_col, vectors, tile_x, layer_count):
    tiles = [[parts[p, t, i] for t in range(parts.shape[1])] for p in range(3)]
    get = functools.partial(expand, tiles, vectors=vectors, tile_x=tile_x)
    inv_lat, top, depth = get(F_INV_LAT), get(F_TOP), get(F_LAYER)
    ratios, pivots = [], []
    for k in range(layer_count):
        pivots.append(get(F_PIVOT + k))
        pivot[k, i] = pivots[k]
        if k + 1 < layer_count:
            ratios.append(get(F_RATIO + k))
            ratio[k, i] = ratios[k]
    forward = [inv_lat]
    for k in range(1, layer_count):
        forward.append(ratios[k - 1] * forward[k - 1])
    bed, surf = None, None
    for k in range(layer_count - 1, -1, -1):
        is_top = depth == float(k + 1)
        if bed is None:
            bed = pivots[k] * forward[k]
            surf = jnp.where(is_top, top, 0.0)
        else:
            bed = pivots[k] * forward[k] + ratios[k] * bed
            surf = jnp.where(is_top, top, ratios[k] * surf)
        bed_col[k, i] = bed
        top_col[k, i] = surf
    return get, inv_lat


def lateral_sum(field, c, k, i, stride):
    centre = field[c, k, i + 1]
    lanes = centre.shape[1]
    return (
        field[c, k, i]
        + field[c, k, i + 2]
        + pltpu.roll(centre, stride, 1)
        + pltpu.roll(centre, lanes - stride, 1)
    )


def wrap_rows(field):
    count = field.shape[2] - 2

    def body(k, carry):
        for c in range(2):
            field[c, k, 0] = pltpu.roll(field[c, k, count], 1, 0)
            field[c, k, count + 1] = pltpu.roll(field[c, k, 1], 7, 0)
        return carry

    lax.fori_loop(0, field.shape[1], body, 0)


def sweep(source, target, ratio, pivot, stride, bed_source=None, top_col=None, top_source=None):
    layer_count = pivot.shape[0]

    def body(i, carry):
        for c in range(2):
            carried = []
            for k in range(layer_count):
                value = lateral_sum(source, c, k, i, stride)
                if k > 0:
                    value = value + ratio[k - 1, i] * carried[k - 1]
                elif bed_source is not None:
                    value = value + bed_source[c, i]
                carried.append(value)
            solved = None
            extra = top_source[c, i] if top_source is not None else None
            for k in range(layer_count - 1, -1, -1):
                value = pivot[k, i] * carried[k]
                if solved is not None:
                    value = value + ratio[k, i] * solved
                solved = value
                if extra is not None:
                    value = value + top_col[k, i] * extra
                target[c, k, i + 1] = value
        return carry

    lax.fori_loop(0, pivot.shape[1], body, 0)
    wrap_rows(target)


def velocity_kernel(
    vectors, flags, message, own, left, right, basis,
    misfit, low, high,
    ratio, pivot, bed_col, top_col, one, two, source, parts, flat, smooth, surface, flat_out,
):
    tile_x = LANES // vectors
    layer_count = pivot.shape[0]
    total_rows = own.shape[1]
    count = total_rows // 8
    tile_y = total_rows - 2 * HALO
    group = lane_ids((8, LANES)) // vectors
    summed = jnp.broadcast_to(jnp.sum(message[...], axis=0, keepdims=True), (8, LANES))
    moments = [fold(jnp.where(group == j + 1, summed, 0.0), vectors) for j in range(6)]
    y = [v[0:1] for v in galerkin(moments)]
    for t in range(3):
        flat[t] = y[0] * basis[0, t] + y[1] * basis[1, t] + y[2] * basis[2, t]
    for t in range(3):
        split_rows(flat.at[t], smooth.at[t])
    split_parts(own, left, right, flags, parts)

    def prepare(i, carry):
        get, inv_lat = prepare_row(
            i, parts, ratio, pivot, bed_col, top_col, vectors, tile_x, layer_count
        )
        for c in range(2):
            bed = get(F_BED + c) * jnp.concatenate([smooth[t, i] for t in range(3)], axis=1)
            source[c, i] = bed * inv_lat
            for k in range(layer_count):
                one[c, k, i + 1] = bed_col[k, i] * bed
        return carry

    lax.fori_loop(0, count, prepare, 0)
    wrap_rows(one)
    sweep(one, two, ratio, pivot, vectors, bed_source=source)
    sweep(two, one, ratio, pivot, vectors, bed_source=source)
    middle = slice(LANES, 2 * LANES)

    def finish(i, carry):
        for c in range(2):
            total = top_col[0, i, :, middle] * source[c, i, :, middle]
            for k in range(layer_count):
                total = total + top_col[k, i, :, middle] * lateral_sum(one, c, k, i, vectors)[:, middle]
            surface[c, i] = total
        return carry

    lax.fori_loop(0, count, finish, 0)

    lane = lane_ids((LANES, LANES))
    for c in range(2):
        total = jnp.zeros((LANES, LANES), jnp.float32)
        for r in range(4):
            cell = message[:, 8 + r : 9 + r].astype(jnp.int32)
            weight = message[:, 4 * c + r : 4 * c + r + 1]
            at_row = (cell % tile_y == lane).astype(jnp.float32)
            at_lane = jnp.where(cell // tile_y == lane // vectors, weight, 0.0)
            total = total + jnp.dot(
                at_row.T, at_lane, precision=highest, preferred_element_type=jnp.float32
            )
        join_rows(surface.at[c], flat_out)
        misfit[c] = total * flat_out[0, HALO : HALO + tile_y, :]
    low[...] = misfit[:, 0:HALO, :]
    high[...] = misfit[:, tile_y - HALO :, :]


def adjoint_kernel(
    vectors, flags, own, left, right, misfit, misfit_left, misfit_right, previous,
    out, stacked,
    ratio, pivot, bed_col, top_col, one, two, source, parts, flat, pulled, bed, reaction_all, lateral, sides,
):
    tile_x = LANES // vectors
    layer_count = pivot.shape[0]
    total_rows = own.shape[1]
    count = total_rows // 8
    split_parts(own, left, right, flags, parts)
    for c in range(2):
        split_rows(misfit_left.at[c], sides.at[c, 0], flags[0])
        split_rows(misfit.at[c], sides.at[c, 1])
        split_rows(misfit_right.at[c], sides.at[c, 2], flags[1])

    def prepare(i, carry):
        get, inv_lat = prepare_row(
            i, parts, ratio, pivot, bed_col, top_col, vectors, tile_x, layer_count
        )
        reaction_all[i] = get(F_REACT)
        lateral[i] = inv_lat
        for c in range(2):
            value = jnp.concatenate([sides[c, t, i] for t in range(3)], axis=1)
            source[c, i] = value
            bed[c, i] = get(F_BED + c)
            for k in range(layer_count):
                one[c, k, i + 1] = top_col[k, i] * value
        return carry

    lax.fori_loop(0, count, prepare, 0)
    wrap_rows(one)
    sweep(one, two, ratio, pivot, vectors, top_col=top_col, top_source=source)
    sweep(two, one, ratio, pivot, vectors, top_col=top_col, top_source=source)

    def finish(i, carry):
        total = None
        for c in range(2):
            value = top_col[0, i] * lateral[i] * source[c, i]
            for k in range(layer_count):
                value = value + bed_col[k, i] * lateral_sum(one, c, k, i, vectors)
            value = bed[c, i] * value
            total = value if total is None else total + value
        pulled[i] = total
        return carry

    lax.fori_loop(0, count, finish, 0)
    join_rows(reaction_all, flat)
    reaction = joined(flat)
    join_rows(pulled, flat)
    v0 = joined(flat)
    v1 = shifted_prior(v0, reaction, vectors)
    v2 = shifted_prior(v1, reaction, vectors)
    v3 = shifted_prior(v2, reaction, vectors)
    v0, v1, v2, v3 = [v[HALO : total_rows - HALO, LANES : 2 * LANES] for v in (v0, v1, v2, v3)]
    x = own[0, HALO : total_rows - HALO, :]
    p = previous[...]
    flipped = [v.T for v in (v0, v1, v2, p, x)]
    for i, value in enumerate(flipped):
        for at in range(tile_x):
            stacked[at, i * vectors : (i + 1) * vectors, :] = value[at * vectors : (at + 1) * vectors, :]
    t0, t1, t2, tp, tx = flipped
    pairs = (
        (t0, v0), (t0, v1), (t1, v1), (t1, v2), (t2, v2),
        (tx, v0), (tx, v1), (tx, v2),
        (t0, p), (t1, p), (t2, p),
        (tx, x), (tx, p), (tp, p),
    )
    same = row_ids((LANES, LANES)) // vectors == lane_ids((LANES, LANES)) // vectors
    group = lane_ids((vectors, LANES)) // vectors
    halves = [jnp.zeros((vectors, LANES), jnp.float32)] * 2
    for n, (a, b) in enumerate(pairs):
        product = jnp.dot(a, b, precision=highest, preferred_element_type=jnp.float32)
        product = jnp.where(same, product, 0.0)
        block = product[0:vectors]
        for at in range(1, tile_x):
            block = block + product[at * vectors : (at + 1) * vectors]
        block = fold(block, vectors)
        halves[n // tile_x] = jnp.where(group == n % tile_x, block, halves[n // tile_x])
    last = fold(jnp.sum(v2 * v3, axis=0, keepdims=True), vectors)
    n = len(pairs)
    halves[n // tile_x] = jnp.where(group == n % tile_x, last, halves[n // tile_x])
    both = jnp.concatenate(halves, axis=1)
    for i in range(out.shape[0]):
        out[i] = both


def partial_kernel(received, out):
    total = jnp.sum(received[...], axis=0)
    for i in range(out.shape[0]):
        out[i] = total


def finish_kernel(cells, received, stacked, beta_ref, next_out, alpha_out, beta_out):
    vectors = beta_ref.shape[0]
    total = jnp.sum(received[...], axis=0)

    def block(n):
        return total[:, n * vectors : (n + 1) * vectors]

    def dot(a, b, dims=((1,), (0,))):
        return lax.dot_general(a, b, (dims, ((), ())), precision=highest, preferred_element_type=jnp.float32)

    shape = (vectors, vectors)
    eye = row_ids(shape) == lane_ids(shape)
    s = [block(n) for n in range(5)]
    moments = [jnp.sum(jnp.where(eye, m, 0.0), axis=0, keepdims=True) for m in s]
    moments.append(block(14)[0:1])
    along = galerkin(moments)
    down = [jnp.sum(jnp.where(eye, v, 0.0), axis=1, keepdims=True) for v in along]
    xv = [block(5 + k) for k in range(3)]
    vp = [block(8 + k) for k in range(3)]
    xx, xp, pp = block(11), block(12), block(13)
    beta = beta_ref[...]
    last = ((1,), (1,))
    first = ((0,), (0,))
    xr = xv[0] * along[0] + xv[1] * along[1] + xv[2] * along[2] - dot(xp, beta, last)
    alpha = xr * (1.0 / cells)
    alpha_out[...] = alpha
    rr = None
    for k in range(3):
        for l in range(3):
            term = down[k] * along[l] * s[k + l]
            rr = term if rr is None else rr + term
    cross = dot(down[0] * vp[0] + down[1] * vp[1] + down[2] * vp[2], beta, last)
    rr = rr - cross - cross.T + dot(beta, dot(pp, beta, last))
    gram = rr * (1.0 / cells) - 2.0 * dot(alpha, alpha, first) + dot(
        alpha, dot(xx * (1.0 / cells), alpha), first
    )
    gram = 0.5 * (gram + gram.T)
    work = jnp.concatenate(
        [gram, eye.astype(jnp.float32), jnp.zeros((vectors, LANES - 2 * vectors), jnp.float32)], axis=1
    )
    down_id = row_ids(work.shape)
    for j in range(vectors):
        row = work[j : j + 1, :]
        scale = 1.0 / jnp.sqrt(row[:, j : j + 1])
        row = row * scale
        column = work[:, j : j + 1] * scale
        work = jnp.where(down_id > j, work - column * row, jnp.where(down_id == j, row, work))
    beta_out[...] = jnp.where(row_ids(shape) <= lane_ids(shape), work[:, 0:vectors], 0.0)
    inverse = work[:, vectors : 2 * vectors]
    mix = jnp.concatenate(
        [inverse * v for v in along] + [-dot(inverse, beta), -dot(inverse, alpha, last)], axis=1
    )
    for at in range(stacked.shape[0]):
        next_out[:, at, :] = dot(mix, stacked[at])


def shards(
    lanczos_block,
    previous_block,
    previous_beta,
    prior_reaction,
    vert_coupling,
    horiz_coupling,
    friction,
    base_velocity,
    layers,
    obs_dest,
    obs_cell,
    obs_weight,
):
    vectors, tile_x, tile_y = lanczos_block.shape
    layer_count = horiz_coupling.shape[0]
    obs_rows = obs_cell.shape[0]
    size_x, size_y = lax.axis_size("mx"), lax.axis_size("my")
    devices = size_x * size_y
    cells = tile_x * tile_y * devices
    at_x, at_y = lax.axis_index("mx"), lax.axis_index("my")
    flags = jnp.stack([at_x > 0, at_x + 1 < size_x]).astype(jnp.float32)
    low_flag = (at_y > 0).astype(jnp.float32)
    high_flag = (at_y + 1 < size_y).astype(jnp.float32)
    forward_y = [(i, (i + 1) % size_y) for i in range(size_y)]
    backward_y = [(i, (i - 1) % size_y) for i in range(size_y)]
    forward_x = [(i, (i + 1) % size_x) for i in range(size_x)]
    backward_x = [(i, (i - 1) % size_x) for i in range(size_x)]
    f32 = jnp.float32
    rows = tile_y + 2 * HALO
    wide = 3 * LANES
    tiles = -(-(vectors * tile_x + FIELDS * tile_x) // LANES)
    smem = pl.BlockSpec(memory_space=pltpu.SMEM)
    vmem = pl.BlockSpec(memory_space=pltpu.VMEM)

    def shape(*dims):
        return jax.ShapeDtypeStruct(dims, f32)

    packed, previous, low, high = pl.pallas_call(
        pack_kernel,
        out_shape=(
            shape(tiles, tile_y, LANES), shape(tile_y, LANES), shape(tiles, HALO, LANES), shape(tiles, HALO, LANES)
        ),
        scratch_shapes=[pltpu.VMEM((tiles * LANES, tile_y), f32)],
        compiler_params=params(),
        name="pack",
    )(
        lanczos_block, previous_block, prior_reaction, vert_coupling, horiz_coupling,
        friction, base_velocity, layers,
    )
    table = pl.pallas_call(
        table_kernel, out_shape=shape(devices, LANES), compiler_params=params(), name="table"
    )(obs_dest, obs_cell.reshape(obs_rows, 1), obs_weight)

    from_low = lax.ppermute(high, "my", forward_y)
    from_high = lax.ppermute(low, "my", backward_y)
    own = jnp.concatenate([from_low * low_flag, packed, from_high * high_flag], axis=1)
    left = lax.ppermute(own, "mx", forward_x)
    right = lax.ppermute(own, "mx", backward_x)

    message, basis = pl.pallas_call(
        functools.partial(moment_kernel, vectors),
        out_shape=(shape(devices, LANES), shape(3, 3, rows, LANES)),
        in_specs=[smem, vmem, vmem, vmem, vmem],
        compiler_params=params(),
        name="moments",
    )(flags, own, left, right, table)
    message = lax.all_to_all(message, AXES, split_axis=0, concat_axis=0, tiled=True)

    count = rows // 8
    columns = [
        pltpu.VMEM((layer_count - 1, count, 8, wide), f32),
        pltpu.VMEM((layer_count, count, 8, wide), f32),
        pltpu.VMEM((layer_count, count, 8, wide), f32),
        pltpu.VMEM((layer_count, count, 8, wide), f32),
        pltpu.VMEM((2, layer_count, count + 2, 8, wide), f32),
        pltpu.VMEM((2, layer_count, count + 2, 8, wide), f32),
        pltpu.VMEM((2, count, 8, wide), f32),
        pltpu.VMEM((3, tiles, count, 8, LANES), f32),
        pltpu.VMEM((3, rows, LANES), f32),
    ]
    misfit, low, high = pl.pallas_call(
        functools.partial(velocity_kernel, vectors),
        out_shape=(shape(2, tile_y, LANES), shape(2, HALO, LANES), shape(2, HALO, LANES)),
        in_specs=[smem] + [vmem] * 5,
        scratch_shapes=columns
        + [
            pltpu.VMEM((3, count, 8, LANES), f32),
            pltpu.VMEM((2, count, 8, LANES), f32),
            pltpu.VMEM((1, rows, LANES), f32),
        ],
        compiler_params=params(),
        name="velocity",
    )(flags, message, own, left, right, basis)

    from_low = lax.ppermute(high, "my", forward_y)
    from_high = lax.ppermute(low, "my", backward_y)
    misfit = jnp.concatenate([from_low * low_flag, misfit, from_high * high_flag], axis=1)
    misfit_left = lax.ppermute(misfit, "mx", forward_x)
    misfit_right = lax.ppermute(misfit, "mx", backward_x)

    products, stacked = pl.pallas_call(
        functools.partial(adjoint_kernel, vectors),
        out_shape=(shape(size_x, vectors, 2 * LANES), shape(tile_x, 5 * vectors, tile_y)),
        in_specs=[smem] + [vmem] * 7,
        scratch_shapes=columns
        + [
            pltpu.VMEM((count, 8, wide), f32),
            pltpu.VMEM((2, count, 8, wide), f32),
            pltpu.VMEM((count, 8, wide), f32),
            pltpu.VMEM((count, 8, wide), f32),
            pltpu.VMEM((2, 3, count, 8, LANES), f32),
        ],
        compiler_params=params(),
        name="adjoint",
    )(flags, own, left, right, misfit, misfit_left, misfit_right, previous)

    products = lax.all_to_all(products, "mx", split_axis=0, concat_axis=0, tiled=True)
    products = pl.pallas_call(
        partial_kernel,
        out_shape=shape(size_y, vectors, 2 * LANES),
        compiler_params=params(),
        name="partial",
    )(products)
    products = lax.all_to_all(products, "my", split_axis=0, concat_axis=0, tiled=True)
    return pl.pallas_call(
        functools.partial(finish_kernel, float(cells)),
        out_shape=(shape(vectors, tile_x, tile_y), shape(vectors, vectors), shape(vectors, vectors)),
        compiler_params=params(),
        name="finish",
    )(products, stacked, previous_beta)


def solution(mesh):
    in_specs = (
        P(None, "mx", "my"),
        P(None, "mx", "my"),
        P(),
        P("mx", "my"),
        P(None, "mx", "my"),
        P(None, "mx", "my"),
        P("mx", "my"),
        P(None, "mx", "my"),
        P("mx", "my"),
        P(("mx", "my"), None),
        P(("mx", "my")),
        P(("mx", "my"), None),
    )
    out_specs = (P(None, "mx", "my"), P(), P())
    return jax.shard_map(shards, mesh=mesh, in_specs=in_specs, out_specs=out_specs, check_vma=False)
```

time: 1260 us -> 143 us (0.11)
  blocking collectives: 833 us -> 44.9 us
  local copies, waits for them, and re-layouts: 162 us -> 5.27 us
  starting transfers between devices: 150 us -> 13.8 us
  Pallas kernels: 0 us -> 65.4 us
  other arithmetic: 64.7 us -> 2.52 us
  waiting for transfers between devices: 34.6 us -> 9.54 us
    psum x12 -> x0, blocking collectives: 795 us -> none  [the longest x10 668 us: cell_sums(): return lax.psum(jnp.sum(values, axis=(1, 2)), ('mx', 'my'))]
    ppermute x48 -> x8, starting transfers between devices: 140 us -> 13.8 us  [the longest x2 9.27 us: shards(): from_high = lax.ppermute(low, 'my', backward_y)]
    slice x38 -> x0, local copies, waits for them, and re-layouts: 81.7 us -> none  [the longest x18 51.3 us: with_halo(): head = lax.slice_in_dim(cells, 0, width, axis=dim)]
    ppermute x12 -> x0, local copies, waits for them, and re-layouts: 66.9 us -> none  [the longest x6 33.5 us: with_halo(): lax.ppermute(head, axis, [((i + 1) % count, i) for i in range(ends)])]
    pallas_call x0 -> x7, Pallas kernels: none -> 65.4 us  [the longest x1 27.3 us: shards(): pl.pallas_call(functools.partial(adjoint_kernel, vectors), out_shape=(sha...]
    add x13 -> x0, other arithmetic: 36.3 us -> none  [the longest x6 34.9 us: column_map(): source + lateral * neighbours(lateral * iterate)]
    ppermute x48 -> x8, waiting for transfers between devices: 30 us -> 9.54 us  [the longest x2 3.69 us: shards(): from_low = lax.ppermute(high, 'my', forward_y)]
    all_to_all x2 -> x3, blocking collectives: 38.5 us -> 44.9 us  [the longest x1 19.4 us: shards(): lax.all_to_all(message, AXES, split_axis=0, concat_axis=0, tiled=True)]
  transfers between devices with their start and end apart: 49 -> 8, of which waited for: 24 -> 5; matrix products, arithmetic and copies ran while one was open for 6% -> 2% of each run, Pallas kernels for 0% -> 2%
where the time goes in v1:
time: 143 us; the launch traced here: 142 us
  Pallas kernels  65.4 us (46%)
  blocking collectives  44.9 us (31%)
  starting transfers between devices  13.8 us (10%)
  waiting for transfers between devices  9.54 us (7%)
  local copies, waits for them, and re-layouts  5.27 us (4%)
  other arithmetic  2.52 us (2%)
    pallas_call x1, Pallas kernels, shards(): pl.pallas_call(functools.partial(adjoint_kernel, vectors), out_shape=(sha...  27.3 us
    pallas_call x1, Pallas kernels, shards(): pl.pallas_call(functools.partial(velocity_kernel, vectors), out_shape=(sh...  24.9 us
    all_to_all x1, blocking collectives, shards(): lax.all_to_all(message, AXES, split_axis=0, concat_axis=0, tiled=True)  19.4 us
    all_to_all x1, blocking collectives, shards(): lax.all_to_all(products, 'my', split_axis=0, concat_axis=0, tiled=True)  15.3 us
    all_to_all x1, blocking collectives, shards(): lax.all_to_all(products, 'mx', split_axis=0, concat_axis=0, tiled=True)  10.1 us
    ppermute x2, starting transfers between devices, shards(): from_high = lax.ppermute(low, 'my', backward_y)  9.27 us
    pallas_call x1, Pallas kernels, shards(): pl.pallas_call(functools.partial(finish_kernel, float(cells)), out_shape=...  4.57 us
    unnamed x20, local copies, waits for them, and re-layouts  4.48 us
  transfers between devices with their start and end apart: 8, of which 5 were waited for; matrix products, arithmetic and copies ran while one was open for 2% of the time, Pallas kernels for 2%

profile of v1, /device:TPU:0, one launch (start us, length us, event | category | flops | bytes accessed | tf_op | source)
XLA Modules:
  0.0 142.2 jit_solution(15770221459130545151)
XLA Ops:
  0.6 2.0 %pack.1 = (f32[4,128,128]{2,1,0:T(8,128)}, f32[128,128]{1,0:T(8,128)}, f32[4,8,128]{2,1,0:T(8,128)}, f32[4,8,128]{2,1,0:T(8,128)}) custom-call(f32[16,8,128]{2,1,0:T(8,128)} %block.1, f32[16,8,128]{2,1,0:T(8,128)} %previous.1, f32[8,128]{1,0:T(8,128)} %reaction.1, f32[15,8,128]{2,1,0:T(8,128)} %vert.1, f32[16,8,128]{2,1,0:T(8,128)} %horiz.1, ...), custom_call_target="tpu_custom_call" | custom-call | tf_op jit(solution)/shard_map/pack/pallas_call | solution.py:553
  2.6 2.0 %collective-permute-start = (f32[4,8,128]{2,1,0:T(8,128)}, f32[4,8,128]{2,1,0:T(8,128)S(1)}, u32[]{:S(2)}, u32[]{:S(2)}) collective-permute-start(f32[4,8,128]{2,1,0:T(8,128)} %get-tuple-element.14), channel_id=1, source_target_pairs={{0,1},{1,2},{2,3},{3,4},{4,5},{5,6},{6,7},{7,8},{8,9},{9,10},{10,1... | collective-permute-start | bytes 49160 | tf_op jit(solution)/shard_map/ppermute | solution.py:569
  4.6 4.6 %collective-permute-start.1 = (f32[4,8,128]{2,1,0:T(8,128)}, f32[4,8,128]{2,1,0:T(8,128)S(1)}, u32[]{:S(2)}, u32[]{:S(2)}) collective-permute-start(f32[4,8,128]{2,1,0:T(8,128)} %get-tuple-element.16), channel_id=1, source_target_pairs={{0,15},{1,0},{2,1},{3,2},{4,3},{5,4},{6,5},{7,6},{8,7},{9,8},{10,9... | collective-permute-start | bytes 49160 | tf_op jit(solution)/shard_map/ppermute | solution.py:570
  9.2 1.9 %collective-permute-done = f32[4,8,128]{2,1,0:T(8,128)S(1)} collective-permute-done((f32[4,8,128]{2,1,0:T(8,128)}, f32[4,8,128]{2,1,0:T(8,128)S(1)}, u32[]{:S(2)}, u32[]{:S(2)}) %collective-permute-start) | collective-permute-done | bytes 16416 | tf_op jit(solution)/shard_map/ppermute | solution.py:569
  11.1 1.0 pad_maximum_fusion.own
  12.1 1.3 collective-permute-start.3
  13.4 0.7 copy-done.7
  14.1 0.8 copy.20.dest
  14.9 0.7 copy-done.8
  15.6 0.8 copy.21.cell
  16.4 0.8 copy.22.weight
  17.2 2.4 %table.1 = f32[128,128]{1,0:T(8,128)} custom-call(s32[256,1]{1,0:T(8,128)} %copy.20.dest, s32[256,1]{1,0:T(8,128)} %copy.21.cell, f32[256,2]{1,0:T(8,128)} %copy.22.weight), custom_call_target="tpu_custom_call" | custom-call | tf_op jit(solution)/shard_map/table/pallas_call | solution.py:565
  19.6 0.6 add_convert_fusion.flags
  20.2 0.5 collective-permute-done.2.left
  20.8 0.2 copy-done.1
  20.9 0.7 copy-done.2
  21.7 2.7 %moments.1 = (f32[128,128]{1,0:T(8,128)}, f32[3,3,144,128]{3,2,1,0:T(8,128)}) custom-call(f32[2]{0:T(128)} %add_convert_fusion.flags, f32[4,144,128]{2,1,0:T(8,128)} %copy-done, f32[4,144,128]{2,1,0:T(8,128)} %copy-done.2, f32[4,144,128]{2,1,0:T(8,128)} %copy-done.1, f32[128,128]{1,0:T(8,128)} %table.1), custom_call_target="tpu_custom_call" | custom-call | tf_op jit(solution)/shard_map/moments/pallas_call | solution.py:575
  24.4 19.4 %all_to_all.21 = f32[128,1,128]{2,1,0:T(1,128)} all-to-all(f32[128,1,128]{2,1,0:T(1,128)} %bitcast.8), channel_id=1, replica_groups=mesh['mx'=8,'my'=16] {'mx','my'}, dimensions={0} | all-to-all | bytes 131072 | tf_op jit(solution)/shard_map/all_to_all | solution.py:582
  43.8 24.9 %velocity.3 = (f32[2,128,128]{2,1,0:T(8,128)}, f32[2,8,128]{2,1,0:T(8,128)}, f32[2,8,128]{2,1,0:T(8,128)}) custom-call(f32[2]{0:T(128)} %add_convert_fusion.flags, f32[128,128]{1,0:T(8,128)} %bitcast.7, f32[4,144,128]{2,1,0:T(8,128)} %copy-done, f32[4,144,128]{2,1,0:T(8,128)} %copy-done.2, f32[4,144,128]{2,1,0:T(8,128)} %copy-done.1, ...), custom_call_target="tpu_custom_call" | custom-call | tf_op jit(solution)/shard_map/velocity/pallas_call | solution.py:596
  68.6 0.7 collective-permute-start.4
  69.4 4.6 %collective-permute-start.5 = (f32[2,8,128]{2,1,0:T(8,128)}, f32[2,8,128]{2,1,0:T(8,128)S(1)}, u32[]{:S(2)}, u32[]{:S(2)}) collective-permute-start(f32[2,8,128]{2,1,0:T(8,128)} %get-tuple-element.21), channel_id=1, source_target_pairs={{0,15},{1,0},{2,1},{3,2},{4,3},{5,4},{6,5},{7,6},{8,7},{9,8},{10,9... | collective-permute-start | bytes 24584 | tf_op jit(solution)/shard_map/ppermute | solution.py:611
  74.0 1.8 %collective-permute-done.4 = f32[2,8,128]{2,1,0:T(8,128)S(1)} collective-permute-done((f32[2,8,128]{2,1,0:T(8,128)}, f32[2,8,128]{2,1,0:T(8,128)S(1)}, u32[]{:S(2)}, u32[]{:S(2)}) %collective-permute-start.4) | collective-permute-done | bytes 8224 | tf_op jit(solution)/shard_map/ppermute | solution.py:610
  75.8 0.9 pad_maximum_fusion.1.misfit
  76.8 0.5 collective-permute-start.6
  77.3 2.2 %collective-permute-done.7.misfit_right = f32[2,144,128]{2,1,0:T(8,128)S(1)} collective-permute-done((f32[2,144,128]{2,1,0:T(8,128)S(1)}, f32[2,144,128]{2,1,0:T(8,128)S(1)}, u32[]{:S(2)}, u32[]{:S(2)}) %collective-permute-start.7) | collective-permute-done | bytes 147488 | tf_op jit(solution)/shard_map/ppermute | solution.py:614
  79.5 3.1 %collective-permute-done.6.misfit_left = f32[2,144,128]{2,1,0:T(8,128)S(1)} collective-permute-done((f32[2,144,128]{2,1,0:T(8,128)S(1)}, f32[2,144,128]{2,1,0:T(8,128)S(1)}, u32[]{:S(2)}, u32[]{:S(2)}) %collective-permute-start.6) | collective-permute-done | bytes 147488 | tf_op jit(solution)/shard_map/ppermute | solution.py:613
  82.6 0.6 copy-done.5
  83.2 27.3 %adjoint.1 = (f32[8,16,256]{2,1,0:T(8,128)}, f32[8,80,128]{2,1,0:T(8,128)}) custom-call(f32[2]{0:T(128)} %add_convert_fusion.flags, f32[4,144,128]{2,1,0:T(8,128)} %copy-done, f32[4,144,128]{2,1,0:T(8,128)} %copy-done.2, f32[4,144,128]{2,1,0:T(8,128)} %copy-done.1, f32[2,144,128]{2,1,0:T(8,128)} %copy-done.3, f32[2,144,128]{2,1,0:T(8,128)} %copy-done.5, ...), custom_call_target="tpu_custom_call" | custom-call | tf_op jit(solution)/shard_map/adjoint/pallas_call | solution.py:616
  110.5 10.1 %all_to_all.22.received = f32[8,16,256]{2,1,0:T(8,128)} all-to-all(f32[8,16,256]{2,1,0:T(8,128)} %get-tuple-element.23), channel_id=1, replica_groups=mesh['mx'=8,'my'=16] {'mx'}, dimensions={0} | all-to-all | bytes 262144 | tf_op jit(solution)/shard_map/all_to_all | solution.py:632
  120.6 1.6 %partial.1 = f32[16,16,256]{2,1,0:T(8,128)} custom-call(f32[8,16,256]{2,1,0:T(8,128)} %all_to_all.22.received), custom_call_target="tpu_custom_call" | custom-call | tf_op jit(solution)/shard_map/partial/pallas_call | solution.py:633
  122.3 15.3 %all_to_all.23.received = f32[16,16,256]{2,1,0:T(8,128)} all-to-all(f32[16,16,256]{2,1,0:T(8,128)} %partial.1), channel_id=1, replica_groups=mesh['mx'=8,'my'=16] {'my'}, dimensions={0} | all-to-all | bytes 524288 | tf_op jit(solution)/shard_map/all_to_all | solution.py:639
  137.6 4.6 %finish.1 = (f32[16,8,128]{2,1,0:T(8,128)}, f32[16,16]{1,0:T(8,128)}, f32[16,16]{1,0:T(8,128)}) custom-call(f32[16,16,256]{2,1,0:T(8,128)} %all_to_all.23.received, f32[8,80,128]{2,1,0:T(8,128)} %get-tuple-element.24.stacked, f32[16,16]{1,0:T(8,128)} %beta_ref.1), custom_call_target="tpu_custom_call" | custom-call | tf_op jit(solution)/shard_map/finish/pallas_call | solution.py:640
  (22 shorter events, 0.1 us)
Async XLA Ops:
  2.6 8.5 %collective-permute-start = (f32[4,8,128]{2,1,0:T(8,128)}, f32[4,8,128]{2,1,0:T(8,128)S(1)}, u32[]{:S(2)}, u32[]{:S(2)}) collective-permute-start(f32[4,8,128]{2,1,0:T(8,128)} %get-tuple-element.14), channel_id=1, source_target_pairs={{0,1},{1,2},{2,3},{3,4},{4,5},{5,6},{6,7},{7,8},{8,9},{9,10},{10,1... | collective-permute-start | bytes 49160 | tf_op jit(solution)/shard_map/ppermute | solution.py:569
  4.6 6.5 %collective-permute-start.1 = (f32[4,8,128]{2,1,0:T(8,128)}, f32[4,8,128]{2,1,0:T(8,128)S(1)}, u32[]{:S(2)}, u32[]{:S(2)}) collective-permute-start(f32[4,8,128]{2,1,0:T(8,128)} %get-tuple-element.16), channel_id=1, source_target_pairs={{0,15},{1,0},{2,1},{3,2},{4,3},{5,4},{6,5},{7,6},{8,7},{9,8},{10,9... | collective-permute-start | bytes 49160 | tf_op jit(solution)/shard_map/ppermute | solution.py:570
  12.1 7.5 %copy-start = (f32[4,144,128]{2,1,0:T(8,128)}, f32[4,144,128]{2,1,0:T(8,128)S(1)}, u32[]{:S(2)}) copy-start(f32[4,144,128]{2,1,0:T(8,128)S(1)} %pad_maximum_fusion.own) | copy-start | bytes 884740
  12.1 8.1 %collective-permute-start.3 = (f32[4,144,128]{2,1,0:T(8,128)S(1)}, f32[4,144,128]{2,1,0:T(8,128)S(1)}, u32[]{:S(2)}, u32[]{:S(2)}) collective-permute-start(f32[4,144,128]{2,1,0:T(8,128)S(1)} %pad_maximum_fusion.own), channel_id=1, source_target_pairs={{0,112},{16,0},{32,16},{48,32},{64,48},{80,64},{96,80},{112,96},{1... | collective-permute-start | bytes 884744 | tf_op jit(solution)/shard_map/ppermute | solution.py:573
  13.4 7.4 %collective-permute-start.2 = (f32[4,144,128]{2,1,0:T(8,128)S(1)}, f32[4,144,128]{2,1,0:T(8,128)S(1)}, u32[]{:S(2)}, u32[]{:S(2)}) collective-permute-start(f32[4,144,128]{2,1,0:T(8,128)S(1)} %pad_maximum_fusion.own), channel_id=1, source_target_pairs={{0,16},{16,32},{32,48},{48,64},{64,80},{80,96},{96,112},{112,0},{1... | collective-permute-start | bytes 884744 | tf_op jit(solution)/shard_map/ppermute | solution.py:572
  13.4 0.7 copy-start.7
  14.9 0.7 copy-start.8
  15.6 0.8 copy-start.6
  20.2 0.7 copy-start.1
  20.9 0.7 copy-start.2
  68.6 7.2 %collective-permute-start.4 = (f32[2,8,128]{2,1,0:T(8,128)}, f32[2,8,128]{2,1,0:T(8,128)S(1)}, u32[]{:S(2)}, u32[]{:S(2)}) collective-permute-start(f32[2,8,128]{2,1,0:T(8,128)} %get-tuple-element.19), channel_id=1, source_target_pairs={{0,1},{1,2},{2,3},{3,4},{4,5},{5,6},{6,7},{7,8},{8,9},{9,10},{10,1... | collective-permute-start | bytes 24584 | tf_op jit(solution)/shard_map/ppermute | solution.py:610
  69.4 6.5 %collective-permute-start.5 = (f32[2,8,128]{2,1,0:T(8,128)}, f32[2,8,128]{2,1,0:T(8,128)S(1)}, u32[]{:S(2)}, u32[]{:S(2)}) collective-permute-start(f32[2,8,128]{2,1,0:T(8,128)} %get-tuple-element.21), channel_id=1, source_target_pairs={{0,15},{1,0},{2,1},{3,2},{4,3},{5,4},{6,5},{7,6},{8,7},{9,8},{10,9... | collective-permute-start | bytes 24584 | tf_op jit(solution)/shard_map/ppermute | solution.py:611
  76.8 5.8 %copy-start.3 = (f32[2,144,128]{2,1,0:T(8,128)}, f32[2,144,128]{2,1,0:T(8,128)S(1)}, u32[]{:S(2)}) copy-start(f32[2,144,128]{2,1,0:T(8,128)S(1)} %pad_maximum_fusion.1.misfit) | copy-start | bytes 442372
  76.8 2.7 %collective-permute-start.7 = (f32[2,144,128]{2,1,0:T(8,128)S(1)}, f32[2,144,128]{2,1,0:T(8,128)S(1)}, u32[]{:S(2)}, u32[]{:S(2)}) collective-permute-start(f32[2,144,128]{2,1,0:T(8,128)S(1)} %pad_maximum_fusion.1.misfit), channel_id=1, source_target_pairs={{0,112},{16,0},{32,16},{48,32},{64,48},{80,64},{96,80},{112,96},{1... | collective-permute-start | bytes 442376 | tf_op jit(solution)/shard_map/ppermute | solution.py:614
  76.8 5.8 %collective-permute-start.6 = (f32[2,144,128]{2,1,0:T(8,128)S(1)}, f32[2,144,128]{2,1,0:T(8,128)S(1)}, u32[]{:S(2)}, u32[]{:S(2)}) collective-permute-start(f32[2,144,128]{2,1,0:T(8,128)S(1)} %pad_maximum_fusion.1.misfit), channel_id=1, source_target_pairs={{0,16},{16,32},{32,48},{48,64},{64,80},{80,96},{96,112},{112,0},{1... | collective-permute-start | bytes 442376 | tf_op jit(solution)/shard_map/ppermute | solution.py:613
  79.5 3.1 %copy-start.4 = (f32[2,144,128]{2,1,0:T(8,128)}, f32[2,144,128]{2,1,0:T(8,128)S(1)}, u32[]{:S(2)}) copy-start(f32[2,144,128]{2,1,0:T(8,128)S(1)} %collective-permute-done.7.misfit_right) | copy-start | bytes 442372
  82.6 0.7 copy-start.5

commit v2 on v1

--- a/solution.py
+++ b/solution.py
@@ -107,32 +107,6 @@
     out[...] = jnp.dot(chosen.T, value, precision=highest, preferred_element_type=jnp.float32)
 
 
-def neighbour_sum(field, stride):
-    rows, lanes = field.shape
-    return (
-        pltpu.roll(field, 1, 0)
-        + pltpu.roll(field, rows - 1, 0)
-        + pltpu.roll(field, stride, 1)
-        + pltpu.roll(field, lanes - stride, 1)
-    )
-
-
-def shifted_prior(field, reaction, stride):
-    image = (reaction - (SHIFT - 4.0)) * field - neighbour_sum(field, stride)
-    return jnp.where(reaction > 0.0, image * (1.0 / SCALE), 0.0)
-
-
-def expand(tiles, field, vectors, tile_x):
-    place = field * tile_x
-    tile, lane = place // LANES, place % LANES
-    out = []
-    for part in tiles:
-        source = part[tile + 1]
-        index = lane + lane_ids(source.shape) // vectors
-        out.append(jnp.take_along_axis(source, index, axis=1))
-    return jnp.concatenate(out, axis=1)
-
-
 def fold(row, stride):
     shift = LANES // 2
     while shift >= stride:
@@ -141,39 +115,176 @@
     return row
 
 
-def moment_kernel(vectors, flags, own, left, right, table, out, basis):
+def gather(tile, index):
+    return jnp.take_along_axis(tile, index, axis=1)
+
+
+def pick(which, values):
+    result = values[-1]
+    for n in range(len(values) - 2, -1, -1):
+        result = jnp.where(which == n, values[n], result)
+    return result
+
+
+def tile_rows(vectors, tiles, offset, tile):
+    return offset + (lane_ids((8, LANES)) // vectors) * tiles + tile
+
+
+def to_blocked(parts, vectors, tiles, offset):
+    tile_x = LANES // vectors
+    out = []
+    for t in range(tiles):
+        row = tile_rows(vectors, tiles, offset, t)
+        index = (row % tile_x) * vectors + lane_ids((8, LANES)) % vectors
+        out.append(pick(row // tile_x, [gather(part, index) for part in parts]))
+    return out
+
+
+def reblock(values, vectors, tiles, offset):
+    out = []
+    for t in range(tiles):
+        row = tile_rows(vectors, tiles, offset, t)
+        index = (row // len(values)) * vectors + lane_ids((8, LANES)) % vectors
+        out.append(pick(row % len(values), [gather(value, index) for value in values]))
+    return out
+
+
+def to_own(values, vectors, offset):
+    tiles = len(values)
+    row = lane_ids((8, LANES)) // vectors + LANES // vectors - offset
+    index = (row // tiles) * vectors + lane_ids((8, LANES)) % vectors
+    return pick(row % tiles, [gather(value, index) for value in values])
+
+
+def split_rows(source, target, flag=None):
+    count = target.shape[-3]
+    for i in range(count):
+        value = source[pl.ds(i, 8, stride=count), :]
+        target[i] = value if flag is None else value * flag
+
+
+def join_rows(source, target):
+    count = source.shape[0]
+    for i in range(count):
+        target[pl.ds(i, 8, stride=count), :] = source[i]
+
+
+def put_tile(field, at, t, tiles, stride, value):
+    field[(*at, t + 1)] = value
+    if t == 0:
+        field[(*at, tiles + 1)] = pltpu.roll(value, LANES - stride, 1)
+    if t == tiles - 1:
+        field[(*at, 0)] = pltpu.roll(value, stride, 1)
+
+
+def lateral_sum(field, at, i, t):
+    return (field[(*at, i, t + 1)] + field[(*at, i + 2, t + 1)]) + (
+        field[(*at, i + 1, t)] + field[(*at, i + 1, t + 2)]
+    )
+
+
+def wrap_rows(field, at, count, tiles):
+    for t in range(1, tiles + 1):
+        field[(*at, 0, t)] = pltpu.roll(field[(*at, count, t)], 1, 0)
+        field[(*at, count + 1, t)] = pltpu.roll(field[(*at, 1, t)], 7, 0)
+
+
+def wrap_layers(field, tiles):
+    count = field.shape[2] - 2
+
+    def body(k, carry):
+        for c in range(2):
+            wrap_rows(field, (c, k), count, tiles)
+        return carry
+
+    lax.fori_loop(0, field.shape[1], body, 0)
+
+
+def own_cells(vectors, tiles, offset, count, tile_y, i, t):
+    tile_x = LANES // vectors
+    row = tile_rows(vectors, tiles, offset, t)
+    column = row_ids((8, LANES)) * count + i
+    return (row >= tile_x) & (row < 2 * tile_x) & (column >= HALO) & (column < HALO + tile_y)
+
+
+def shifted_prior(field, i, t, reaction):
+    image = (reaction - (SHIFT - 4.0)) * field[i + 1, t + 1] - lateral_sum(field, (), i, t)
+    return jnp.where(reaction > 0.0, image * (1.0 / SCALE), 0.0)
+
+
+def krylov(first, second, third, reaction, vectors, count, tile_y):
+    tiles = reaction.shape[1]
+
+    def step(source, target):
+        wrap_rows(source, (), count, tiles)
+        for i in range(count):
+            for t in range(tiles):
+                value = shifted_prior(source, i, t, reaction[i, t])
+                put_tile(target, (i + 1,), t, tiles, vectors, value)
+
+    step(first, second)
+    step(second, third)
+    wrap_rows(third, (), count, tiles)
+    total = jnp.zeros((8, LANES), jnp.float32)
+    for i in range(count):
+        for t in range(tiles):
+            value = shifted_prior(third, i, t, reaction[i, t]) * third[i + 1, t + 1]
+            total = total + jnp.where(own_cells(vectors, tiles, 0, count, tile_y, i, t), value, 0.0)
+    return total
+
+
+def moment_kernel(
+    vectors, flags, own, left, right, table, out, basis, fields, parts, reaction, v0, v1, v2
+):
     tile_x = LANES // vectors
     rows = own.shape[1]
-    weights = (flags[0], None, flags[1])
-
-    def part_tile(t):
-        result = []
-        for ref, flag in zip((left, own, right), weights):
-            value = ref[t]
-            result.append(value if flag is None else value * flag)
-        return result
-
-    place = F_REACT * tile_x
-    tile, lane = place // LANES, place % LANES
-    index = lane + lane_ids((rows, LANES)) // vectors
-    reaction = jnp.concatenate(
-        [jnp.take_along_axis(part, index, axis=1) for part in part_tile(tile + 1)], axis=1
-    )
-    v0 = jnp.concatenate(part_tile(0), axis=1)
-    v1 = shifted_prior(v0, reaction, vectors)
-    v2 = shifted_prior(v1, reaction, vectors)
-    v3 = shifted_prior(v2, reaction, vectors)
-    for i, value in enumerate((v0, v1, v2)):
+    count = rows // 8
+    tile_y = rows - 2 * HALO
+    for p, (ref, flag) in enumerate(((left, flags[0]), (own, None), (right, flags[1]))):
+        for t in range(own.shape[0]):
+            split_rows(ref.at[t], parts.at[p, t], flag)
+    lane = lane_ids((8, LANES))
+
+    def arrange(i, carry):
+        for t, value in enumerate(to_blocked([parts[p, 0, i] for p in range(3)], vectors, 3, 0)):
+            put_tile(v0, (i + 1,), t, 3, vectors, value)
+        for q in range(fields.shape[0]):
+            per_tile = LANES // (4 * tile_x)
+            index = (q % per_tile) * 4 * tile_x + (lane // 32) * tile_x + lane % tile_x
+            fields[q, i] = pick(
+                (lane % 32) // tile_x, [gather(parts[p, 1 + q // per_tile, i], index) for p in range(3)]
+            )
         for t in range(3):
-            basis[i, t] = value[:, t * LANES : (t + 1) * LANES]
-    own_of = [v[HALO : rows - HALO, LANES : 2 * LANES] for v in (v0, v1, v2, v3)]
-    pairs = ((0, 0), (0, 1), (1, 1), (1, 2), (2, 2), (2, 3))
+            reaction[i, t] = expand(fields, F_REACT, i, t, 3, 0, vectors)
+        return carry
+
+    lax.fori_loop(0, count, arrange, 0)
+    last = krylov(v0, v1, v2, reaction, vectors, count, tile_y)
+    sums = [jnp.zeros((8, LANES), jnp.float32) for _ in range(5)]
+    for i in range(count):
+        for t in range(3):
+            mine = own_cells(vectors, 3, 0, count, tile_y, i, t)
+            a, b, c = v0[i + 1, t + 1], v1[i + 1, t + 1], v2[i + 1, t + 1]
+            basis[0, i, t] = a
+            basis[1, i, t] = b
+            basis[2, i, t] = c
+            a, b, c = [jnp.where(mine, v, 0.0) for v in (a, b, c)]
+            sums = [
+                total + one * two
+                for total, one, two in zip(sums, (a, a, b, b, c), (a, b, b, c, c))
+            ]
+    sums.append(last)
     group = lane_ids((1, LANES)) // vectors
     message = jnp.zeros((1, LANES), jnp.float32)
-    for j, (a, b) in enumerate(pairs):
-        total = fold(jnp.sum(own_of[a] * own_of[b], axis=0, keepdims=True), vectors)
+    for j, value in enumerate(sums):
+        total = fold(jnp.sum(value, axis=0, keepdims=True), vectors)
         message = jnp.where(group == j + 1, total, message)
     out[...] = table[...] + message
+
+
+def expand(fields, field, i, t, tiles, offset, vectors):
+    index = (field % 4) * 32 + tile_rows(vectors, tiles, offset, t)
+    return gather(fields[field // 4, i], index)
 
 
 def galerkin(moments):
@@ -196,153 +307,146 @@
     return y0, y1, y2
 
 
-def split_rows(source, target, flag=None):
-    count = target.shape[-3]
-    for i in range(count):
-        value = source[pl.ds(i, 8, stride=count), :]
-        target[i] = value if flag is None else value * flag
-
-
-def join_rows(source, target):
-    count = source.shape[0]
-    for t in range(target.shape[0]):
-        for i in range(count):
-            target[t, pl.ds(i, 8, stride=count), :] = source[i, :, t * LANES : (t + 1) * LANES]
-
-
-def joined(flat):
-    return jnp.concatenate([flat[t] for t in range(3)], axis=1)
-
-
-def split_parts(own, left, right, flags, parts):
-    for p, (ref, flag) in enumerate(((left, flags[0]), (own, None), (right, flags[1]))):
-        for t in range(own.shape[0]):
-            split_rows(ref.at[t], parts.at[p, t], flag)
-
-
-def prepare_row(i, parts, ratio, pivot, bed_col, top_col, vectors, tile_x, layer_count):
-    tiles = [[parts[p, t, i] for t in range(parts.shape[1])] for p in range(3)]
-    get = functools.partial(expand, tiles, vectors=vectors, tile_x=tile_x)
-    inv_lat, top, depth = get(F_INV_LAT), get(F_TOP), get(F_LAYER)
-    ratios, pivots = [], []
-    for k in range(layer_count):
-        pivots.append(get(F_PIVOT + k))
-        pivot[k, i] = pivots[k]
-        if k + 1 < layer_count:
-            ratios.append(get(F_RATIO + k))
-            ratio[k, i] = ratios[k]
+def expand_all(fields, wide, vectors, offset):
+    groups, count = fields.shape[:2]
+    value = fields[...].reshape(groups * count * 8, LANES)
+    high = value.astype(jnp.bfloat16)
+    value = value - high.astype(jnp.float32)
+    middle = value.astype(jnp.bfloat16)
+    low = (value - middle.astype(jnp.float32)).astype(jnp.bfloat16)
+    both = jnp.concatenate([high, middle], axis=1)
+    lanes = wide.shape[-1]
+    shape = (2 * LANES, lanes)
+    column = lane_ids(shape)
+    row = offset + (column % LANES // vectors) * (lanes // LANES) + column // LANES
+    source = row_ids(shape) % LANES
+    for j in range(4):
+        chosen = (source == j * 32 + row).astype(jnp.float32).astype(jnp.bfloat16)
+        out = jnp.dot(both, chosen, preferred_element_type=jnp.float32)
+        out = out + jnp.dot(low, chosen[:LANES], preferred_element_type=jnp.float32)
+        wide[j] = out.reshape(groups, count, 8, lanes)
+
+
+def get_field(wide, field, i, t):
+    return wide[field % 4, field // 4, i, :, t * LANES : (t + 1) * LANES]
+
+
+def prepare_row(wide, i, bed_col, top_col, layer_count, tiles):
+    across = range(tiles)
+    get = functools.partial(get_field, wide, i=i)
+    inv_lat = [get(F_INV_LAT, t=t) for t in across]
+    top = [get(F_TOP, t=t) for t in across]
+    depth = [get(F_LAYER, t=t) for t in across]
     forward = [inv_lat]
     for k in range(1, layer_count):
-        forward.append(ratios[k - 1] * forward[k - 1])
-    bed, surf = None, None
+        forward.append([get(F_RATIO + k - 1, t=t) * forward[k - 1][t] for t in across])
+    beds, tops = [None] * layer_count, [None] * layer_count
     for k in range(layer_count - 1, -1, -1):
-        is_top = depth == float(k + 1)
-        if bed is None:
-            bed = pivots[k] * forward[k]
-            surf = jnp.where(is_top, top, 0.0)
-        else:
-            bed = pivots[k] * forward[k] + ratios[k] * bed
-            surf = jnp.where(is_top, top, ratios[k] * surf)
-        bed_col[k, i] = bed
-        top_col[k, i] = surf
-    return get, inv_lat
-
-
-def lateral_sum(field, c, k, i, stride):
-    centre = field[c, k, i + 1]
-    lanes = centre.shape[1]
-    return (
-        field[c, k, i]
-        + field[c, k, i + 2]
-        + pltpu.roll(centre, stride, 1)
-        + pltpu.roll(centre, lanes - stride, 1)
-    )
-
-
-def wrap_rows(field):
-    count = field.shape[2] - 2
-
-    def body(k, carry):
-        for c in range(2):
-            field[c, k, 0] = pltpu.roll(field[c, k, count], 1, 0)
-            field[c, k, count + 1] = pltpu.roll(field[c, k, 1], 7, 0)
+        beds[k], tops[k] = [], []
+        for t in across:
+            bed = get(F_PIVOT + k, t=t) * forward[k][t]
+            below = 0.0
+            if k + 1 < layer_count:
+                ratio = get(F_RATIO + k, t=t)
+                bed = bed + ratio * beds[k + 1][t]
+                below = ratio * tops[k + 1][t]
+            surf = jnp.where(depth[t] == float(k + 1), top[t], below)
+            if bed_col is not None:
+                bed_col[k, i, t] = bed
+            top_col[k, i, t] = surf
+            beds[k].append(bed)
+            tops[k].append(surf)
+    return inv_lat, beds, tops
+
+
+def put_outer(field, i, columns, values, stride):
+    tiles = len(values[0])
+    right = [pltpu.roll(v[0], LANES - stride, 1) for v in values]
+    left = [pltpu.roll(v[tiles - 1], stride, 1) for v in values]
+    for k, column in enumerate(columns):
+        right_column = pltpu.roll(column[0], LANES - stride, 1)
+        left_column = pltpu.roll(column[tiles - 1], stride, 1)
+        for c, value in enumerate(values):
+            field[c, k, i + 1, 0] = left_column * left[c]
+            for t in range(tiles):
+                field[c, k, i + 1, t + 1] = column[t] * value[t]
+            field[c, k, i + 1, tiles + 1] = right_column * right[c]
+
+
+def sweep(source, target, wide, stride, bed_source=None, top_col=None, top_source=None):
+    layer_count, count, tiles = target.shape[1], target.shape[2] - 2, target.shape[3] - 2
+    across = [(t, c) for t in range(tiles) for c in range(2)]
+
+    def body(i, carry):
+        carried = []
+        for k in range(layer_count):
+            now = {}
+            for t, c in across:
+                value = lateral_sum(source, (c, k), i, t)
+                if k > 0:
+                    value = value + get_field(wide, F_RATIO + k - 1, i, t) * carried[k - 1][t, c]
+                elif bed_source is not None:
+                    value = value + bed_source[c, i, t]
+                now[t, c] = value
+            carried.append(now)
+        solved = {}
+        for k in range(layer_count - 1, -1, -1):
+            for t, c in across:
+                value = get_field(wide, F_PIVOT + k, i, t) * carried[k][t, c]
+                if k + 1 < layer_count:
+                    value = value + get_field(wide, F_RATIO + k, i, t) * solved[t, c]
+                solved[t, c] = value
+                if top_source is not None:
+                    value = value + top_col[k, i, t] * top_source[c, i, t]
+                put_tile(target, (c, k, i + 1), t, tiles, stride, value)
         return carry
 
-    lax.fori_loop(0, field.shape[1], body, 0)
-
-
-def sweep(source, target, ratio, pivot, stride, bed_source=None, top_col=None, top_source=None):
-    layer_count = pivot.shape[0]
-
-    def body(i, carry):
-        for c in range(2):
-            carried = []
-            for k in range(layer_count):
-                value = lateral_sum(source, c, k, i, stride)
-                if k > 0:
-                    value = value + ratio[k - 1, i] * carried[k - 1]
-                elif bed_source is not None:
-                    value = value + bed_source[c, i]
-                carried.append(value)
-            solved = None
-            extra = top_source[c, i] if top_source is not None else None
-            for k in range(layer_count - 1, -1, -1):
-                value = pivot[k, i] * carried[k]
-                if solved is not None:
-                    value = value + ratio[k, i] * solved
-                solved = value
-                if extra is not None:
-                    value = value + top_col[k, i] * extra
-                target[c, k, i + 1] = value
-        return carry
-
-    lax.fori_loop(0, pivot.shape[1], body, 0)
-    wrap_rows(target)
+    lax.fori_loop(0, count, body, 0)
+    wrap_layers(target, tiles)
 
 
 def velocity_kernel(
-    vectors, flags, message, own, left, right, basis,
+    vectors, flags, message, basis, fields,
     misfit, low, high,
-    ratio, pivot, bed_col, top_col, one, two, source, parts, flat, smooth, surface, flat_out,
+    wide, top_col, one, two, source, surface, flat,
 ):
     tile_x = LANES // vectors
-    layer_count = pivot.shape[0]
-    total_rows = own.shape[1]
-    count = total_rows // 8
-    tile_y = total_rows - 2 * HALO
+    layer_count, count, tiles = top_col.shape[:3]
+    tile_y = count * 8 - 2 * HALO
+    offset = tile_x // 2
     group = lane_ids((8, LANES)) // vectors
     summed = jnp.broadcast_to(jnp.sum(message[...], axis=0, keepdims=True), (8, LANES))
     moments = [fold(jnp.where(group == j + 1, summed, 0.0), vectors) for j in range(6)]
-    y = [v[0:1] for v in galerkin(moments)]
-    for t in range(3):
-        flat[t] = y[0] * basis[0, t] + y[1] * basis[1, t] + y[2] * basis[2, t]
-    for t in range(3):
-        split_rows(flat.at[t], smooth.at[t])
-    split_parts(own, left, right, flags, parts)
+    y = galerkin(moments)
 
     def prepare(i, carry):
-        get, inv_lat = prepare_row(
-            i, parts, ratio, pivot, bed_col, top_col, vectors, tile_x, layer_count
-        )
+        smooth = [y[0] * basis[0, i, t] + y[1] * basis[1, i, t] + y[2] * basis[2, i, t] for t in range(3)]
+        smooth = reblock(smooth, vectors, tiles, offset)
+        inv_lat, beds, _ = prepare_row(wide, i, None, top_col, layer_count, tiles)
+        values = [
+            [get_field(wide, F_BED + c, i, t) * smooth[t] for t in range(tiles)] for c in range(2)
+        ]
         for c in range(2):
-            bed = get(F_BED + c) * jnp.concatenate([smooth[t, i] for t in range(3)], axis=1)
-            source[c, i] = bed * inv_lat
-            for k in range(layer_count):
-                one[c, k, i + 1] = bed_col[k, i] * bed
+            for t in range(tiles):
+                source[c, i, t] = values[c][t] * inv_lat[t]
+        put_outer(one, i, beds, values, vectors)
         return carry
 
+    expand_all(fields, wide, vectors, offset)
+
     lax.fori_loop(0, count, prepare, 0)
-    wrap_rows(one)
-    sweep(one, two, ratio, pivot, vectors, bed_source=source)
-    sweep(two, one, ratio, pivot, vectors, bed_source=source)
-    middle = slice(LANES, 2 * LANES)
+    wrap_layers(one, tiles)
+    sweep(one, two, wide, vectors, bed_source=source)
+    sweep(two, one, wide, vectors, bed_source=source)
 
     def finish(i, carry):
+        across = [(c, t) for c in range(2) for t in range(tiles)]
+        values = {(c, t): top_col[0, i, t] * source[c, i, t] for c, t in across}
+        for k in range(layer_count):
+            for c, t in across:
+                values[c, t] = values[c, t] + top_col[k, i, t] * lateral_sum(one, (c, k), i, t)
         for c in range(2):
-            total = top_col[0, i, :, middle] * source[c, i, :, middle]
-            for k in range(layer_count):
-                total = total + top_col[k, i, :, middle] * lateral_sum(one, c, k, i, vectors)[:, middle]
-            surface[c, i] = total
+            surface[c, i] = to_own([values[c, t] for t in range(tiles)], vectors, offset)
         return carry
 
     lax.fori_loop(0, count, finish, 0)
@@ -358,67 +462,70 @@
             total = total + jnp.dot(
                 at_row.T, at_lane, precision=highest, preferred_element_type=jnp.float32
             )
-        join_rows(surface.at[c], flat_out)
-        misfit[c] = total * flat_out[0, HALO : HALO + tile_y, :]
+        join_rows(surface.at[c], flat)
+        misfit[c] = total * flat[HALO : HALO + tile_y, :]
     low[...] = misfit[:, 0:HALO, :]
     high[...] = misfit[:, tile_y - HALO :, :]
 
 
 def adjoint_kernel(
-    vectors, flags, own, left, right, misfit, misfit_left, misfit_right, previous,
+    vectors, flags, fields, misfit, misfit_left, misfit_right, basis, previous,
     out, stacked,
-    ratio, pivot, bed_col, top_col, one, two, source, parts, flat, pulled, bed, reaction_all, lateral, sides,
+    wide, top_col, one, two, source, bed_col, sides, bed, reaction, v0, v1, v2, natural, flat,
 ):
     tile_x = LANES // vectors
-    layer_count = pivot.shape[0]
-    total_rows = own.shape[1]
-    count = total_rows // 8
-    split_parts(own, left, right, flags, parts)
+    layer_count, count, tiles = top_col.shape[:3]
+    tile_y = count * 8 - 2 * HALO
     for c in range(2):
         split_rows(misfit_left.at[c], sides.at[c, 0], flags[0])
         split_rows(misfit.at[c], sides.at[c, 1])
         split_rows(misfit_right.at[c], sides.at[c, 2], flags[1])
 
     def prepare(i, carry):
-        get, inv_lat = prepare_row(
-            i, parts, ratio, pivot, bed_col, top_col, vectors, tile_x, layer_count
-        )
-        reaction_all[i] = get(F_REACT)
-        lateral[i] = inv_lat
-        for c in range(2):
-            value = jnp.concatenate([sides[c, t, i] for t in range(3)], axis=1)
-            source[c, i] = value
-            bed[c, i] = get(F_BED + c)
-            for k in range(layer_count):
-                one[c, k, i + 1] = top_col[k, i] * value
+        values = [to_blocked([sides[c, p, i] for p in range(3)], vectors, tiles, 0) for c in range(2)]
+        inv_lat, _, tops = prepare_row(wide, i, bed_col, top_col, layer_count, tiles)
+        for t in range(tiles):
+            reaction[i, t] = get_field(wide, F_REACT, i, t)
+            total = None
+            for c in range(2):
+                value = values[c][t]
+                source[c, i, t] = value
+                drag = get_field(wide, F_BED + c, i, t)
+                bed[c, i, t] = drag
+                total = drag * value if total is None else total + drag * value
+            v1[i + 1, t + 1] = total * (tops[0][t] * inv_lat[t])
+        put_outer(one, i, tops, values, vectors)
         return carry
 
+    expand_all(fields, wide, vectors, 0)
+
     lax.fori_loop(0, count, prepare, 0)
-    wrap_rows(one)
-    sweep(one, two, ratio, pivot, vectors, top_col=top_col, top_source=source)
-    sweep(two, one, ratio, pivot, vectors, top_col=top_col, top_source=source)
+    wrap_layers(one, tiles)
+    sweep(one, two, wide, vectors, top_col=top_col, top_source=source)
+    sweep(two, one, wide, vectors, top_col=top_col, top_source=source)
 
     def finish(i, carry):
-        total = None
-        for c in range(2):
-            value = top_col[0, i] * lateral[i] * source[c, i]
-            for k in range(layer_count):
-                value = value + bed_col[k, i] * lateral_sum(one, c, k, i, vectors)
-            value = bed[c, i] * value
-            total = value if total is None else total + value
-        pulled[i] = total
+        totals = {}
+        for k in range(layer_count):
+            for c in range(2):
+                for t in range(tiles):
+                    value = bed_col[k, i, t] * lateral_sum(one, (c, k), i, t)
+                    totals[c, t] = value if k == 0 else totals[c, t] + value
+        for t in range(tiles):
+            value = v1[i + 1, t + 1] + (bed[0, i, t] * totals[0, t] + bed[1, i, t] * totals[1, t])
+            put_tile(v0, (i + 1,), t, tiles, vectors, value)
         return carry
 
     lax.fori_loop(0, count, finish, 0)
-    join_rows(reaction_all, flat)
-    reaction = joined(flat)
-    join_rows(pulled, flat)
-    v0 = joined(flat)
-    v1 = shifted_prior(v0, reaction, vectors)
-    v2 = shifted_prior(v1, reaction, vectors)
-    v3 = shifted_prior(v2, reaction, vectors)
-    v0, v1, v2, v3 = [v[HALO : total_rows - HALO, LANES : 2 * LANES] for v in (v0, v1, v2, v3)]
-    x = own[0, HALO : total_rows - HALO, :]
+    last = krylov(v0, v1, v2, reaction, vectors, count, tile_y)
+    own = []
+    for n, field in enumerate((v0, v1, v2, basis.at[0])):
+        at = 0 if n == 3 else 1
+        for i in range(count):
+            natural[i] = to_own([field[i + at, t + at] for t in range(tiles)], vectors, 0)
+        join_rows(natural, flat)
+        own.append(flat[HALO : HALO + tile_y, :])
+    v0, v1, v2, x = own
     p = previous[...]
     flipped = [v.T for v in (v0, v1, v2, p, x)]
     for i, value in enumerate(flipped):
@@ -442,7 +549,7 @@
             block = block + product[at * vectors : (at + 1) * vectors]
         block = fold(block, vectors)
         halves[n // tile_x] = jnp.where(group == n % tile_x, block, halves[n // tile_x])
-    last = fold(jnp.sum(v2 * v3, axis=0, keepdims=True), vectors)
+    last = fold(jnp.sum(last, axis=0, keepdims=True), vectors)
     n = len(pairs)
     halves[n // tile_x] = jnp.where(group == n % tile_x, last, halves[n // tile_x])
     both = jnp.concatenate(halves, axis=1)
@@ -542,7 +649,6 @@
     backward_x = [(i, (i - 1) % size_x) for i in range(size_x)]
     f32 = jnp.float32
     rows = tile_y + 2 * HALO
-    wide = 3 * LANES
     tiles = -(-(vectors * tile_x + FIELDS * tile_x) // LANES)
     smem = pl.BlockSpec(memory_space=pltpu.SMEM)
     vmem = pl.BlockSpec(memory_space=pltpu.VMEM)
@@ -572,40 +678,41 @@
     left = lax.ppermute(own, "mx", forward_x)
     right = lax.ppermute(own, "mx", backward_x)
 
-    message, basis = pl.pallas_call(
+    count = rows // 8
+    groups = -(-FIELDS // 4)
+
+    def blocked(*dims):
+        return pltpu.VMEM((*dims, 8, LANES), f32)
+
+    message, basis, fields = pl.pallas_call(
         functools.partial(moment_kernel, vectors),
-        out_shape=(shape(devices, LANES), shape(3, 3, rows, LANES)),
+        out_shape=(
+            shape(devices, LANES), shape(3, count, 3, 8, LANES), shape(groups, count, 8, LANES)
+        ),
         in_specs=[smem, vmem, vmem, vmem, vmem],
+        scratch_shapes=[blocked(3, tiles, count), blocked(count, 3)] + [blocked(count + 2, 5)] * 3,
         compiler_params=params(),
         name="moments",
     )(flags, own, left, right, table)
     message = lax.all_to_all(message, AXES, split_axis=0, concat_axis=0, tiled=True)
 
-    count = rows // 8
-    columns = [
-        pltpu.VMEM((layer_count - 1, count, 8, wide), f32),
-        pltpu.VMEM((layer_count, count, 8, wide), f32),
-        pltpu.VMEM((layer_count, count, 8, wide), f32),
-        pltpu.VMEM((layer_count, count, 8, wide), f32),
-        pltpu.VMEM((2, layer_count, count + 2, 8, wide), f32),
-        pltpu.VMEM((2, layer_count, count + 2, 8, wide), f32),
-        pltpu.VMEM((2, count, 8, wide), f32),
-        pltpu.VMEM((3, tiles, count, 8, LANES), f32),
-        pltpu.VMEM((3, rows, LANES), f32),
-    ]
+    def columns(width):
+        return [
+            pltpu.VMEM((4, groups, count, 8, width * LANES), f32),
+            blocked(layer_count, count, width),
+            blocked(2, layer_count, count + 2, width + 2),
+            blocked(2, layer_count, count + 2, width + 2),
+            blocked(2, count, width),
+        ]
+
     misfit, low, high = pl.pallas_call(
         functools.partial(velocity_kernel, vectors),
         out_shape=(shape(2, tile_y, LANES), shape(2, HALO, LANES), shape(2, HALO, LANES)),
-        in_specs=[smem] + [vmem] * 5,
-        scratch_shapes=columns
-        + [
-            pltpu.VMEM((3, count, 8, LANES), f32),
-            pltpu.VMEM((2, count, 8, LANES), f32),
-            pltpu.VMEM((1, rows, LANES), f32),
-        ],
+        in_specs=[smem] + [vmem] * 3,
+        scratch_shapes=columns(2) + [blocked(2, count), pltpu.VMEM((rows, LANES), f32)],
         compiler_params=params(),
         name="velocity",
-    )(flags, message, own, left, right, basis)
+    )(flags, message, basis, fields)
 
     from_low = lax.ppermute(high, "my", forward_y)
     from_high = lax.ppermute(low, "my", backward_y)
@@ -616,18 +723,14 @@
     products, stacked = pl.pallas_call(
         functools.partial(adjoint_kernel, vectors),
         out_shape=(shape(size_x, vectors, 2 * LANES), shape(tile_x, 5 * vectors, tile_y)),
-        in_specs=[smem] + [vmem] * 7,
-        scratch_shapes=columns
-        + [
-            pltpu.VMEM((count, 8, wide), f32),
-            pltpu.VMEM((2, count, 8, wide), f32),
-            pltpu.VMEM((count, 8, wide), f32),
-            pltpu.VMEM((count, 8, wide), f32),
-            pltpu.VMEM((2, 3, count, 8, LANES), f32),
-        ],
+        in_specs=[smem] + [vmem] * 6,
+        scratch_shapes=columns(3)
+        + [blocked(layer_count, count, 3), blocked(2, 3, count), blocked(2, count, 3), blocked(count, 3)]
+        + [blocked(count + 2, 5)] * 3
+        + [blocked(count), pltpu.VMEM((rows, LANES), f32)],
         compiler_params=params(),
         name="adjoint",
-    )(flags, own, left, right, misfit, misfit_left, misfit_right, previous)
+    )(flags, fields, misfit, misfit_left, misfit_right, basis, previous)
 
     products = lax.all_to_all(products, "mx", split_axis=0, concat_axis=0, tiled=True)
     products = pl.pallas_call(

time: 143 us -> 134 us (0.937)
  Pallas kernels: 65.4 us -> 56.8 us
    pallas_call x1, Pallas kernels: 27.3 us -> 21.3 us  [shards(): pl.pallas_call(functools.partial(adjoint_kernel, vectors), out_shape=(sha...]
    pallas_call x1, Pallas kernels: 24.9 us -> 19.1 us  [shards(): pl.pallas_call(functools.partial(velocity_kernel, vectors), out_shape=(sh...]
    pallas_call x1, Pallas kernels: 2.69 us -> 5.84 us  [shards(): pl.pallas_call(functools.partial(moment_kernel, vectors), out_shape=(shap...]
where the time goes in v2:
time: 134 us
  Pallas kernels  56.8 us (42%)
  blocking collectives  44.9 us (34%)
  starting transfers between devices  13.8 us (10%)
  waiting for transfers between devices  9.53 us (7%)
  local copies, waits for them, and re-layouts  5.34 us (4%)
  other arithmetic  2.5 us (2%)
    pallas_call x1, Pallas kernels, shards(): pl.pallas_call(functools.partial(adjoint_kernel, vectors), out_shape=(sha...  21.3 us
    all_to_all x1, blocking collectives, shards(): lax.all_to_all(message, AXES, split_axis=0, concat_axis=0, tiled=True)  19.4 us
    pallas_call x1, Pallas kernels, shards(): pl.pallas_call(functools.partial(velocity_kernel, vectors), out_shape=(sh...  19.1 us
    all_to_all x1, blocking collectives, shards(): lax.all_to_all(products, 'my', split_axis=0, concat_axis=0, tiled=True)  15.3 us
    all_to_all x1, blocking collectives, shards(): lax.all_to_all(products, 'mx', split_axis=0, concat_axis=0, tiled=True)  10.1 us
    ppermute x2, starting transfers between devices, shards(): from_high = lax.ppermute(low, 'my', backward_y)  9.33 us
    pallas_call x1, Pallas kernels, shards(): pl.pallas_call(functools.partial(moment_kernel, vectors), out_shape=(shap...  5.84 us
    pallas_call x1, Pallas kernels, shards(): pl.pallas_call(functools.partial(finish_kernel, float(cells)), out_shape=...  4.57 us
  transfers between devices with their start and end apart: 8, of which 5 were waited for; matrix products, arithmetic and copies ran while one was open for 2% of the time, Pallas kernels for 2%

profile of v2, /device:TPU:0, one launch (start us, length us, event | category | flops | bytes accessed | tf_op | source)
XLA Modules:
  0.0 133.6 jit_solution(3976111943662486192)
XLA Ops:
  0.6 2.0 %pack.1 = (f32[4,128,128]{2,1,0:T(8,128)}, f32[128,128]{1,0:T(8,128)}, f32[4,8,128]{2,1,0:T(8,128)}, f32[4,8,128]{2,1,0:T(8,128)}) custom-call(f32[16,8,128]{2,1,0:T(8,128)} %block.1, f32[16,8,128]{2,1,0:T(8,128)} %previous.1, f32[8,128]{1,0:T(8,128)} %reaction.1, f32[15,8,128]{2,1,0:T(8,128)} %vert.1, f32[16,8,128]{2,1,0:T(8,128)} %horiz.1, ...), custom_call_target="tpu_custom_call" | custom-call | tf_op jit(solution)/shard_map/pack/pallas_call | solution.py:659
  2.6 2.0 %collective-permute-start = (f32[4,8,128]{2,1,0:T(8,128)}, f32[4,8,128]{2,1,0:T(8,128)S(1)}, u32[]{:S(2)}, u32[]{:S(2)}) collective-permute-start(f32[4,8,128]{2,1,0:T(8,128)} %get-tuple-element.15), channel_id=1, source_target_pairs={{0,1},{1,2},{2,3},{3,4},{4,5},{5,6},{6,7},{7,8},{8,9},{9,10},{10,1... | collective-permute-start | bytes 49160 | tf_op jit(solution)/shard_map/ppermute | solution.py:675
  4.6 4.6 %collective-permute-start.1 = (f32[4,8,128]{2,1,0:T(8,128)}, f32[4,8,128]{2,1,0:T(8,128)S(1)}, u32[]{:S(2)}, u32[]{:S(2)}) collective-permute-start(f32[4,8,128]{2,1,0:T(8,128)} %get-tuple-element.17), channel_id=1, source_target_pairs={{0,15},{1,0},{2,1},{3,2},{4,3},{5,4},{6,5},{7,6},{8,7},{9,8},{10,9... | collective-permute-start | bytes 49160 | tf_op jit(solution)/shard_map/ppermute | solution.py:676
  9.2 1.9 %collective-permute-done = f32[4,8,128]{2,1,0:T(8,128)S(1)} collective-permute-done((f32[4,8,128]{2,1,0:T(8,128)}, f32[4,8,128]{2,1,0:T(8,128)S(1)}, u32[]{:S(2)}, u32[]{:S(2)}) %collective-permute-start) | collective-permute-done | bytes 16416 | tf_op jit(solution)/shard_map/ppermute | solution.py:675
  11.1 1.0 pad_maximum_fusion.own
  12.1 1.3 %collective-permute-start.3 = (f32[4,144,128]{2,1,0:T(8,128)S(1)}, f32[4,144,128]{2,1,0:T(8,128)S(1)}, u32[]{:S(2)}, u32[]{:S(2)}) collective-permute-start(f32[4,144,128]{2,1,0:T(8,128)S(1)} %pad_maximum_fusion.own), channel_id=1, source_target_pairs={{0,112},{16,0},{32,16},{48,32},{64,48},{80,64},{96,80},{112,96},{1... | collective-permute-start | bytes 884744 | tf_op jit(solution)/shard_map/ppermute | solution.py:679
  13.4 0.7 copy-done.7
  14.1 0.8 copy.20.dest
  14.9 0.7 copy-done.8
  15.6 0.8 copy.21.cell
  16.4 0.8 copy.22.weight
  17.2 2.5 %table.1 = f32[128,128]{1,0:T(8,128)} custom-call(s32[256,1]{1,0:T(8,128)} %copy.20.dest, s32[256,1]{1,0:T(8,128)} %copy.21.cell, f32[256,2]{1,0:T(8,128)} %copy.22.weight), custom_call_target="tpu_custom_call" | custom-call | tf_op jit(solution)/shard_map/table/pallas_call | solution.py:671
  19.6 0.6 add_convert_fusion.flags
  20.2 0.5 collective-permute-done.2.left
  20.8 0.2 copy-done.2
  21.0 0.7 copy-done.3
  21.7 5.8 %moments.1 = (f32[128,128]{1,0:T(8,128)}, f32[3,18,3,8,128]{4,3,2,1,0:T(8,128)}, f32[10,18,8,128]{3,2,1,0:T(8,128)}) custom-call(f32[2]{0:T(128)} %add_convert_fusion.flags, f32[4,144,128]{2,1,0:T(8,128)} %copy-done, f32[4,144,128]{2,1,0:T(8,128)} %copy-done.3, f32[4,144,128]{2,1,0:T(8,128)} %copy-done.2, f32[128,128]{1,0:T(8,128)} %table.1), custom_call_target="tpu_custom_call" | custom-call | tf_op jit(solution)/shard_map/moments/pallas_call | solution.py:687
  27.5 19.4 %all_to_all.21 = f32[128,1,128]{2,1,0:T(1,128)} all-to-all(f32[128,1,128]{2,1,0:T(1,128)} %bitcast.8), channel_id=1, replica_groups=mesh['mx'=8,'my'=16] {'mx','my'}, dimensions={0} | all-to-all | bytes 131072 | tf_op jit(solution)/shard_map/all_to_all | solution.py:697
  47.0 19.1 %velocity.3 = (f32[2,128,128]{2,1,0:T(8,128)}, f32[2,8,128]{2,1,0:T(8,128)}, f32[2,8,128]{2,1,0:T(8,128)}) custom-call(f32[2]{0:T(128)} %add_convert_fusion.flags, f32[128,128]{1,0:T(8,128)} %bitcast.7, f32[3,18,3,8,128]{4,3,2,1,0:T(8,128)} %get-tuple-element.20.basis, f32[10,18,8,128]{3,2,1,0:T(8,128)} %get-tuple-element.18.fields), custom_call_target="tpu_custom_call" | custom-call | tf_op jit(solution)/shard_map/velocity/pallas_call | solution.py:708
  66.1 0.7 collective-permute-start.4
  66.7 4.7 %collective-permute-start.5 = (f32[2,8,128]{2,1,0:T(8,128)}, f32[2,8,128]{2,1,0:T(8,128)S(1)}, u32[]{:S(2)}, u32[]{:S(2)}) collective-permute-start(f32[2,8,128]{2,1,0:T(8,128)} %get-tuple-element.23), channel_id=1, source_target_pairs={{0,15},{1,0},{2,1},{3,2},{4,3},{5,4},{6,5},{7,6},{8,7},{9,8},{10,9... | collective-permute-start | bytes 24584 | tf_op jit(solution)/shard_map/ppermute | solution.py:718
  71.4 1.8 %collective-permute-done.4 = f32[2,8,128]{2,1,0:T(8,128)S(1)} collective-permute-done((f32[2,8,128]{2,1,0:T(8,128)}, f32[2,8,128]{2,1,0:T(8,128)S(1)}, u32[]{:S(2)}, u32[]{:S(2)}) %collective-permute-start.4) | collective-permute-done | bytes 8224 | tf_op jit(solution)/shard_map/ppermute | solution.py:717
  73.3 0.9 pad_maximum_fusion.1.misfit
  74.2 0.5 collective-permute-start.6
  74.7 2.2 %collective-permute-done.7.misfit_right = f32[2,144,128]{2,1,0:T(8,128)S(1)} collective-permute-done((f32[2,144,128]{2,1,0:T(8,128)S(1)}, f32[2,144,128]{2,1,0:T(8,128)S(1)}, u32[]{:S(2)}, u32[]{:S(2)}) %collective-permute-start.7) | collective-permute-done | bytes 147488 | tf_op jit(solution)/shard_map/ppermute | solution.py:721
  76.9 3.1 %collective-permute-done.6.misfit_left = f32[2,144,128]{2,1,0:T(8,128)S(1)} collective-permute-done((f32[2,144,128]{2,1,0:T(8,128)S(1)}, f32[2,144,128]{2,1,0:T(8,128)S(1)}, u32[]{:S(2)}, u32[]{:S(2)}) %collective-permute-start.6) | collective-permute-done | bytes 147488 | tf_op jit(solution)/shard_map/ppermute | solution.py:720
  80.0 0.7 copy-done.5
  80.7 21.3 %adjoint.1 = (f32[8,16,256]{2,1,0:T(8,128)}, f32[8,80,128]{2,1,0:T(8,128)}) custom-call(f32[2]{0:T(128)} %add_convert_fusion.flags, f32[10,18,8,128]{3,2,1,0:T(8,128)} %get-tuple-element.18.fields, f32[2,144,128]{2,1,0:T(8,128)} %copy-done.1, f32[2,144,128]{2,1,0:T(8,128)} %copy-done.5, f32[2,144,128]{2,1,0:T(8,128)} %copy-done.4, ...), custom_call_target="tpu_custom_call" | custom-call | tf_op jit(solution)/shard_map/adjoint/pallas_call | solution.py:723
  102.0 10.1 %all_to_all.22.received = f32[8,16,256]{2,1,0:T(8,128)} all-to-all(f32[8,16,256]{2,1,0:T(8,128)} %get-tuple-element.25), channel_id=1, replica_groups=mesh['mx'=8,'my'=16] {'mx'}, dimensions={0} | all-to-all | bytes 262144 | tf_op jit(solution)/shard_map/all_to_all | solution.py:735
  112.1 1.6 %partial.1 = f32[16,16,256]{2,1,0:T(8,128)} custom-call(f32[8,16,256]{2,1,0:T(8,128)} %all_to_all.22.received), custom_call_target="tpu_custom_call" | custom-call | tf_op jit(solution)/shard_map/partial/pallas_call | solution.py:736
  113.7 15.3 %all_to_all.23.received = f32[16,16,256]{2,1,0:T(8,128)} all-to-all(f32[16,16,256]{2,1,0:T(8,128)} %partial.1), channel_id=1, replica_groups=mesh['mx'=8,'my'=16] {'my'}, dimensions={0} | all-to-all | bytes 524288 | tf_op jit(solution)/shard_map/all_to_all | solution.py:742
  129.0 4.6 %finish.1 = (f32[16,8,128]{2,1,0:T(8,128)}, f32[16,16]{1,0:T(8,128)}, f32[16,16]{1,0:T(8,128)}) custom-call(f32[16,16,256]{2,1,0:T(8,128)} %all_to_all.23.received, f32[8,80,128]{2,1,0:T(8,128)} %get-tuple-element.26.stacked, f32[16,16]{1,0:T(8,128)} %beta_ref.1), custom_call_target="tpu_custom_call" | custom-call | tf_op jit(solution)/shard_map/finish/pallas_call | solution.py:743
  (22 shorter events, 0.1 us)
Async XLA Ops:
  2.6 8.5 %collective-permute-start = (f32[4,8,128]{2,1,0:T(8,128)}, f32[4,8,128]{2,1,0:T(8,128)S(1)}, u32[]{:S(2)}, u32[]{:S(2)}) collective-permute-start(f32[4,8,128]{2,1,0:T(8,128)} %get-tuple-element.15), channel_id=1, source_target_pairs={{0,1},{1,2},{2,3},{3,4},{4,5},{5,6},{6,7},{7,8},{8,9},{9,10},{10,1... | collective-permute-start | bytes 49160 | tf_op jit(solution)/shard_map/ppermute | solution.py:675
  4.6 6.5 %collective-permute-start.1 = (f32[4,8,128]{2,1,0:T(8,128)}, f32[4,8,128]{2,1,0:T(8,128)S(1)}, u32[]{:S(2)}, u32[]{:S(2)}) collective-permute-start(f32[4,8,128]{2,1,0:T(8,128)} %get-tuple-element.17), channel_id=1, source_target_pairs={{0,15},{1,0},{2,1},{3,2},{4,3},{5,4},{6,5},{7,6},{8,7},{9,8},{10,9... | collective-permute-start | bytes 49160 | tf_op jit(solution)/shard_map/ppermute | solution.py:676
  12.1 7.6 %copy-start = (f32[4,144,128]{2,1,0:T(8,128)}, f32[4,144,128]{2,1,0:T(8,128)S(1)}, u32[]{:S(2)}) copy-start(f32[4,144,128]{2,1,0:T(8,128)S(1)} %pad_maximum_fusion.own) | copy-start | bytes 884740
  12.1 8.2 %collective-permute-start.3 = (f32[4,144,128]{2,1,0:T(8,128)S(1)}, f32[4,144,128]{2,1,0:T(8,128)S(1)}, u32[]{:S(2)}, u32[]{:S(2)}) collective-permute-start(f32[4,144,128]{2,1,0:T(8,128)S(1)} %pad_maximum_fusion.own), channel_id=1, source_target_pairs={{0,112},{16,0},{32,16},{48,32},{64,48},{80,64},{96,80},{112,96},{1... | collective-permute-start | bytes 884744 | tf_op jit(solution)/shard_map/ppermute | solution.py:679
  13.4 7.4 %collective-permute-start.2 = (f32[4,144,128]{2,1,0:T(8,128)S(1)}, f32[4,144,128]{2,1,0:T(8,128)S(1)}, u32[]{:S(2)}, u32[]{:S(2)}) collective-permute-start(f32[4,144,128]{2,1,0:T(8,128)S(1)} %pad_maximum_fusion.own), channel_id=1, source_target_pairs={{0,16},{16,32},{32,48},{48,64},{64,80},{80,96},{96,112},{112,0},{1... | collective-permute-start | bytes 884744 | tf_op jit(solution)/shard_map/ppermute | solution.py:678
  13.4 0.7 copy-start.7
  14.9 0.7 copy-start.8
  15.6 0.8 copy-start.6
  20.2 0.7 copy-start.2
  21.0 0.7 copy-start.3
  66.1 7.2 %collective-permute-start.4 = (f32[2,8,128]{2,1,0:T(8,128)}, f32[2,8,128]{2,1,0:T(8,128)S(1)}, u32[]{:S(2)}, u32[]{:S(2)}) collective-permute-start(f32[2,8,128]{2,1,0:T(8,128)} %get-tuple-element.21), channel_id=1, source_target_pairs={{0,1},{1,2},{2,3},{3,4},{4,5},{5,6},{6,7},{7,8},{8,9},{9,10},{10,1... | collective-permute-start | bytes 24584 | tf_op jit(solution)/shard_map/ppermute | solution.py:717
  66.7 6.5 %collective-permute-start.5 = (f32[2,8,128]{2,1,0:T(8,128)}, f32[2,8,128]{2,1,0:T(8,128)S(1)}, u32[]{:S(2)}, u32[]{:S(2)}) collective-permute-start(f32[2,8,128]{2,1,0:T(8,128)} %get-tuple-element.23), channel_id=1, source_target_pairs={{0,15},{1,0},{2,1},{3,2},{4,3},{5,4},{6,5},{7,6},{8,7},{9,8},{10,9... | collective-permute-start | bytes 24584 | tf_op jit(solution)/shard_map/ppermute | solution.py:718
  74.2 5.8 %copy-start.1 = (f32[2,144,128]{2,1,0:T(8,128)}, f32[2,144,128]{2,1,0:T(8,128)S(1)}, u32[]{:S(2)}) copy-start(f32[2,144,128]{2,1,0:T(8,128)S(1)} %pad_maximum_fusion.1.misfit) | copy-start | bytes 442372
  74.2 2.7 %collective-permute-start.7 = (f32[2,144,128]{2,1,0:T(8,128)S(1)}, f32[2,144,128]{2,1,0:T(8,128)S(1)}, u32[]{:S(2)}, u32[]{:S(2)}) collective-permute-start(f32[2,144,128]{2,1,0:T(8,128)S(1)} %pad_maximum_fusion.1.misfit), channel_id=1, source_target_pairs={{0,112},{16,0},{32,16},{48,32},{64,48},{80,64},{96,80},{112,96},{1... | collective-permute-start | bytes 442376 | tf_op jit(solution)/shard_map/ppermute | solution.py:721
  74.2 5.8 %collective-permute-start.6 = (f32[2,144,128]{2,1,0:T(8,128)S(1)}, f32[2,144,128]{2,1,0:T(8,128)S(1)}, u32[]{:S(2)}, u32[]{:S(2)}) collective-permute-start(f32[2,144,128]{2,1,0:T(8,128)S(1)} %pad_maximum_fusion.1.misfit), channel_id=1, source_target_pairs={{0,16},{16,32},{32,48},{48,64},{64,80},{80,96},{96,112},{112,0},{1... | collective-permute-start | bytes 442376 | tf_op jit(solution)/shard_map/ppermute | solution.py:720
  76.9 3.1 %copy-start.4 = (f32[2,144,128]{2,1,0:T(8,128)}, f32[2,144,128]{2,1,0:T(8,128)S(1)}, u32[]{:S(2)}) copy-start(f32[2,144,128]{2,1,0:T(8,128)S(1)} %collective-permute-done.7.misfit_right) | copy-start | bytes 442372
  80.0 0.7 copy-start.5

commit v3 on v2

--- a/solution.py
+++ b/solution.py
@@ -87,12 +87,25 @@
 
 
 def table_kernel(dest, cell, weight, out):
-    count = dest.shape[0]
+    count = dest.shape[1]
     devices = out.shape[0]
-    onehot = dest[...] == lane_ids((count, devices))
+    rows = jnp.concatenate(
+        [
+            dest[...].astype(jnp.float32),
+            cell[...].astype(jnp.float32),
+            weight[...],
+            jnp.zeros((4, count), jnp.float32),
+        ],
+        axis=0,
+    )
+    columns = rows.T
+    target = columns[:, 0:1].astype(jnp.int32)
+    onehot = target == lane_ids((count, devices))
     lower = row_ids((count, count)) >= lane_ids((count, count))
     running = jnp.dot(
-        lower.astype(jnp.bfloat16), onehot.astype(jnp.bfloat16), preferred_element_type=jnp.float32
+        lower.astype(jnp.float32).astype(jnp.bfloat16),
+        onehot.astype(jnp.float32).astype(jnp.bfloat16),
+        preferred_element_type=jnp.float32,
     )
     chosen = onehot.astype(jnp.float32)
     rank = jnp.sum(running * chosen, axis=1, keepdims=True).astype(jnp.int32) - 1
@@ -100,11 +113,22 @@
     kind = lane // 4
     value = jnp.where(
         kind == 0,
-        weight[:, 0:1],
-        jnp.where(kind == 1, weight[:, 1:2], jnp.where(kind == 2, cell[...].astype(jnp.float32), 0.0)),
+        columns[:, 2:3],
+        jnp.where(kind == 1, columns[:, 3:4], jnp.where(kind == 2, columns[:, 1:2], 0.0)),
     )
     value = jnp.where(lane % 4 == rank, value, 0.0)
-    out[...] = jnp.dot(chosen.T, value, precision=highest, preferred_element_type=jnp.float32)
+    chosen = (row_ids((devices, count)) == dest[...]).astype(jnp.float32).astype(jnp.bfloat16)
+    out[...] = select_sum(chosen, value)
+
+
+def select_sum(chosen, value):
+    total = None
+    for _ in range(3):
+        piece = value.astype(jnp.bfloat16)
+        value = value - piece.astype(jnp.float32)
+        part = jnp.dot(chosen, piece, preferred_element_type=jnp.float32)
+        total = part if total is None else total + part
+    return total
 
 
 def fold(row, stride):
@@ -197,7 +221,7 @@
             wrap_rows(field, (c, k), count, tiles)
         return carry
 
-    lax.fori_loop(0, field.shape[1], body, 0)
+    lax.fori_loop(0, field.shape[1], body, 0, unroll=4)
 
 
 def own_cells(vectors, tiles, offset, count, tile_y, i, t):
@@ -258,7 +282,7 @@
             reaction[i, t] = expand(fields, F_REACT, i, t, 3, 0, vectors)
         return carry
 
-    lax.fori_loop(0, count, arrange, 0)
+    lax.fori_loop(0, count, arrange, 0, unroll=3)
     last = krylov(v0, v1, v2, reaction, vectors, count, tile_y)
     sums = [jnp.zeros((8, LANES), jnp.float32) for _ in range(5)]
     for i in range(count):
@@ -375,33 +399,30 @@
 
 def sweep(source, target, wide, stride, bed_source=None, top_col=None, top_source=None):
     layer_count, count, tiles = target.shape[1], target.shape[2] - 2, target.shape[3] - 2
-    across = [(t, c) for t in range(tiles) for c in range(2)]
-
     def body(i, carry):
-        carried = []
-        for k in range(layer_count):
-            now = {}
-            for t, c in across:
-                value = lateral_sum(source, (c, k), i, t)
-                if k > 0:
-                    value = value + get_field(wide, F_RATIO + k - 1, i, t) * carried[k - 1][t, c]
-                elif bed_source is not None:
-                    value = value + bed_source[c, i, t]
-                now[t, c] = value
-            carried.append(now)
-        solved = {}
-        for k in range(layer_count - 1, -1, -1):
-            for t, c in across:
-                value = get_field(wide, F_PIVOT + k, i, t) * carried[k][t, c]
-                if k + 1 < layer_count:
-                    value = value + get_field(wide, F_RATIO + k, i, t) * solved[t, c]
-                solved[t, c] = value
-                if top_source is not None:
-                    value = value + top_col[k, i, t] * top_source[c, i, t]
-                put_tile(target, (c, k, i + 1), t, tiles, stride, value)
+        for t in range(tiles):
+            carried = [[], []]
+            for k in range(layer_count):
+                for c in range(2):
+                    value = lateral_sum(source, (c, k), i, t)
+                    if k > 0:
+                        value = value + get_field(wide, F_RATIO + k - 1, i, t) * carried[c][k - 1]
+                    elif bed_source is not None:
+                        value = value + bed_source[c, i, t]
+                    carried[c].append(value)
+            solved = [None, None]
+            for k in range(layer_count - 1, -1, -1):
+                for c in range(2):
+                    value = get_field(wide, F_PIVOT + k, i, t) * carried[c][k]
+                    if k + 1 < layer_count:
+                        value = value + get_field(wide, F_RATIO + k, i, t) * solved[c]
+                    solved[c] = value
+                    if top_source is not None:
+                        value = value + top_col[k, i, t] * top_source[c, i, t]
+                    put_tile(target, (c, k, i + 1), t, tiles, stride, value)
         return carry
 
-    lax.fori_loop(0, count, body, 0)
+    lax.fori_loop(0, count, body, 0, unroll=6)
     wrap_layers(target, tiles)
 
 
@@ -434,7 +455,7 @@
 
     expand_all(fields, wide, vectors, offset)
 
-    lax.fori_loop(0, count, prepare, 0)
+    lax.fori_loop(0, count, prepare, 0, unroll=6)
     wrap_layers(one, tiles)
     sweep(one, two, wide, vectors, bed_source=source)
     sweep(two, one, wide, vectors, bed_source=source)
@@ -449,21 +470,25 @@
             surface[c, i] = to_own([values[c, t] for t in range(tiles)], vectors, offset)
         return carry
 
-    lax.fori_loop(0, count, finish, 0)
-
-    lane = lane_ids((LANES, LANES))
+    lax.fori_loop(0, count, finish, 0, unroll=6)
+
+    table = message[...]
+    flipped = table.T
+    lane = lane_ids((LANES, 2 * LANES))
+    second = lane >= LANES
+    at_row, at_lane = [], []
+    for r in range(4):
+        cell = flipped[8 + r : 9 + r, :].astype(jnp.int32)
+        at_row.append((row_ids((tile_y, LANES)) == cell % tile_y).astype(jnp.float32))
+        cell = table[:, 8 + r : 9 + r].astype(jnp.int32)
+        weight = jnp.where(second, table[:, 4 + r : 5 + r], table[:, r : r + 1])
+        at_lane.append(jnp.where(cell // tile_y == lane % LANES // vectors, weight, 0.0))
+    weights = select_sum(
+        jnp.concatenate(at_row, axis=1).astype(jnp.bfloat16), jnp.concatenate(at_lane, axis=0)
+    )
     for c in range(2):
-        total = jnp.zeros((LANES, LANES), jnp.float32)
-        for r in range(4):
-            cell = message[:, 8 + r : 9 + r].astype(jnp.int32)
-            weight = message[:, 4 * c + r : 4 * c + r + 1]
-            at_row = (cell % tile_y == lane).astype(jnp.float32)
-            at_lane = jnp.where(cell // tile_y == lane // vectors, weight, 0.0)
-            total = total + jnp.dot(
-                at_row.T, at_lane, precision=highest, preferred_element_type=jnp.float32
-            )
         join_rows(surface.at[c], flat)
-        misfit[c] = total * flat[HALO : HALO + tile_y, :]
+        misfit[c] = weights[:, c * LANES : (c + 1) * LANES] * flat[HALO : HALO + tile_y, :]
     low[...] = misfit[:, 0:HALO, :]
     high[...] = misfit[:, tile_y - HALO :, :]
 
@@ -499,7 +524,7 @@
 
     expand_all(fields, wide, vectors, 0)
 
-    lax.fori_loop(0, count, prepare, 0)
+    lax.fori_loop(0, count, prepare, 0, unroll=6)
     wrap_layers(one, tiles)
     sweep(one, two, wide, vectors, top_col=top_col, top_source=source)
     sweep(two, one, wide, vectors, top_col=top_col, top_source=source)
@@ -516,7 +541,7 @@
             put_tile(v0, (i + 1,), t, tiles, vectors, value)
         return carry
 
-    lax.fori_loop(0, count, finish, 0)
+    lax.fori_loop(0, count, finish, 0, unroll=6)
     last = krylov(v0, v1, v2, reaction, vectors, count, tile_y)
     own = []
     for n, field in enumerate((v0, v1, v2, basis.at[0])):
@@ -555,12 +580,6 @@
     both = jnp.concatenate(halves, axis=1)
     for i in range(out.shape[0]):
         out[i] = both
-
-
-def partial_kernel(received, out):
-    total = jnp.sum(received[...], axis=0)
-    for i in range(out.shape[0]):
-        out[i] = total
 
 
 def finish_kernel(cells, received, stacked, beta_ref, next_out, alpha_out, beta_out):
@@ -670,7 +689,7 @@
     )
     table = pl.pallas_call(
         table_kernel, out_shape=shape(devices, LANES), compiler_params=params(), name="table"
-    )(obs_dest, obs_cell.reshape(obs_rows, 1), obs_weight)
+    )(obs_dest.reshape(1, obs_rows), obs_cell.reshape(1, obs_rows), obs_weight.T)
 
     from_low = lax.ppermute(high, "my", forward_y)
     from_high = lax.ppermute(low, "my", backward_y)
@@ -733,12 +752,7 @@
     )(flags, fields, misfit, misfit_left, misfit_right, basis, previous)
 
     products = lax.all_to_all(products, "mx", split_axis=0, concat_axis=0, tiled=True)
-    products = pl.pallas_call(
-        partial_kernel,
-        out_shape=shape(size_y, vectors, 2 * LANES),
-        compiler_params=params(),
-        name="partial",
-    )(products)
+    products = jnp.broadcast_to(jnp.sum(products, axis=0)[None], (size_y, vectors, 2 * LANES))
     products = lax.all_to_all(products, "my", split_axis=0, concat_axis=0, tiled=True)
     return pl.pallas_call(
         functools.partial(finish_kernel, float(cells)),

time: 134 us -> 119 us (0.89)
  Pallas kernels: 56.8 us -> 45 us
  waiting for transfers between devices: 9.53 us -> 13.5 us
  local copies, waits for them, and re-layouts: 5.34 us -> 1.42 us
  blocking collectives: 44.9 us -> 42 us
    pallas_call x1, Pallas kernels: 19.1 us -> 12.8 us  [shards(): pl.pallas_call(functools.partial(velocity_kernel, vectors), out_shape=(sh...]
    pallas_call x1, Pallas kernels: 21.3 us -> 17.7 us  [shards(): pl.pallas_call(functools.partial(adjoint_kernel, vectors), out_shape=(sha...]
    unnamed x20 -> x12, local copies, waits for them, and re-layouts: 4.53 us -> 1.4 us
    ppermute x1, waiting for transfers between devices: 0.54 us -> 3.11 us  [shards(): left = lax.ppermute(own, 'mx', forward_x)]
    all_to_all x1, blocking collectives: 19.4 us -> 17.4 us  [shards(): lax.all_to_all(message, AXES, split_axis=0, concat_axis=0, tiled=True)]
    pallas_call x1 -> x0, Pallas kernels: 1.64 us -> none  [shards(): pl.pallas_call(partial_kernel, out_shape=shape(size_y, vectors, 2 * LANES...]
    ppermute x1, waiting for transfers between devices: 0.01 us -> 1.36 us  [shards(): right = lax.ppermute(own, 'mx', backward_x)]
  transfers between devices with their start and end apart: 8 -> 8, of which waited for: 5 -> 6; matrix products, arithmetic and copies ran while one was open for 2% -> 1% of each run, Pallas kernels for 2% -> 2%
where the time goes in v3:
time: 119 us
  Pallas kernels  45 us (38%)
  blocking collectives  42 us (35%)
  starting transfers between devices  13.8 us (12%)
  waiting for transfers between devices  13.5 us (11%)
  other arithmetic  2.58 us (2%)
  local copies, waits for them, and re-layouts  1.42 us (1%)
    pallas_call x1, Pallas kernels, shards(): pl.pallas_call(functools.partial(adjoint_kernel, vectors), out_shape=(sha...  17.7 us
    all_to_all x1, blocking collectives, shards(): lax.all_to_all(message, AXES, split_axis=0, concat_axis=0, tiled=True)  17.4 us
    all_to_all x1, blocking collectives, shards(): lax.all_to_all(products, 'my', split_axis=0, concat_axis=0, tiled=True)  15.1 us
    pallas_call x1, Pallas kernels, shards(): pl.pallas_call(functools.partial(velocity_kernel, vectors), out_shape=(sh...  12.8 us
    all_to_all x1, blocking collectives, shards(): lax.all_to_all(products, 'mx', split_axis=0, concat_axis=0, tiled=True)  9.41 us
    ppermute x2, starting transfers between devices, shards(): from_high = lax.ppermute(low, 'my', backward_y)  9.35 us
    pallas_call x1, Pallas kernels, shards(): pl.pallas_call(functools.partial(moment_kernel, vectors), out_shape=(shap...  5.75 us
    pallas_call x1, Pallas kernels, shards(): pl.pallas_call(functools.partial(finish_kernel, float(cells)), out_shape=...  4.57 us
  transfers between devices with their start and end apart: 8, of which 6 were waited for; matrix products, arithmetic and copies ran while one was open for 1% of the time, Pallas kernels for 2%

profile of v3, /device:TPU:0, one launch (start us, length us, event | category | flops | bytes accessed | tf_op | source)
XLA Modules:
  0.0 118.9 jit_solution(3745054813178947442)
XLA Ops:
  0.6 2.0 %pack.1 = (f32[4,128,128]{2,1,0:T(8,128)}, f32[128,128]{1,0:T(8,128)}, f32[4,8,128]{2,1,0:T(8,128)}, f32[4,8,128]{2,1,0:T(8,128)}) custom-call(f32[16,8,128]{2,1,0:T(8,128)} %block.1, f32[16,8,128]{2,1,0:T(8,128)} %previous.1, f32[8,128]{1,0:T(8,128)} %reaction.1, f32[15,8,128]{2,1,0:T(8,128)} %vert.1, f32[16,8,128]{2,1,0:T(8,128)} %horiz.1, ...), custom_call_target="tpu_custom_call" | custom-call | tf_op jit(solution)/shard_map/pack/pallas_call | solution.py:678
  2.6 2.0 %collective-permute-start = (f32[4,8,128]{2,1,0:T(8,128)}, f32[4,8,128]{2,1,0:T(8,128)S(1)}, u32[]{:S(2)}, u32[]{:S(2)}) collective-permute-start(f32[4,8,128]{2,1,0:T(8,128)} %get-tuple-element.15), channel_id=1, source_target_pairs={{0,1},{1,2},{2,3},{3,4},{4,5},{5,6},{6,7},{7,8},{8,9},{9,10},{10,1... | collective-permute-start | bytes 49160 | tf_op jit(solution)/shard_map/ppermute | solution.py:694
  4.6 4.6 %collective-permute-start.1 = (f32[4,8,128]{2,1,0:T(8,128)}, f32[4,8,128]{2,1,0:T(8,128)S(1)}, u32[]{:S(2)}, u32[]{:S(2)}) collective-permute-start(f32[4,8,128]{2,1,0:T(8,128)} %get-tuple-element.17), channel_id=1, source_target_pairs={{0,15},{1,0},{2,1},{3,2},{4,3},{5,4},{6,5},{7,6},{8,7},{9,8},{10,9... | collective-permute-start | bytes 49160 | tf_op jit(solution)/shard_map/ppermute | solution.py:695
  9.2 1.9 %collective-permute-done = f32[4,8,128]{2,1,0:T(8,128)S(1)} collective-permute-done((f32[4,8,128]{2,1,0:T(8,128)}, f32[4,8,128]{2,1,0:T(8,128)S(1)}, u32[]{:S(2)}, u32[]{:S(2)}) %collective-permute-start) | collective-permute-done | bytes 16416 | tf_op jit(solution)/shard_map/ppermute | solution.py:694
  11.1 0.0 collective-permute-done.1
  11.1 1.0 pad_maximum_fusion.own
  12.1 0.0 copy-start
  12.1 1.3 %collective-permute-start.3 = (f32[4,144,128]{2,1,0:T(8,128)S(1)}, f32[4,144,128]{2,1,0:T(8,128)S(1)}, u32[]{:S(2)}, u32[]{:S(2)}) collective-permute-start(f32[4,144,128]{2,1,0:T(8,128)S(1)} %pad_maximum_fusion.own), channel_id=1, source_target_pairs={{0,112},{16,0},{32,16},{48,32},{64,48},{80,64},{96,80},{112,96},{1... | collective-permute-start | bytes 884744 | tf_op jit(solution)/shard_map/ppermute | solution.py:698
  13.4 0.0 collective-permute-start.2
  13.4 2.2 %table.1 = f32[128,128]{1,0:T(8,128)} custom-call(s32[1,256]{1,0:T(1,128)} %bitcast.12, s32[1,256]{1,0:T(1,128)} %bitcast.13, f32[2,256]{1,0:T(2,128)} %bitcast.11), custom_call_target="tpu_custom_call" | custom-call | tf_op jit(solution)/shard_map/table/pallas_call | solution.py:690
  15.6 0.7 add_convert_fusion.flags
  16.3 1.4 %collective-permute-done.3.right = f32[4,144,128]{2,1,0:T(8,128)S(1)} collective-permute-done((f32[4,144,128]{2,1,0:T(8,128)S(1)}, f32[4,144,128]{2,1,0:T(8,128)S(1)}, u32[]{:S(2)}, u32[]{:S(2)}) %collective-permute-start.3) | collective-permute-done | bytes 294944 | tf_op jit(solution)/shard_map/ppermute | solution.py:698
  17.7 3.1 %collective-permute-done.2.left = f32[4,144,128]{2,1,0:T(8,128)S(1)} collective-permute-done((f32[4,144,128]{2,1,0:T(8,128)S(1)}, f32[4,144,128]{2,1,0:T(8,128)S(1)}, u32[]{:S(2)}, u32[]{:S(2)}) %collective-permute-start.2) | collective-permute-done | bytes 294944 | tf_op jit(solution)/shard_map/ppermute | solution.py:697
  20.8 0.0 copy-done.2
  20.8 0.7 copy-done.3
  21.5 5.7 %moments.1 = (f32[128,128]{1,0:T(8,128)}, f32[3,18,3,8,128]{4,3,2,1,0:T(8,128)}, f32[10,18,8,128]{3,2,1,0:T(8,128)}) custom-call(f32[2]{0:T(128)} %add_convert_fusion.flags, f32[4,144,128]{2,1,0:T(8,128)} %copy-done, f32[4,144,128]{2,1,0:T(8,128)} %copy-done.3, f32[4,144,128]{2,1,0:T(8,128)} %copy-done.2, f32[128,128]{1,0:T(8,128)} %table.1), custom_call_target="tpu_custom_call" | custom-call | tf_op jit(solution)/shard_map/moments/pallas_call | solution.py:706
  27.3 17.4 %all_to_all.21 = f32[128,1,128]{2,1,0:T(1,128)} all-to-all(f32[128,1,128]{2,1,0:T(1,128)} %bitcast.10), channel_id=1, replica_groups=mesh['mx'=8,'my'=16] {'mx','my'}, dimensions={0} | all-to-all | bytes 131072 | tf_op jit(solution)/shard_map/all_to_all | solution.py:716
  44.7 12.8 %velocity.3 = (f32[2,128,128]{2,1,0:T(8,128)}, f32[2,8,128]{2,1,0:T(8,128)}, f32[2,8,128]{2,1,0:T(8,128)}) custom-call(f32[2]{0:T(128)} %add_convert_fusion.flags, f32[128,128]{1,0:T(8,128)} %bitcast.9, f32[3,18,3,8,128]{4,3,2,1,0:T(8,128)} %get-tuple-element.20.basis, f32[10,18,8,128]{3,2,1,0:T(8,128)} %get-tuple-element.18.fields), custom_call_target="tpu_custom_call" | custom-call | tf_op jit(solution)/shard_map/velocity/pallas_call | solution.py:727
  57.5 0.6 collective-permute-start.4
  58.1 4.7 %collective-permute-start.5 = (f32[2,8,128]{2,1,0:T(8,128)}, f32[2,8,128]{2,1,0:T(8,128)S(1)}, u32[]{:S(2)}, u32[]{:S(2)}) collective-permute-start(f32[2,8,128]{2,1,0:T(8,128)} %get-tuple-element.23), channel_id=1, source_target_pairs={{0,15},{1,0},{2,1},{3,2},{4,3},{5,4},{6,5},{7,6},{8,7},{9,8},{10,9... | collective-permute-start | bytes 24584 | tf_op jit(solution)/shard_map/ppermute | solution.py:737
  62.9 1.8 %collective-permute-done.4 = f32[2,8,128]{2,1,0:T(8,128)S(1)} collective-permute-done((f32[2,8,128]{2,1,0:T(8,128)}, f32[2,8,128]{2,1,0:T(8,128)S(1)}, u32[]{:S(2)}, u32[]{:S(2)}) %collective-permute-start.4) | collective-permute-done | bytes 8224 | tf_op jit(solution)/shard_map/ppermute | solution.py:736
  64.7 0.0 collective-permute-done.5
  64.7 0.9 pad_maximum_fusion.1.misfit
  65.6 0.0 collective-permute-start.7
  65.7 0.5 collective-permute-start.6
  66.2 2.2 %collective-permute-done.7.misfit_right = f32[2,144,128]{2,1,0:T(8,128)S(1)} collective-permute-done((f32[2,144,128]{2,1,0:T(8,128)S(1)}, f32[2,144,128]{2,1,0:T(8,128)S(1)}, u32[]{:S(2)}, u32[]{:S(2)}) %collective-permute-start.7) | collective-permute-done | bytes 147488 | tf_op jit(solution)/shard_map/ppermute | solution.py:740
  68.3 3.1 %collective-permute-done.6.misfit_left = f32[2,144,128]{2,1,0:T(8,128)S(1)} collective-permute-done((f32[2,144,128]{2,1,0:T(8,128)S(1)}, f32[2,144,128]{2,1,0:T(8,128)S(1)}, u32[]{:S(2)}, u32[]{:S(2)}) %collective-permute-start.6) | collective-permute-done | bytes 147488 | tf_op jit(solution)/shard_map/ppermute | solution.py:739
  71.5 0.7 copy-done.5
  72.1 17.7 %adjoint.1 = (f32[8,16,256]{2,1,0:T(8,128)}, f32[8,80,128]{2,1,0:T(8,128)}) custom-call(f32[2]{0:T(128)} %add_convert_fusion.flags, f32[10,18,8,128]{3,2,1,0:T(8,128)} %get-tuple-element.18.fields, f32[2,144,128]{2,1,0:T(8,128)} %copy-done.1, f32[2,144,128]{2,1,0:T(8,128)} %copy-done.5, f32[2,144,128]{2,1,0:T(8,128)} %copy-done.4, ...), custom_call_target="tpu_custom_call" | custom-call | tf_op jit(solution)/shard_map/adjoint/pallas_call | solution.py:742
  89.8 9.4 %all_to_all.22 = f32[8,16,256]{2,1,0:T(8,128)S(1)} all-to-all(f32[8,16,256]{2,1,0:T(8,128)} %get-tuple-element.25), channel_id=1, replica_groups=mesh['mx'=8,'my'=16] {'mx'}, dimensions={0} | all-to-all | bytes 262144 | tf_op jit(solution)/shard_map/all_to_all | solution.py:754
  99.2 15.1 %all_to_all.23.received = f32[16,16,256]{2,1,0:T(8,128)} all-to-all(f32[16,16,256]{2,1,0:T(8,128)S(1)} %broadcast_in_dim.2), channel_id=1, replica_groups=mesh['mx'=8,'my'=16] {'my'}, dimensions={0} | all-to-all | bytes 524288 | tf_op jit(solution)/shard_map/all_to_all | solution.py:756
  114.4 4.6 %finish.1 = (f32[16,8,128]{2,1,0:T(8,128)}, f32[16,16]{1,0:T(8,128)}, f32[16,16]{1,0:T(8,128)}) custom-call(f32[16,16,256]{2,1,0:T(8,128)} %all_to_all.23.received, f32[8,80,128]{2,1,0:T(8,128)} %get-tuple-element.26.stacked, f32[16,16]{1,0:T(8,128)} %beta_ref.1), custom_call_target="tpu_custom_call" | custom-call | tf_op jit(solution)/shard_map/finish/pallas_call | solution.py:757
  (14 shorter events, 0.1 us)
Async XLA Ops:
  2.6 8.5 %collective-permute-start = (f32[4,8,128]{2,1,0:T(8,128)}, f32[4,8,128]{2,1,0:T(8,128)S(1)}, u32[]{:S(2)}, u32[]{:S(2)}) collective-permute-start(f32[4,8,128]{2,1,0:T(8,128)} %get-tuple-element.15), channel_id=1, source_target_pairs={{0,1},{1,2},{2,3},{3,4},{4,5},{5,6},{6,7},{7,8},{8,9},{9,10},{10,1... | collective-permute-start | bytes 49160 | tf_op jit(solution)/shard_map/ppermute | solution.py:694
  4.6 6.5 %collective-permute-start.1 = (f32[4,8,128]{2,1,0:T(8,128)}, f32[4,8,128]{2,1,0:T(8,128)S(1)}, u32[]{:S(2)}, u32[]{:S(2)}) collective-permute-start(f32[4,8,128]{2,1,0:T(8,128)} %get-tuple-element.17), channel_id=1, source_target_pairs={{0,15},{1,0},{2,1},{3,2},{4,3},{5,4},{6,5},{7,6},{8,7},{9,8},{10,9... | collective-permute-start | bytes 49160 | tf_op jit(solution)/shard_map/ppermute | solution.py:695
  12.1 8.7 %copy-start = (f32[4,144,128]{2,1,0:T(8,128)}, f32[4,144,128]{2,1,0:T(8,128)S(1)}, u32[]{:S(2)}) copy-start(f32[4,144,128]{2,1,0:T(8,128)S(1)} %pad_maximum_fusion.own) | copy-start | bytes 884740
  12.1 5.6 %collective-permute-start.3 = (f32[4,144,128]{2,1,0:T(8,128)S(1)}, f32[4,144,128]{2,1,0:T(8,128)S(1)}, u32[]{:S(2)}, u32[]{:S(2)}) collective-permute-start(f32[4,144,128]{2,1,0:T(8,128)S(1)} %pad_maximum_fusion.own), channel_id=1, source_target_pairs={{0,112},{16,0},{32,16},{48,32},{64,48},{80,64},{96,80},{112,96},{1... | collective-permute-start | bytes 884744 | tf_op jit(solution)/shard_map/ppermute | solution.py:698
  13.4 7.4 %collective-permute-start.2 = (f32[4,144,128]{2,1,0:T(8,128)S(1)}, f32[4,144,128]{2,1,0:T(8,128)S(1)}, u32[]{:S(2)}, u32[]{:S(2)}) collective-permute-start(f32[4,144,128]{2,1,0:T(8,128)S(1)} %pad_maximum_fusion.own), channel_id=1, source_target_pairs={{0,16},{16,32},{32,48},{48,64},{64,80},{80,96},{96,112},{112,0},{1... | collective-permute-start | bytes 884744 | tf_op jit(solution)/shard_map/ppermute | solution.py:697
  17.7 3.1 %copy-start.2 = (f32[4,144,128]{2,1,0:T(8,128)}, f32[4,144,128]{2,1,0:T(8,128)S(1)}, u32[]{:S(2)}) copy-start(f32[4,144,128]{2,1,0:T(8,128)S(1)} %collective-permute-done.3.right) | copy-start | bytes 884740
  20.8 0.7 copy-start.3
  57.5 7.2 %collective-permute-start.4 = (f32[2,8,128]{2,1,0:T(8,128)}, f32[2,8,128]{2,1,0:T(8,128)S(1)}, u32[]{:S(2)}, u32[]{:S(2)}) collective-permute-start(f32[2,8,128]{2,1,0:T(8,128)} %get-tuple-element.21), channel_id=1, source_target_pairs={{0,1},{1,2},{2,3},{3,4},{4,5},{5,6},{6,7},{7,8},{8,9},{9,10},{10,1... | collective-permute-start | bytes 24584 | tf_op jit(solution)/shard_map/ppermute | solution.py:736
  58.1 6.6 %collective-permute-start.5 = (f32[2,8,128]{2,1,0:T(8,128)}, f32[2,8,128]{2,1,0:T(8,128)S(1)}, u32[]{:S(2)}, u32[]{:S(2)}) collective-permute-start(f32[2,8,128]{2,1,0:T(8,128)} %get-tuple-element.23), channel_id=1, source_target_pairs={{0,15},{1,0},{2,1},{3,2},{4,3},{5,4},{6,5},{7,6},{8,7},{9,8},{10,9... | collective-permute-start | bytes 24584 | tf_op jit(solution)/shard_map/ppermute | solution.py:737
  65.6 5.8 %copy-start.1 = (f32[2,144,128]{2,1,0:T(8,128)}, f32[2,144,128]{2,1,0:T(8,128)S(1)}, u32[]{:S(2)}) copy-start(f32[2,144,128]{2,1,0:T(8,128)S(1)} %pad_maximum_fusion.1.misfit) | copy-start | bytes 442372
  65.6 2.7 %collective-permute-start.7 = (f32[2,144,128]{2,1,0:T(8,128)S(1)}, f32[2,144,128]{2,1,0:T(8,128)S(1)}, u32[]{:S(2)}, u32[]{:S(2)}) collective-permute-start(f32[2,144,128]{2,1,0:T(8,128)S(1)} %pad_maximum_fusion.1.misfit), channel_id=1, source_target_pairs={{0,112},{16,0},{32,16},{48,32},{64,48},{80,64},{96,80},{112,96},{1... | collective-permute-start | bytes 442376 | tf_op jit(solution)/shard_map/ppermute | solution.py:740
  65.7 5.8 %collective-permute-start.6 = (f32[2,144,128]{2,1,0:T(8,128)S(1)}, f32[2,144,128]{2,1,0:T(8,128)S(1)}, u32[]{:S(2)}, u32[]{:S(2)}) collective-permute-start(f32[2,144,128]{2,1,0:T(8,128)S(1)} %pad_maximum_fusion.1.misfit), channel_id=1, source_target_pairs={{0,16},{16,32},{32,48},{48,64},{64,80},{80,96},{96,112},{112,0},{1... | collective-permute-start | bytes 442376 | tf_op jit(solution)/shard_map/ppermute | solution.py:739
  68.3 3.1 %copy-start.4 = (f32[2,144,128]{2,1,0:T(8,128)}, f32[2,144,128]{2,1,0:T(8,128)S(1)}, u32[]{:S(2)}) copy-start(f32[2,144,128]{2,1,0:T(8,128)S(1)} %collective-permute-done.7.misfit_right) | copy-start | bytes 442372
  71.5 0.7 copy-start.5

commit v4 on v3

--- a/solution.py
+++ b/solution.py
@@ -121,6 +121,20 @@
     out[...] = select_sum(chosen, value)
 
 
+def pieces(value, axis):
+    parts = []
+    for _ in range(3):
+        piece = value.astype(jnp.bfloat16)
+        value = value - piece.astype(jnp.float32)
+        parts.append(piece)
+    return jnp.concatenate(parts, axis=axis)
+
+
+def thrice(chosen):
+    chosen = chosen.astype(jnp.float32).astype(jnp.bfloat16)
+    return jnp.concatenate([chosen] * 3, axis=0)
+
+
 def select_sum(chosen, value):
     total = None
     for _ in range(3):
@@ -154,14 +168,12 @@
     return offset + (lane_ids((8, LANES)) // vectors) * tiles + tile
 
 
-def to_blocked(parts, vectors, tiles, offset):
-    tile_x = LANES // vectors
-    out = []
-    for t in range(tiles):
-        row = tile_rows(vectors, tiles, offset, t)
-        index = (row % tile_x) * vectors + lane_ids((8, LANES)) % vectors
-        out.append(pick(row // tile_x, [gather(part, index) for part in parts]))
-    return out
+def to_blocked(value, vectors, tiles):
+    shape = (3 * LANES, tiles * LANES)
+    column, source = lane_ids(shape), row_ids(shape)
+    row = (column % LANES // vectors) * tiles + column // LANES
+    chosen = source == row * vectors + column % vectors
+    return jnp.dot(pieces(value, 1), thrice(chosen), preferred_element_type=jnp.float32)
 
 
 def reblock(values, vectors, tiles, offset):
@@ -258,31 +270,40 @@
 
 
 def moment_kernel(
-    vectors, flags, own, left, right, table, out, basis, fields, parts, reaction, v0, v1, v2
+    vectors, flags, own, left, right, table, out, basis, fields, flat, parts, reaction, v0, v1, v2
 ):
     tile_x = LANES // vectors
     rows = own.shape[1]
     count = rows // 8
     tile_y = rows - 2 * HALO
-    for p, (ref, flag) in enumerate(((left, flags[0]), (own, None), (right, flags[1]))):
-        for t in range(own.shape[0]):
-            split_rows(ref.at[t], parts.at[p, t], flag)
-    lane = lane_ids((8, LANES))
-
-    def arrange(i, carry):
-        for t, value in enumerate(to_blocked([parts[p, 0, i] for p in range(3)], vectors, 3, 0)):
-            put_tile(v0, (i + 1,), t, 3, vectors, value)
-        for q in range(fields.shape[0]):
-            per_tile = LANES // (4 * tile_x)
-            index = (q % per_tile) * 4 * tile_x + (lane // 32) * tile_x + lane % tile_x
-            fields[q, i] = pick(
-                (lane % 32) // tile_x, [gather(parts[p, 1 + q // per_tile, i], index) for p in range(3)]
-            )
+    def beside(tiles):
+        value = jnp.concatenate([left[tiles] * flags[0], own[tiles], right[tiles] * flags[1]], axis=-1)
+        return value.reshape(-1, 3 * LANES)
+
+    blocked = to_blocked(beside(0), vectors, 3)
+    for t in range(3):
+        flat[t] = blocked[:, t * LANES : (t + 1) * LANES]
+    per_tile = LANES // (4 * tile_x)
+    shape = (3 * LANES, per_tile * LANES)
+    column, at = lane_ids(shape), row_ids(shape)
+    lane = column % 32
+    field = column // LANES * 4 + column % LANES // 32
+    chosen = (at == lane // tile_x * LANES + field * tile_x + lane % tile_x) & (lane < 3 * tile_x)
+    value = beside(slice(1, own.shape[0]))
+    out_all = jnp.dot(pieces(value, 1), thrice(chosen), preferred_element_type=jnp.float32)
+    for q in range(fields.shape[0]):
+        first = q // per_tile * rows
+        lanes = q % per_tile * LANES
+        flat[3 + q] = out_all[first : first + rows, lanes : lanes + LANES]
+    for t in range(3):
+        split_rows(flat.at[t], parts.at[t])
+    for q in range(fields.shape[0]):
+        split_rows(flat.at[3 + q], fields.at[q])
+
+    for i in range(count):
         for t in range(3):
+            put_tile(v0, (i + 1,), t, 3, vectors, parts[t, i])
             reaction[i, t] = expand(fields, F_REACT, i, t, 3, 0, vectors)
-        return carry
-
-    lax.fori_loop(0, count, arrange, 0, unroll=3)
     last = krylov(v0, v1, v2, reaction, vectors, count, tile_y)
     sums = [jnp.zeros((8, LANES), jnp.float32) for _ in range(5)]
     for i in range(count):
@@ -333,26 +354,22 @@
 
 def expand_all(fields, wide, vectors, offset):
     groups, count = fields.shape[:2]
-    value = fields[...].reshape(groups * count * 8, LANES)
-    high = value.astype(jnp.bfloat16)
-    value = value - high.astype(jnp.float32)
-    middle = value.astype(jnp.bfloat16)
-    low = (value - middle.astype(jnp.float32)).astype(jnp.bfloat16)
-    both = jnp.concatenate([high, middle], axis=1)
-    lanes = wide.shape[-1]
-    shape = (2 * LANES, lanes)
+    value = pieces(fields[...].reshape(groups * count * 8, LANES), 1)
+    half = wide.shape[-1] // 2
+    tiles = half // (2 * LANES)
+    shape = (LANES, half)
     column = lane_ids(shape)
-    row = offset + (column % LANES // vectors) * (lanes // LANES) + column // LANES
-    source = row_ids(shape) % LANES
-    for j in range(4):
-        chosen = (source == j * 32 + row).astype(jnp.float32).astype(jnp.bfloat16)
-        out = jnp.dot(both, chosen, preferred_element_type=jnp.float32)
-        out = out + jnp.dot(low, chosen[:LANES], preferred_element_type=jnp.float32)
-        wide[j] = out.reshape(groups, count, 8, lanes)
+    tile = column // LANES
+    row = offset + (column % LANES // vectors) * tiles + tile % tiles
+    for j in range(2):
+        chosen = row_ids(shape) == (2 * j + tile // tiles) * 32 + row
+        out = jnp.dot(value, thrice(chosen), preferred_element_type=jnp.float32)
+        wide[:, :, :, j * half : (j + 1) * half] = out.reshape(groups, count, 8, half)
 
 
 def get_field(wide, field, i, t):
-    return wide[field % 4, field // 4, i, :, t * LANES : (t + 1) * LANES]
+    at = (field % 4) * (wide.shape[-1] // (4 * LANES)) + t
+    return wide[field // 4, i, :, at * LANES : (at + 1) * LANES]
 
 
 def prepare_row(wide, i, bed_col, top_col, layer_count, tiles):
@@ -496,18 +513,22 @@
 def adjoint_kernel(
     vectors, flags, fields, misfit, misfit_left, misfit_right, basis, previous,
     out, stacked,
-    wide, top_col, one, two, source, bed_col, sides, bed, reaction, v0, v1, v2, natural, flat,
+    wide, top_col, one, two, source, bed_col, sides, spread, bed, reaction, v0, v1, v2, natural, flat,
 ):
     tile_x = LANES // vectors
     layer_count, count, tiles = top_col.shape[:3]
     tile_y = count * 8 - 2 * HALO
+    value = jnp.concatenate(
+        [misfit_left[...] * flags[0], misfit[...], misfit_right[...] * flags[1]], axis=-1
+    )
+    value = to_blocked(value.reshape(-1, 3 * LANES), vectors, tiles)
     for c in range(2):
-        split_rows(misfit_left.at[c], sides.at[c, 0], flags[0])
-        split_rows(misfit.at[c], sides.at[c, 1])
-        split_rows(misfit_right.at[c], sides.at[c, 2], flags[1])
+        for t in range(tiles):
+            sides[c, t] = value[c * count * 8 : (c + 1) * count * 8, t * LANES : (t + 1) * LANES]
+            split_rows(sides.at[c, t], spread.at[c, t])
 
     def prepare(i, carry):
-        values = [to_blocked([sides[c, p, i] for p in range(3)], vectors, tiles, 0) for c in range(2)]
+        values = [[spread[c, t, i] for t in range(tiles)] for c in range(2)]
         inv_lat, _, tops = prepare_row(wide, i, bed_col, top_col, layer_count, tiles)
         for t in range(tiles):
             reaction[i, t] = get_field(wide, F_REACT, i, t)
@@ -623,12 +644,12 @@
         [gram, eye.astype(jnp.float32), jnp.zeros((vectors, LANES - 2 * vectors), jnp.float32)], axis=1
     )
     down_id = row_ids(work.shape)
-    for j in range(vectors):
+    for j in range(vectors - 1):
         row = work[j : j + 1, :]
-        scale = 1.0 / jnp.sqrt(row[:, j : j + 1])
-        row = row * scale
-        column = work[:, j : j + 1] * scale
-        work = jnp.where(down_id > j, work - column * row, jnp.where(down_id == j, row, work))
+        column = jnp.where(down_id > j, work[:, j : j + 1], 0.0)
+        work = work - column * (row * (1.0 / row[:, j : j + 1]))
+    pivot = jnp.sum(jnp.where(eye, work[:, 0:vectors], 0.0), axis=1, keepdims=True)
+    work = work * (1.0 / jnp.sqrt(pivot))
     beta_out[...] = jnp.where(row_ids(shape) <= lane_ids(shape), work[:, 0:vectors], 0.0)
     inverse = work[:, vectors : 2 * vectors]
     mix = jnp.concatenate(
@@ -709,7 +730,8 @@
             shape(devices, LANES), shape(3, count, 3, 8, LANES), shape(groups, count, 8, LANES)
         ),
         in_specs=[smem, vmem, vmem, vmem, vmem],
-        scratch_shapes=[blocked(3, tiles, count), blocked(count, 3)] + [blocked(count + 2, 5)] * 3,
+        scratch_shapes=[pltpu.VMEM((3 + groups, rows, LANES), f32), blocked(3, count), blocked(count, 3)]
+        + [blocked(count + 2, 5)] * 3,
         compiler_params=params(),
         name="moments",
     )(flags, own, left, right, table)
@@ -717,7 +739,7 @@
 
     def columns(width):
         return [
-            pltpu.VMEM((4, groups, count, 8, width * LANES), f32),
+            pltpu.VMEM((groups, count, 8, 4 * width * LANES), f32),
             blocked(layer_count, count, width),
             blocked(2, layer_count, count + 2, width + 2),
             blocked(2, layer_count, count + 2, width + 2),
@@ -744,7 +766,7 @@
         out_shape=(shape(size_x, vectors, 2 * LANES), shape(tile_x, 5 * vectors, tile_y)),
         in_specs=[smem] + [vmem] * 6,
         scratch_shapes=columns(3)
-        + [blocked(layer_count, count, 3), blocked(2, 3, count), blocked(2, count, 3), blocked(count, 3)]
+        + [blocked(layer_count, count, 3), pltpu.VMEM((2, 3, rows, LANES), f32), blocked(2, 3, count), blocked(2, count, 3), blocked(count, 3)]
         + [blocked(count + 2, 5)] * 3
         + [blocked(count), pltpu.VMEM((rows, LANES), f32)],
         compiler_params=params(),

time: 119 us -> 116 us (0.975)
  Pallas kernels: 45 us -> 42 us
    pallas_call x1, Pallas kernels: 5.75 us -> 3.53 us  [shards(): pl.pallas_call(functools.partial(moment_kernel, vectors), out_shape=(shap...]
where the time goes in v4:
time: 116 us
  Pallas kernels  42 us (36%)
  blocking collectives  42 us (36%)
  starting transfers between devices  13.8 us (12%)
  waiting for transfers between devices  13.5 us (12%)
  other arithmetic  2.58 us (2%)
  local copies, waits for them, and re-layouts  1.42 us (1%)
    all_to_all x1, blocking collectives, shards(): lax.all_to_all(message, AXES, split_axis=0, concat_axis=0, tiled=True)  17.4 us
    pallas_call x1, Pallas kernels, shards(): pl.pallas_call(functools.partial(adjoint_kernel, vectors), out_shape=(sha...  17.2 us
    all_to_all x1, blocking collectives, shards(): lax.all_to_all(products, 'my', split_axis=0, concat_axis=0, tiled=True)  15.1 us
    pallas_call x1, Pallas kernels, shards(): pl.pallas_call(functools.partial(velocity_kernel, vectors), out_shape=(sh...  12.7 us
    all_to_all x1, blocking collectives, shards(): lax.all_to_all(products, 'mx', split_axis=0, concat_axis=0, tiled=True)  9.41 us
    ppermute x2, starting transfers between devices, shards(): from_high = lax.ppermute(low, 'my', backward_y)  9.34 us
    pallas_call x1, Pallas kernels, shards(): pl.pallas_call(functools.partial(finish_kernel, float(cells)), out_shape=...  4.41 us
    ppermute x2, waiting for transfers between devices, shards(): from_low = lax.ppermute(high, 'my', forward_y)  3.69 us
  transfers between devices with their start and end apart: 8, of which 6 were waited for; matrix products, arithmetic and copies ran while one was open for 1% of the time, Pallas kernels for 2%

profile of v4, /device:TPU:0, one launch (start us, length us, event | category | flops | bytes accessed | tf_op | source)
XLA Modules:
  0.0 116.0 jit_solution(18154206590030043373)
XLA Ops:
  0.6 2.0 %pack.1 = (f32[4,128,128]{2,1,0:T(8,128)}, f32[128,128]{1,0:T(8,128)}, f32[4,8,128]{2,1,0:T(8,128)}, f32[4,8,128]{2,1,0:T(8,128)}) custom-call(f32[16,8,128]{2,1,0:T(8,128)} %block.1, f32[16,8,128]{2,1,0:T(8,128)} %previous.1, f32[8,128]{1,0:T(8,128)} %reaction.1, f32[15,8,128]{2,1,0:T(8,128)} %vert.1, f32[16,8,128]{2,1,0:T(8,128)} %horiz.1, ...), custom_call_target="tpu_custom_call" | custom-call | tf_op jit(solution)/shard_map/pack/pallas_call | solution.py:699
  2.6 2.0 %collective-permute-start = (f32[4,8,128]{2,1,0:T(8,128)}, f32[4,8,128]{2,1,0:T(8,128)S(1)}, u32[]{:S(2)}, u32[]{:S(2)}) collective-permute-start(f32[4,8,128]{2,1,0:T(8,128)} %get-tuple-element.15), channel_id=1, source_target_pairs={{0,1},{1,2},{2,3},{3,4},{4,5},{5,6},{6,7},{7,8},{8,9},{9,10},{10,1... | collective-permute-start | bytes 49160 | tf_op jit(solution)/shard_map/ppermute | solution.py:715
  4.6 4.6 %collective-permute-start.1 = (f32[4,8,128]{2,1,0:T(8,128)}, f32[4,8,128]{2,1,0:T(8,128)S(1)}, u32[]{:S(2)}, u32[]{:S(2)}) collective-permute-start(f32[4,8,128]{2,1,0:T(8,128)} %get-tuple-element.17), channel_id=1, source_target_pairs={{0,15},{1,0},{2,1},{3,2},{4,3},{5,4},{6,5},{7,6},{8,7},{9,8},{10,9... | collective-permute-start | bytes 49160 | tf_op jit(solution)/shard_map/ppermute | solution.py:716
  9.2 1.9 %collective-permute-done = f32[4,8,128]{2,1,0:T(8,128)S(1)} collective-permute-done((f32[4,8,128]{2,1,0:T(8,128)}, f32[4,8,128]{2,1,0:T(8,128)S(1)}, u32[]{:S(2)}, u32[]{:S(2)}) %collective-permute-start) | collective-permute-done | bytes 16416 | tf_op jit(solution)/shard_map/ppermute | solution.py:715
  11.1 0.0 collective-permute-done.1
  11.1 1.0 pad_maximum_fusion.own
  12.1 1.3 %collective-permute-start.3 = (f32[4,144,128]{2,1,0:T(8,128)S(1)}, f32[4,144,128]{2,1,0:T(8,128)S(1)}, u32[]{:S(2)}, u32[]{:S(2)}) collective-permute-start(f32[4,144,128]{2,1,0:T(8,128)S(1)} %pad_maximum_fusion.own), channel_id=1, source_target_pairs={{0,112},{16,0},{32,16},{48,32},{64,48},{80,64},{96,80},{112,96},{1... | collective-permute-start | bytes 884744 | tf_op jit(solution)/shard_map/ppermute | solution.py:719
  13.4 0.0 collective-permute-start.2
  13.4 2.2 %table.1 = f32[128,128]{1,0:T(8,128)} custom-call(s32[1,256]{1,0:T(1,128)} %bitcast.12, s32[1,256]{1,0:T(1,128)} %bitcast.13, f32[2,256]{1,0:T(2,128)} %bitcast.11), custom_call_target="tpu_custom_call" | custom-call | tf_op jit(solution)/shard_map/table/pallas_call | solution.py:711
  15.6 0.7 add_convert_fusion.flags
  16.3 1.4 %collective-permute-done.3.right = f32[4,144,128]{2,1,0:T(8,128)S(1)} collective-permute-done((f32[4,144,128]{2,1,0:T(8,128)S(1)}, f32[4,144,128]{2,1,0:T(8,128)S(1)}, u32[]{:S(2)}, u32[]{:S(2)}) %collective-permute-start.3) | collective-permute-done | bytes 294944 | tf_op jit(solution)/shard_map/ppermute | solution.py:719
  17.7 3.1 %collective-permute-done.2.left = f32[4,144,128]{2,1,0:T(8,128)S(1)} collective-permute-done((f32[4,144,128]{2,1,0:T(8,128)S(1)}, f32[4,144,128]{2,1,0:T(8,128)S(1)}, u32[]{:S(2)}, u32[]{:S(2)}) %collective-permute-start.2) | collective-permute-done | bytes 294944 | tf_op jit(solution)/shard_map/ppermute | solution.py:718
  20.8 0.0 copy-done.2
  20.8 0.7 copy-done.3
  21.5 3.5 %moments.1 = (f32[128,128]{1,0:T(8,128)}, f32[3,18,3,8,128]{4,3,2,1,0:T(8,128)}, f32[10,18,8,128]{3,2,1,0:T(8,128)}) custom-call(f32[2]{0:T(128)} %add_convert_fusion.flags, f32[4,144,128]{2,1,0:T(8,128)} %copy-done, f32[4,144,128]{2,1,0:T(8,128)} %copy-done.3, f32[4,144,128]{2,1,0:T(8,128)} %copy-done.2, f32[128,128]{1,0:T(8,128)} %table.1), custom_call_target="tpu_custom_call" | custom-call | tf_op jit(solution)/shard_map/moments/pallas_call | solution.py:727
  25.0 17.4 %all_to_all.21 = f32[128,1,128]{2,1,0:T(1,128)} all-to-all(f32[128,1,128]{2,1,0:T(1,128)} %bitcast.10), channel_id=1, replica_groups=mesh['mx'=8,'my'=16] {'mx','my'}, dimensions={0} | all-to-all | bytes 131072 | tf_op jit(solution)/shard_map/all_to_all | solution.py:738
  42.5 12.7 %velocity.3 = (f32[2,128,128]{2,1,0:T(8,128)}, f32[2,8,128]{2,1,0:T(8,128)}, f32[2,8,128]{2,1,0:T(8,128)}) custom-call(f32[2]{0:T(128)} %add_convert_fusion.flags, f32[128,128]{1,0:T(8,128)} %bitcast.9, f32[3,18,3,8,128]{4,3,2,1,0:T(8,128)} %get-tuple-element.20.basis, f32[10,18,8,128]{3,2,1,0:T(8,128)} %get-tuple-element.18.fields), custom_call_target="tpu_custom_call" | custom-call | tf_op jit(solution)/shard_map/velocity/pallas_call | solution.py:749
  55.2 0.6 collective-permute-start.4
  55.8 4.7 %collective-permute-start.5 = (f32[2,8,128]{2,1,0:T(8,128)}, f32[2,8,128]{2,1,0:T(8,128)S(1)}, u32[]{:S(2)}, u32[]{:S(2)}) collective-permute-start(f32[2,8,128]{2,1,0:T(8,128)} %get-tuple-element.23), channel_id=1, source_target_pairs={{0,15},{1,0},{2,1},{3,2},{4,3},{5,4},{6,5},{7,6},{8,7},{9,8},{10,9... | collective-permute-start | bytes 24584 | tf_op jit(solution)/shard_map/ppermute | solution.py:759
  60.5 1.8 %collective-permute-done.4 = f32[2,8,128]{2,1,0:T(8,128)S(1)} collective-permute-done((f32[2,8,128]{2,1,0:T(8,128)}, f32[2,8,128]{2,1,0:T(8,128)S(1)}, u32[]{:S(2)}, u32[]{:S(2)}) %collective-permute-start.4) | collective-permute-done | bytes 8224 | tf_op jit(solution)/shard_map/ppermute | solution.py:758
  62.4 0.0 collective-permute-done.5
  62.4 0.9 pad_maximum_fusion.1.misfit
  63.3 0.0 collective-permute-start.7
  63.3 0.5 collective-permute-start.6
  63.8 2.2 %collective-permute-done.7.misfit_right = f32[2,144,128]{2,1,0:T(8,128)S(1)} collective-permute-done((f32[2,144,128]{2,1,0:T(8,128)S(1)}, f32[2,144,128]{2,1,0:T(8,128)S(1)}, u32[]{:S(2)}, u32[]{:S(2)}) %collective-permute-start.7) | collective-permute-done | bytes 147488 | tf_op jit(solution)/shard_map/ppermute | solution.py:762
  66.0 3.1 %collective-permute-done.6.misfit_left = f32[2,144,128]{2,1,0:T(8,128)S(1)} collective-permute-done((f32[2,144,128]{2,1,0:T(8,128)S(1)}, f32[2,144,128]{2,1,0:T(8,128)S(1)}, u32[]{:S(2)}, u32[]{:S(2)}) %collective-permute-start.6) | collective-permute-done | bytes 147488 | tf_op jit(solution)/shard_map/ppermute | solution.py:761
  69.1 0.0 copy-done.1
  69.1 0.7 copy-done.5
  69.8 17.2 %adjoint.1 = (f32[8,16,256]{2,1,0:T(8,128)}, f32[8,80,128]{2,1,0:T(8,128)}) custom-call(f32[2]{0:T(128)} %add_convert_fusion.flags, f32[10,18,8,128]{3,2,1,0:T(8,128)} %get-tuple-element.18.fields, f32[2,144,128]{2,1,0:T(8,128)} %copy-done.1, f32[2,144,128]{2,1,0:T(8,128)} %copy-done.5, f32[2,144,128]{2,1,0:T(8,128)} %copy-done.4, ...), custom_call_target="tpu_custom_call" | custom-call | tf_op jit(solution)/shard_map/adjoint/pallas_call | solution.py:764
  87.0 9.4 %all_to_all.22 = f32[8,16,256]{2,1,0:T(8,128)S(1)} all-to-all(f32[8,16,256]{2,1,0:T(8,128)} %get-tuple-element.25), channel_id=1, replica_groups=mesh['mx'=8,'my'=16] {'mx'}, dimensions={0} | all-to-all | bytes 262144 | tf_op jit(solution)/shard_map/all_to_all | solution.py:776
  96.4 15.1 %all_to_all.23.received = f32[16,16,256]{2,1,0:T(8,128)} all-to-all(f32[16,16,256]{2,1,0:T(8,128)S(1)} %broadcast_in_dim.2), channel_id=1, replica_groups=mesh['mx'=8,'my'=16] {'my'}, dimensions={0} | all-to-all | bytes 524288 | tf_op jit(solution)/shard_map/all_to_all | solution.py:778
  111.5 4.4 %finish.1 = (f32[16,8,128]{2,1,0:T(8,128)}, f32[16,16]{1,0:T(8,128)}, f32[16,16]{1,0:T(8,128)}) custom-call(f32[16,16,256]{2,1,0:T(8,128)} %all_to_all.23.received, f32[8,80,128]{2,1,0:T(8,128)} %get-tuple-element.26.stacked, f32[16,16]{1,0:T(8,128)} %beta_ref.1), custom_call_target="tpu_custom_call" | custom-call | tf_op jit(solution)/shard_map/finish/pallas_call | solution.py:779
  (14 shorter events, 0.1 us)
Async XLA Ops:
  2.6 8.5 %collective-permute-start = (f32[4,8,128]{2,1,0:T(8,128)}, f32[4,8,128]{2,1,0:T(8,128)S(1)}, u32[]{:S(2)}, u32[]{:S(2)}) collective-permute-start(f32[4,8,128]{2,1,0:T(8,128)} %get-tuple-element.15), channel_id=1, source_target_pairs={{0,1},{1,2},{2,3},{3,4},{4,5},{5,6},{6,7},{7,8},{8,9},{9,10},{10,1... | collective-permute-start | bytes 49160 | tf_op jit(solution)/shard_map/ppermute | solution.py:715
  4.6 6.5 %collective-permute-start.1 = (f32[4,8,128]{2,1,0:T(8,128)}, f32[4,8,128]{2,1,0:T(8,128)S(1)}, u32[]{:S(2)}, u32[]{:S(2)}) collective-permute-start(f32[4,8,128]{2,1,0:T(8,128)} %get-tuple-element.17), channel_id=1, source_target_pairs={{0,15},{1,0},{2,1},{3,2},{4,3},{5,4},{6,5},{7,6},{8,7},{9,8},{10,9... | collective-permute-start | bytes 49160 | tf_op jit(solution)/shard_map/ppermute | solution.py:716
  12.1 8.7 %copy-start = (f32[4,144,128]{2,1,0:T(8,128)}, f32[4,144,128]{2,1,0:T(8,128)S(1)}, u32[]{:S(2)}) copy-start(f32[4,144,128]{2,1,0:T(8,128)S(1)} %pad_maximum_fusion.own) | copy-start | bytes 884740
  12.1 5.6 %collective-permute-start.3 = (f32[4,144,128]{2,1,0:T(8,128)S(1)}, f32[4,144,128]{2,1,0:T(8,128)S(1)}, u32[]{:S(2)}, u32[]{:S(2)}) collective-permute-start(f32[4,144,128]{2,1,0:T(8,128)S(1)} %pad_maximum_fusion.own), channel_id=1, source_target_pairs={{0,112},{16,0},{32,16},{48,32},{64,48},{80,64},{96,80},{112,96},{1... | collective-permute-start | bytes 884744 | tf_op jit(solution)/shard_map/ppermute | solution.py:719
  13.4 7.4 %collective-permute-start.2 = (f32[4,144,128]{2,1,0:T(8,128)S(1)}, f32[4,144,128]{2,1,0:T(8,128)S(1)}, u32[]{:S(2)}, u32[]{:S(2)}) collective-permute-start(f32[4,144,128]{2,1,0:T(8,128)S(1)} %pad_maximum_fusion.own), channel_id=1, source_target_pairs={{0,16},{16,32},{32,48},{48,64},{64,80},{80,96},{96,112},{112,0},{1... | collective-permute-start | bytes 884744 | tf_op jit(solution)/shard_map/ppermute | solution.py:718
  17.7 3.1 %copy-start.2 = (f32[4,144,128]{2,1,0:T(8,128)}, f32[4,144,128]{2,1,0:T(8,128)S(1)}, u32[]{:S(2)}) copy-start(f32[4,144,128]{2,1,0:T(8,128)S(1)} %collective-permute-done.3.right) | copy-start | bytes 884740
  20.8 0.7 copy-start.3
  55.2 7.2 %collective-permute-start.4 = (f32[2,8,128]{2,1,0:T(8,128)}, f32[2,8,128]{2,1,0:T(8,128)S(1)}, u32[]{:S(2)}, u32[]{:S(2)}) collective-permute-start(f32[2,8,128]{2,1,0:T(8,128)} %get-tuple-element.21), channel_id=1, source_target_pairs={{0,1},{1,2},{2,3},{3,4},{4,5},{5,6},{6,7},{7,8},{8,9},{9,10},{10,1... | collective-permute-start | bytes 24584 | tf_op jit(solution)/shard_map/ppermute | solution.py:758
  55.8 6.5 %collective-permute-start.5 = (f32[2,8,128]{2,1,0:T(8,128)}, f32[2,8,128]{2,1,0:T(8,128)S(1)}, u32[]{:S(2)}, u32[]{:S(2)}) collective-permute-start(f32[2,8,128]{2,1,0:T(8,128)} %get-tuple-element.23), channel_id=1, source_target_pairs={{0,15},{1,0},{2,1},{3,2},{4,3},{5,4},{6,5},{7,6},{8,7},{9,8},{10,9... | collective-permute-start | bytes 24584 | tf_op jit(solution)/shard_map/ppermute | solution.py:759
  63.3 5.8 %copy-start.1 = (f32[2,144,128]{2,1,0:T(8,128)}, f32[2,144,128]{2,1,0:T(8,128)S(1)}, u32[]{:S(2)}) copy-start(f32[2,144,128]{2,1,0:T(8,128)S(1)} %pad_maximum_fusion.1.misfit) | copy-start | bytes 442372
  63.3 2.7 %collective-permute-start.7 = (f32[2,144,128]{2,1,0:T(8,128)S(1)}, f32[2,144,128]{2,1,0:T(8,128)S(1)}, u32[]{:S(2)}, u32[]{:S(2)}) collective-permute-start(f32[2,144,128]{2,1,0:T(8,128)S(1)} %pad_maximum_fusion.1.misfit), channel_id=1, source_target_pairs={{0,112},{16,0},{32,16},{48,32},{64,48},{80,64},{96,80},{112,96},{1... | collective-permute-start | bytes 442376 | tf_op jit(solution)/shard_map/ppermute | solution.py:762
  63.3 5.8 %collective-permute-start.6 = (f32[2,144,128]{2,1,0:T(8,128)S(1)}, f32[2,144,128]{2,1,0:T(8,128)S(1)}, u32[]{:S(2)}, u32[]{:S(2)}) collective-permute-start(f32[2,144,128]{2,1,0:T(8,128)S(1)} %pad_maximum_fusion.1.misfit), channel_id=1, source_target_pairs={{0,16},{16,32},{32,48},{48,64},{64,80},{80,96},{96,112},{112,0},{1... | collective-permute-start | bytes 442376 | tf_op jit(solution)/shard_map/ppermute | solution.py:761
  66.0 3.1 %copy-start.4 = (f32[2,144,128]{2,1,0:T(8,128)}, f32[2,144,128]{2,1,0:T(8,128)S(1)}, u32[]{:S(2)}) copy-start(f32[2,144,128]{2,1,0:T(8,128)S(1)} %collective-permute-done.7.misfit_right) | copy-start | bytes 442372
  69.1 0.7 copy-start.5

commit v5 on v4

--- a/solution.py
+++ b/solution.py
@@ -14,7 +14,7 @@
 LANES = 128
 HALO = 8
 AXES = ("mx", "my")
-VMEM_LIMIT = 56 * 1024 * 1024
+VMEM_LIMIT = 50 * 1024 * 1024
 
 F_RATIO = 0
 F_PIVOT = 15
@@ -390,13 +390,14 @@
             if k + 1 < layer_count:
                 ratio = get(F_RATIO + k, t=t)
                 bed = bed + ratio * beds[k + 1][t]
-                below = ratio * tops[k + 1][t]
-            surf = jnp.where(depth[t] == float(k + 1), top[t], below)
-            if bed_col is not None:
+                if top_col is not None:
+                    below = ratio * tops[k + 1][t]
+            beds[k].append(bed)
+            if top_col is not None:
+                surf = jnp.where(depth[t] == float(k + 1), top[t], below)
                 bed_col[k, i, t] = bed
-            top_col[k, i, t] = surf
-            beds[k].append(bed)
-            tops[k].append(surf)
+                top_col[k, i, t] = surf
+                tops[k].append(surf)
     return inv_lat, beds, tops
 
 
@@ -414,7 +415,7 @@
             field[c, k, i + 1, tiles + 1] = right_column * right[c]
 
 
-def sweep(source, target, wide, stride, bed_source=None, top_col=None, top_source=None):
+def sweep(source, target, wide, stride, unroll, bed_source=None, top_col=None, top_source=None):
     layer_count, count, tiles = target.shape[1], target.shape[2] - 2, target.shape[3] - 2
     def body(i, carry):
         for t in range(tiles):
@@ -439,17 +440,17 @@
                     put_tile(target, (c, k, i + 1), t, tiles, stride, value)
         return carry
 
-    lax.fori_loop(0, count, body, 0, unroll=6)
+    lax.fori_loop(0, count, body, 0, unroll=unroll)
     wrap_layers(target, tiles)
 
 
 def velocity_kernel(
     vectors, flags, message, basis, fields,
     misfit, low, high,
-    wide, top_col, one, two, source, surface, flat,
+    wide, one, two, source, surface, flat,
 ):
     tile_x = LANES // vectors
-    layer_count, count, tiles = top_col.shape[:3]
+    layer_count, count, tiles = one.shape[1], one.shape[2] - 2, one.shape[3] - 2
     tile_y = count * 8 - 2 * HALO
     offset = tile_x // 2
     group = lane_ids((8, LANES)) // vectors
@@ -460,7 +461,7 @@
     def prepare(i, carry):
         smooth = [y[0] * basis[0, i, t] + y[1] * basis[1, i, t] + y[2] * basis[2, i, t] for t in range(3)]
         smooth = reblock(smooth, vectors, tiles, offset)
-        inv_lat, beds, _ = prepare_row(wide, i, None, top_col, layer_count, tiles)
+        inv_lat, beds, _ = prepare_row(wide, i, None, None, layer_count, tiles)
         values = [
             [get_field(wide, F_BED + c, i, t) * smooth[t] for t in range(tiles)] for c in range(2)
         ]
@@ -474,15 +475,25 @@
 
     lax.fori_loop(0, count, prepare, 0, unroll=6)
     wrap_layers(one, tiles)
-    sweep(one, two, wide, vectors, bed_source=source)
-    sweep(two, one, wide, vectors, bed_source=source)
+    sweep(one, two, wide, vectors, count, bed_source=source)
+    sweep(two, one, wide, vectors, count, bed_source=source)
 
     def finish(i, carry):
         across = [(c, t) for c in range(2) for t in range(tiles)]
-        values = {(c, t): top_col[0, i, t] * source[c, i, t] for c, t in across}
+        values, carried = {}, {}
         for k in range(layer_count):
             for c, t in across:
-                values[c, t] = values[c, t] + top_col[k, i, t] * lateral_sum(one, (c, k), i, t)
+                value = lateral_sum(one, (c, k), i, t)
+                if k == 0:
+                    value = value + source[c, i, t]
+                    values[c, t] = value
+                else:
+                    value = value + get_field(wide, F_RATIO + k - 1, i, t) * carried[c, t]
+                    deep = get_field(wide, F_LAYER, i, t) > float(k)
+                    values[c, t] = jnp.where(deep, value, values[c, t])
+                carried[c, t] = value
+        for c, t in across:
+            values[c, t] = values[c, t] * get_field(wide, F_TOP, i, t)
         for c in range(2):
             surface[c, i] = to_own([values[c, t] for t in range(tiles)], vectors, offset)
         return carry
@@ -513,7 +524,7 @@
 def adjoint_kernel(
     vectors, flags, fields, misfit, misfit_left, misfit_right, basis, previous,
     out, stacked,
-    wide, top_col, one, two, source, bed_col, sides, spread, bed, reaction, v0, v1, v2, natural, flat,
+    wide, one, two, source, top_col, bed_col, sides, spread, bed, reaction, v0, v1, v2, natural, flat,
 ):
     tile_x = LANES // vectors
     layer_count, count, tiles = top_col.shape[:3]
@@ -547,8 +558,8 @@
 
     lax.fori_loop(0, count, prepare, 0, unroll=6)
     wrap_layers(one, tiles)
-    sweep(one, two, wide, vectors, top_col=top_col, top_source=source)
-    sweep(two, one, wide, vectors, top_col=top_col, top_source=source)
+    sweep(one, two, wide, vectors, 6, top_col=top_col, top_source=source)
+    sweep(two, one, wide, vectors, 6, top_col=top_col, top_source=source)
 
     def finish(i, carry):
         totals = {}
@@ -696,20 +707,34 @@
     def shape(*dims):
         return jax.ShapeDtypeStruct(dims, f32)
 
+    def near(*dims):
+        return pltpu.VMEM(dims, f32)
+
+    def keep(array):
+        return pltpu.with_memory_space_constraint(array, pltpu.VMEM)
+
+    def far(array):
+        return pltpu.with_memory_space_constraint(array, pltpu.HBM)
+
     packed, previous, low, high = pl.pallas_call(
         pack_kernel,
         out_shape=(
-            shape(tiles, tile_y, LANES), shape(tile_y, LANES), shape(tiles, HALO, LANES), shape(tiles, HALO, LANES)
+            near(tiles, tile_y, LANES), near(tile_y, LANES), near(tiles, HALO, LANES), near(tiles, HALO, LANES)
         ),
         scratch_shapes=[pltpu.VMEM((tiles * LANES, tile_y), f32)],
         compiler_params=params(),
         name="pack",
     )(
-        lanczos_block, previous_block, prior_reaction, vert_coupling, horiz_coupling,
-        friction, base_velocity, layers,
+        *map(
+            far,
+            (
+                lanczos_block, previous_block, prior_reaction, vert_coupling, horiz_coupling,
+                friction, base_velocity, layers,
+            ),
+        )
     )
     table = pl.pallas_call(
-        table_kernel, out_shape=shape(devices, LANES), compiler_params=params(), name="table"
+        table_kernel, out_shape=near(devices, LANES), compiler_params=params(), name="table"
     )(obs_dest.reshape(1, obs_rows), obs_cell.reshape(1, obs_rows), obs_weight.T)
 
     from_low = lax.ppermute(high, "my", forward_y)
@@ -727,20 +752,19 @@
     message, basis, fields = pl.pallas_call(
         functools.partial(moment_kernel, vectors),
         out_shape=(
-            shape(devices, LANES), shape(3, count, 3, 8, LANES), shape(groups, count, 8, LANES)
+            near(devices, LANES), near(3, count, 3, 8, LANES), near(groups, count, 8, LANES)
         ),
         in_specs=[smem, vmem, vmem, vmem, vmem],
         scratch_shapes=[pltpu.VMEM((3 + groups, rows, LANES), f32), blocked(3, count), blocked(count, 3)]
         + [blocked(count + 2, 5)] * 3,
         compiler_params=params(),
         name="moments",
-    )(flags, own, left, right, table)
+    )(flags, keep(own), keep(left), keep(right), table)
     message = lax.all_to_all(message, AXES, split_axis=0, concat_axis=0, tiled=True)
 
     def columns(width):
         return [
             pltpu.VMEM((groups, count, 8, 4 * width * LANES), f32),
-            blocked(layer_count, count, width),
             blocked(2, layer_count, count + 2, width + 2),
             blocked(2, layer_count, count + 2, width + 2),
             blocked(2, count, width),
@@ -748,7 +772,7 @@
 
     misfit, low, high = pl.pallas_call(
         functools.partial(velocity_kernel, vectors),
-        out_shape=(shape(2, tile_y, LANES), shape(2, HALO, LANES), shape(2, HALO, LANES)),
+        out_shape=(near(2, tile_y, LANES), near(2, HALO, LANES), near(2, HALO, LANES)),
         in_specs=[smem] + [vmem] * 3,
         scratch_shapes=columns(2) + [blocked(2, count), pltpu.VMEM((rows, LANES), f32)],
         compiler_params=params(),
@@ -763,15 +787,16 @@
 
     products, stacked = pl.pallas_call(
         functools.partial(adjoint_kernel, vectors),
-        out_shape=(shape(size_x, vectors, 2 * LANES), shape(tile_x, 5 * vectors, tile_y)),
+        out_shape=(near(size_x, vectors, 2 * LANES), near(tile_x, 5 * vectors, tile_y)),
         in_specs=[smem] + [vmem] * 6,
         scratch_shapes=columns(3)
-        + [blocked(layer_count, count, 3), pltpu.VMEM((2, 3, rows, LANES), f32), blocked(2, 3, count), blocked(2, count, 3), blocked(count, 3)]
+        + [blocked(layer_count, count, 3)] * 2
+        + [pltpu.VMEM((2, 3, rows, LANES), f32), blocked(2, 3, count), blocked(2, count, 3), blocked(count, 3)]
         + [blocked(count + 2, 5)] * 3
         + [blocked(count), pltpu.VMEM((rows, LANES), f32)],
         compiler_params=params(),
         name="adjoint",
-    )(flags, fields, misfit, misfit_left, misfit_right, basis, previous)
+    )(flags, fields, keep(misfit), keep(misfit_left), keep(misfit_right), basis, previous)
 
     products = lax.all_to_all(products, "mx", split_axis=0, concat_axis=0, tiled=True)
     products = jnp.broadcast_to(jnp.sum(products, axis=0)[None], (size_y, vectors, 2 * LANES))

time: 116 us -> 104 us (0.90)
  Pallas kernels: 42 us -> 33.6 us
  other arithmetic: 2.58 us -> 0.14 us
  blocking collectives: 42 us -> 40.1 us
    pallas_call x5, Pallas kernels: 37.6 us -> 30.3 us  [the longest x1 15.5 us: shards(): pl.pallas_call(functools.partial(adjoint_kernel, vectors), out_shape=(nea...]
    ppermute x1, waiting for transfers between devices: 1.36 us -> 2.57 us  [shards(): right = lax.ppermute(own, 'mx', backward_x)]
  transfers between devices with their start and end apart: 8 -> 8, of which waited for: 6 -> 6; matrix products, arithmetic and copies ran while one was open for 1% -> 0% of each run, Pallas kernels for 2% -> 1%
where the time goes in v5:
time: 104 us
  blocking collectives  40.1 us (39%)
  Pallas kernels  33.6 us (32%)
  waiting for transfers between devices  14.2 us (14%)
  starting transfers between devices  14 us (13%)
    all_to_all x1, blocking collectives, shards(): lax.all_to_all(message, AXES, split_axis=0, concat_axis=0, tiled=True)  16.6 us
    pallas_call x1, Pallas kernels, shards(): pl.pallas_call(functools.partial(adjoint_kernel, vectors), out_shape=(nea...  15.5 us
    all_to_all x1, blocking collectives, shards(): lax.all_to_all(products, 'my', split_axis=0, concat_axis=0, tiled=True)  15 us
    pallas_call x1, Pallas kernels, shards(): pl.pallas_call(functools.partial(velocity_kernel, vectors), out_shape=(ne...  10.6 us
    ppermute x2, starting transfers between devices, shards(): from_high = lax.ppermute(low, 'my', backward_y)  9.17 us
    all_to_all x1, blocking collectives, shards(): lax.all_to_all(products, 'mx', split_axis=0, concat_axis=0, tiled=True)  8.52 us
    pallas_call x1, Pallas kernels, shards(): pl.pallas_call(functools.partial(finish_kernel, float(cells)), out_shape=...  3.36 us
    ppermute x2, waiting for transfers between devices, shards(): from_low = lax.ppermute(high, 'my', forward_y)  3.26 us
  transfers between devices with their start and end apart: 8, of which 6 were waited for; matrix products, arithmetic and copies ran while one was open for 0% of the time, Pallas kernels for 1%

profile of v5, /device:TPU:0, one launch (start us, length us, event | category | flops | bytes accessed | tf_op | source)
XLA Modules:
  0.0 103.6 jit_solution(17026972077516199014)
XLA Ops:
  0.6 1.2 %pack.1 = (f32[4,128,128]{2,1,0:T(8,128)S(1)}, f32[128,128]{1,0:T(8,128)S(1)}, f32[4,8,128]{2,1,0:T(8,128)S(1)}, f32[4,8,128]{2,1,0:T(8,128)S(1)}) custom-call(f32[16,8,128]{2,1,0:T(8,128)} %block.1, f32[16,8,128]{2,1,0:T(8,128)} %previous.1, f32[8,128]{1,0:T(8,128)} %reaction.1, f32[15,8,128]{2,1,0:T(8,128)} %vert.1, f32[16,8,128]{2,1,0:T(8,128)} %horiz.1, ...), custom_call_target="tpu_custom_call" | custom-call | tf_op jit(solution)/shard_map/pack/pallas_call | solution.py:719
  1.9 2.1 %collective-permute-start = (f32[4,8,128]{2,1,0:T(8,128)S(1)}, f32[4,8,128]{2,1,0:T(8,128)S(1)}, u32[]{:S(2)}, u32[]{:S(2)}) collective-permute-start(f32[4,8,128]{2,1,0:T(8,128)S(1)} %get-tuple-element.15), channel_id=1, source_target_pairs={{0,1},{1,2},{2,3},{3,4},{4,5},{5,6},{6,7},{7,8},{8,9},{9,10},{10,1... | collective-permute-start | bytes 49160 | tf_op jit(solution)/shard_map/ppermute | solution.py:740
  3.9 4.7 %collective-permute-start.1 = (f32[4,8,128]{2,1,0:T(8,128)S(1)}, f32[4,8,128]{2,1,0:T(8,128)S(1)}, u32[]{:S(2)}, u32[]{:S(2)}) collective-permute-start(f32[4,8,128]{2,1,0:T(8,128)S(1)} %get-tuple-element.17), channel_id=1, source_target_pairs={{0,15},{1,0},{2,1},{3,2},{4,3},{5,4},{6,5},{7,6},{8,7},{9,8},{10,9... | collective-permute-start | bytes 49160 | tf_op jit(solution)/shard_map/ppermute | solution.py:741
  8.6 1.6 %collective-permute-done = f32[4,8,128]{2,1,0:T(8,128)S(1)} collective-permute-done((f32[4,8,128]{2,1,0:T(8,128)S(1)}, f32[4,8,128]{2,1,0:T(8,128)S(1)}, u32[]{:S(2)}, u32[]{:S(2)}) %collective-permute-start) | collective-permute-done | bytes 16416 | tf_op jit(solution)/shard_map/ppermute | solution.py:740
  10.2 0.0 collective-permute-done.1
  10.3 1.3 %collective-permute-start.3 = (f32[4,144,128]{2,1,0:T(8,128)S(1)}, f32[4,144,128]{2,1,0:T(8,128)S(1)}, u32[]{:S(2)}, u32[]{:S(2)}) collective-permute-start(f32[4,144,128]{2,1,0:T(8,128)S(1)} %pad_maximum_fusion.own), channel_id=1, source_target_pairs={{0,112},{16,0},{32,16},{48,32},{64,48},{80,64},{96,80},{112,96},{1... | collective-permute-start | bytes 884744 | tf_op jit(solution)/shard_map/ppermute | solution.py:744
  11.6 0.0 collective-permute-start.2
  11.6 0.0 copy-start.3
  11.6 0.7 copy-done.3
  12.3 0.0 copy-done.1
  12.3 0.0 copy-done.2
  12.3 0.9 table.1
  13.2 0.1 add_convert_fusion.flags
  13.3 2.6 %collective-permute-done.3.right = f32[4,144,128]{2,1,0:T(8,128)S(1)} collective-permute-done((f32[4,144,128]{2,1,0:T(8,128)S(1)}, f32[4,144,128]{2,1,0:T(8,128)S(1)}, u32[]{:S(2)}, u32[]{:S(2)}) %collective-permute-start.3) | collective-permute-done | bytes 294944 | tf_op jit(solution)/shard_map/ppermute | solution.py:744
  15.8 3.1 %collective-permute-done.2.left = f32[4,144,128]{2,1,0:T(8,128)S(1)} collective-permute-done((f32[4,144,128]{2,1,0:T(8,128)S(1)}, f32[4,144,128]{2,1,0:T(8,128)S(1)}, u32[]{:S(2)}, u32[]{:S(2)}) %collective-permute-start.2) | collective-permute-done | bytes 294944 | tf_op jit(solution)/shard_map/ppermute | solution.py:743
  19.0 2.1 %moments.1 = (f32[128,128]{1,0:T(8,128)S(1)}, f32[3,18,3,8,128]{4,3,2,1,0:T(8,128)S(1)}, f32[10,18,8,128]{3,2,1,0:T(8,128)S(1)}) custom-call(f32[2]{0:T(128)S(1)} %add_convert_fusion.flags, f32[4,144,128]{2,1,0:T(8,128)S(1)} %pad_maximum_fusion.own, f32[4,144,128]{2,1,0:T(8,128)S(1)} %collective-permute-done.2.left, ...), custom_call_target="tpu_custom_call" | custom-call | tf_op jit(solution)/shard_map/moments/pallas_call | solution.py:752
  21.1 16.6 %all_to_all.21 = f32[128,1,128]{2,1,0:T(1,128)S(1)} all-to-all(f32[128,1,128]{2,1,0:T(1,128)S(1)} %bitcast.10), channel_id=1, replica_groups=mesh['mx'=8,'my'=16] {'mx','my'}, dimensions={0} | all-to-all | bytes 131072 | tf_op jit(solution)/shard_map/all_to_all | solution.py:763
  37.7 10.6 %velocity.3 = (f32[2,128,128]{2,1,0:T(8,128)S(1)}, f32[2,8,128]{2,1,0:T(8,128)S(1)}, f32[2,8,128]{2,1,0:T(8,128)S(1)}) custom-call(f32[2]{0:T(128)S(1)} %add_convert_fusion.flags, f32[128,128]{1,0:T(8,128)S(1)} %bitcast.9, f32[3,18,3,8,128]{4,3,2,1,0:T(8,128)S(1)} %get-tuple-element.20.basis, f32[10,18,8,128]{3,2,1,0:T(8,128)S(1)} %get-tuple-element.18.fields), custom_call_target="tpu_custom_call" | custom-call | tf_op jit(solution)/shard_map/velocity/pallas_call | solution.py:773
  48.2 0.9 collective-permute-start.4
  49.1 4.5 %collective-permute-start.5 = (f32[2,8,128]{2,1,0:T(8,128)S(1)}, f32[2,8,128]{2,1,0:T(8,128)S(1)}, u32[]{:S(2)}, u32[]{:S(2)}) collective-permute-start(f32[2,8,128]{2,1,0:T(8,128)S(1)} %get-tuple-element.23), channel_id=1, source_target_pairs={{0,15},{1,0},{2,1},{3,2},{4,3},{5,4},{6,5},{7,6},{8,7},{9,8},{10,9... | collective-permute-start | bytes 24584 | tf_op jit(solution)/shard_map/ppermute | solution.py:783
  53.6 1.6 %collective-permute-done.4 = f32[2,8,128]{2,1,0:T(8,128)S(1)} collective-permute-done((f32[2,8,128]{2,1,0:T(8,128)S(1)}, f32[2,8,128]{2,1,0:T(8,128)S(1)}, u32[]{:S(2)}, u32[]{:S(2)}) %collective-permute-start.4) | collective-permute-done | bytes 8224 | tf_op jit(solution)/shard_map/ppermute | solution.py:782
  55.3 0.0 collective-permute-done.5
  55.3 0.0 collective-permute-start.7
  55.3 0.5 collective-permute-start.6
  55.8 2.2 %collective-permute-done.7.misfit_right = f32[2,144,128]{2,1,0:T(8,128)S(1)} collective-permute-done((f32[2,144,128]{2,1,0:T(8,128)S(1)}, f32[2,144,128]{2,1,0:T(8,128)S(1)}, u32[]{:S(2)}, u32[]{:S(2)}) %collective-permute-start.7) | collective-permute-done | bytes 147488 | tf_op jit(solution)/shard_map/ppermute | solution.py:786
  58.0 3.1 %collective-permute-done.6.misfit_left = f32[2,144,128]{2,1,0:T(8,128)S(1)} collective-permute-done((f32[2,144,128]{2,1,0:T(8,128)S(1)}, f32[2,144,128]{2,1,0:T(8,128)S(1)}, u32[]{:S(2)}, u32[]{:S(2)}) %collective-permute-start.6) | collective-permute-done | bytes 147488 | tf_op jit(solution)/shard_map/ppermute | solution.py:785
  61.1 15.5 %adjoint.1 = (f32[8,16,256]{2,1,0:T(8,128)S(1)}, f32[8,80,128]{2,1,0:T(8,128)S(1)}) custom-call(f32[2]{0:T(128)S(1)} %add_convert_fusion.flags, f32[10,18,8,128]{3,2,1,0:T(8,128)S(1)} %get-tuple-element.18.fields, f32[2,144,128]{2,1,0:T(8,128)S(1)} %pad_maximum_fusion.1.misfit, f32[2,144,128]{2,1,0:T(8,128)S(1)} %collective-permute-done.6.misfit_left, ...), custom_call_target="tpu_custom_call" | custom-call | tf_op jit(solution)/shard_map/adjoint/pallas_call | solution.py:788
  76.6 8.5 %all_to_all.22 = f32[8,16,256]{2,1,0:T(8,128)S(1)} all-to-all(f32[8,16,256]{2,1,0:T(8,128)S(1)} %get-tuple-element.25), channel_id=1, replica_groups=mesh['mx'=8,'my'=16] {'mx'}, dimensions={0} | all-to-all | bytes 262144 | tf_op jit(solution)/shard_map/all_to_all | solution.py:801
  85.2 0.0 copy-start
  85.2 15.0 %all_to_all.23.received = f32[16,16,256]{2,1,0:T(8,128)S(1)} all-to-all(f32[16,16,256]{2,1,0:T(8,128)S(1)} %broadcast_in_dim.2), channel_id=1, replica_groups=mesh['mx'=8,'my'=16] {'my'}, dimensions={0} | all-to-all | bytes 524288 | tf_op jit(solution)/shard_map/all_to_all | solution.py:803
  100.2 0.0 copy-done
  100.2 3.4 %finish.1 = (f32[16,8,128]{2,1,0:T(8,128)}, f32[16,16]{1,0:T(8,128)}, f32[16,16]{1,0:T(8,128)}) custom-call(f32[16,16,256]{2,1,0:T(8,128)S(1)} %all_to_all.23.received, f32[8,80,128]{2,1,0:T(8,128)S(1)} %get-tuple-element.26.stacked, f32[16,16]{1,0:T(8,128)S(1)} %copy-done), custom_call_target="tpu_custom_call" | custom-call | tf_op jit(solution)/shard_map/finish/pallas_call | solution.py:804
  (10 shorter events, 0.1 us)
Async XLA Ops:
  1.9 8.4 %collective-permute-start = (f32[4,8,128]{2,1,0:T(8,128)S(1)}, f32[4,8,128]{2,1,0:T(8,128)S(1)}, u32[]{:S(2)}, u32[]{:S(2)}) collective-permute-start(f32[4,8,128]{2,1,0:T(8,128)S(1)} %get-tuple-element.15), channel_id=1, source_target_pairs={{0,1},{1,2},{2,3},{3,4},{4,5},{5,6},{6,7},{7,8},{8,9},{9,10},{10,1... | collective-permute-start | bytes 49160 | tf_op jit(solution)/shard_map/ppermute | solution.py:740
  3.9 6.3 %collective-permute-start.1 = (f32[4,8,128]{2,1,0:T(8,128)S(1)}, f32[4,8,128]{2,1,0:T(8,128)S(1)}, u32[]{:S(2)}, u32[]{:S(2)}) collective-permute-start(f32[4,8,128]{2,1,0:T(8,128)S(1)} %get-tuple-element.17), channel_id=1, source_target_pairs={{0,15},{1,0},{2,1},{3,2},{4,3},{5,4},{6,5},{7,6},{8,7},{9,8},{10,9... | collective-permute-start | bytes 49160 | tf_op jit(solution)/shard_map/ppermute | solution.py:741
  10.3 5.6 %collective-permute-start.3 = (f32[4,144,128]{2,1,0:T(8,128)S(1)}, f32[4,144,128]{2,1,0:T(8,128)S(1)}, u32[]{:S(2)}, u32[]{:S(2)}) collective-permute-start(f32[4,144,128]{2,1,0:T(8,128)S(1)} %pad_maximum_fusion.own), channel_id=1, source_target_pairs={{0,112},{16,0},{32,16},{48,32},{64,48},{80,64},{96,80},{112,96},{1... | collective-permute-start | bytes 884744 | tf_op jit(solution)/shard_map/ppermute | solution.py:744
  11.6 7.4 %collective-permute-start.2 = (f32[4,144,128]{2,1,0:T(8,128)S(1)}, f32[4,144,128]{2,1,0:T(8,128)S(1)}, u32[]{:S(2)}, u32[]{:S(2)}) collective-permute-start(f32[4,144,128]{2,1,0:T(8,128)S(1)} %pad_maximum_fusion.own), channel_id=1, source_target_pairs={{0,16},{16,32},{32,48},{48,64},{64,80},{80,96},{96,112},{112,0},{1... | collective-permute-start | bytes 884744 | tf_op jit(solution)/shard_map/ppermute | solution.py:743
  11.6 0.7 copy-start.3
  11.6 0.7 copy-start.1
  11.6 0.7 copy-start.2
  48.2 7.0 %collective-permute-start.4 = (f32[2,8,128]{2,1,0:T(8,128)S(1)}, f32[2,8,128]{2,1,0:T(8,128)S(1)}, u32[]{:S(2)}, u32[]{:S(2)}) collective-permute-start(f32[2,8,128]{2,1,0:T(8,128)S(1)} %get-tuple-element.21), channel_id=1, source_target_pairs={{0,1},{1,2},{2,3},{3,4},{4,5},{5,6},{6,7},{7,8},{8,9},{9,10},{10,1... | collective-permute-start | bytes 24584 | tf_op jit(solution)/shard_map/ppermute | solution.py:782
  49.1 6.1 %collective-permute-start.5 = (f32[2,8,128]{2,1,0:T(8,128)S(1)}, f32[2,8,128]{2,1,0:T(8,128)S(1)}, u32[]{:S(2)}, u32[]{:S(2)}) collective-permute-start(f32[2,8,128]{2,1,0:T(8,128)S(1)} %get-tuple-element.23), channel_id=1, source_target_pairs={{0,15},{1,0},{2,1},{3,2},{4,3},{5,4},{6,5},{7,6},{8,7},{9,8},{10,9... | collective-permute-start | bytes 24584 | tf_op jit(solution)/shard_map/ppermute | solution.py:783
  55.3 2.7 %collective-permute-start.7 = (f32[2,144,128]{2,1,0:T(8,128)S(1)}, f32[2,144,128]{2,1,0:T(8,128)S(1)}, u32[]{:S(2)}, u32[]{:S(2)}) collective-permute-start(f32[2,144,128]{2,1,0:T(8,128)S(1)} %pad_maximum_fusion.1.misfit), channel_id=1, source_target_pairs={{0,112},{16,0},{32,16},{48,32},{64,48},{80,64},{96,80},{112,96},{1... | collective-permute-start | bytes 442376 | tf_op jit(solution)/shard_map/ppermute | solution.py:786
  55.3 5.8 %collective-permute-start.6 = (f32[2,144,128]{2,1,0:T(8,128)S(1)}, f32[2,144,128]{2,1,0:T(8,128)S(1)}, u32[]{:S(2)}, u32[]{:S(2)}) collective-permute-start(f32[2,144,128]{2,1,0:T(8,128)S(1)} %pad_maximum_fusion.1.misfit), channel_id=1, source_target_pairs={{0,16},{16,32},{32,48},{48,64},{64,80},{80,96},{96,112},{112,0},{1... | collective-permute-start | bytes 442376 | tf_op jit(solution)/shard_map/ppermute | solution.py:785
  85.2 15.1 %copy-start = (f32[16,16]{1,0:T(8,128)S(1)}, f32[16,16]{1,0:T(8,128)}, u32[]{:S(2)}) copy-start(f32[16,16]{1,0:T(8,128)} %beta_ref.1) | copy-start | bytes 3076

commit v6 on v5

--- a/solution.py
+++ b/solution.py
@@ -14,7 +14,6 @@
 LANES = 128
 HALO = 8
 AXES = ("mx", "my")
-VMEM_LIMIT = 50 * 1024 * 1024
 
 F_RATIO = 0
 F_PIVOT = 15
@@ -26,8 +25,8 @@
 FIELDS = 37
 
 
-def params():
-    return pltpu.CompilerParams(vmem_limit_bytes=VMEM_LIMIT)
+def params(mebibytes=34):
+    return pltpu.CompilerParams(vmem_limit_bytes=mebibytes * 1024 * 1024)
 
 
 def lane_ids(shape):
@@ -521,10 +520,25 @@
     high[...] = misfit[:, tile_y - HALO :, :]
 
 
+def spread_kernel(vectors, after, fields, wide, done):
+    expand_all(fields, wide, vectors, 0)
+    done[...] = jnp.ones(done.shape, jnp.float32)
+
+
+def column_kernel(after, wide, bed_col, top_col):
+    layer_count, count, tiles = top_col.shape[:3]
+
+    def body(i, carry):
+        prepare_row(wide, i, bed_col, top_col, layer_count, tiles)
+        return carry
+
+    lax.fori_loop(0, count, body, 0, unroll=6)
+
+
 def adjoint_kernel(
-    vectors, flags, fields, misfit, misfit_left, misfit_right, basis, previous,
+    vectors, flags, wide, bed_col, top_col, misfit, misfit_left, misfit_right, basis, previous,
     out, stacked,
-    wide, one, two, source, top_col, bed_col, sides, spread, bed, reaction, v0, v1, v2, natural, flat,
+    one, two, source, sides, spread, bed, reaction, v0, v1, v2, natural, flat,
 ):
     tile_x = LANES // vectors
     layer_count, count, tiles = top_col.shape[:3]
@@ -540,7 +554,8 @@
 
     def prepare(i, carry):
         values = [[spread[c, t, i] for t in range(tiles)] for c in range(2)]
-        inv_lat, _, tops = prepare_row(wide, i, bed_col, top_col, layer_count, tiles)
+        inv_lat = [get_field(wide, F_INV_LAT, i, t) for t in range(tiles)]
+        tops = [[top_col[k, i, t] for t in range(tiles)] for k in range(layer_count)]
         for t in range(tiles):
             reaction[i, t] = get_field(wide, F_REACT, i, t)
             total = None
@@ -554,7 +569,6 @@
         put_outer(one, i, tops, values, vectors)
         return carry
 
-    expand_all(fields, wide, vectors, 0)
 
     lax.fori_loop(0, count, prepare, 0, unroll=6)
     wrap_layers(one, tiles)
@@ -779,24 +793,42 @@
         name="velocity",
     )(flags, message, basis, fields)
 
+    after, low, high = lax.optimization_barrier((flags, low, high))
     from_low = lax.ppermute(high, "my", forward_y)
     from_high = lax.ppermute(low, "my", backward_y)
-    misfit = jnp.concatenate([from_low * low_flag, misfit, from_high * high_flag], axis=1)
+    wide, done = pl.pallas_call(
+        functools.partial(spread_kernel, vectors),
+        out_shape=(near(groups, count, 8, 12 * LANES), near(8, LANES)),
+        in_specs=[smem, vmem],
+        compiler_params=params(16),
+        name="spread",
+    )(after, fields)
+    misfit = jnp.concatenate(
+        [from_low * (done * low_flag), misfit, from_high * (done * high_flag)], axis=1
+    )
+    after, misfit = lax.optimization_barrier((flags, misfit))
     misfit_left = lax.ppermute(misfit, "mx", forward_x)
     misfit_right = lax.ppermute(misfit, "mx", backward_x)
+
+    bed_col, top_col = pl.pallas_call(
+        column_kernel,
+        out_shape=(near(layer_count, count, 3, 8, LANES), near(layer_count, count, 3, 8, LANES)),
+        in_specs=[smem, vmem],
+        compiler_params=params(16),
+        name="columns",
+    )(after, wide)
 
     products, stacked = pl.pallas_call(
         functools.partial(adjoint_kernel, vectors),
         out_shape=(near(size_x, vectors, 2 * LANES), near(tile_x, 5 * vectors, tile_y)),
-        in_specs=[smem] + [vmem] * 6,
-        scratch_shapes=columns(3)
-        + [blocked(layer_count, count, 3)] * 2
+        in_specs=[smem] + [vmem] * 8,
+        scratch_shapes=columns(3)[1:]
         + [pltpu.VMEM((2, 3, rows, LANES), f32), blocked(2, 3, count), blocked(2, count, 3), blocked(count, 3)]
         + [blocked(count + 2, 5)] * 3
         + [blocked(count), pltpu.VMEM((rows, LANES), f32)],
         compiler_params=params(),
         name="adjoint",
-    )(flags, fields, keep(misfit), keep(misfit_left), keep(misfit_right), basis, previous)
+    )(flags, wide, bed_col, top_col, keep(misfit), keep(misfit_left), keep(misfit_right), basis, previous)
 
     products = lax.all_to_all(products, "mx", split_axis=0, concat_axis=0, tiled=True)
     products = jnp.broadcast_to(jnp.sum(products, axis=0)[None], (size_y, vectors, 2 * LANES))

time: 104 us -> 102 us (0.981)
  waiting for transfers between devices: 14.2 us -> 9.78 us
  Pallas kernels: 33.6 us -> 36.3 us
  blocking collectives: 40.1 us -> 38.7 us
  local copies, waits for them, and re-layouts: 0.73 us -> 2.06 us
    pallas_call x0 -> x2, Pallas kernels: none -> 4.53 us  [the longest x1 3.03 us: shards(): pl.pallas_call(functools.partial(spread_kernel, vectors), out_shape=(near...]
    pallas_call x1, Pallas kernels: 15.5 us -> 13.7 us  [shards(): pl.pallas_call(functools.partial(adjoint_kernel, vectors), out_shape=(nea...]
    ppermute x2, waiting for transfers between devices: 3.26 us -> 1.64 us  [shards(): from_low = lax.ppermute(high, 'my', forward_y)]
    ppermute x1, waiting for transfers between devices: 2.17 us -> 0.66 us  [shards(): misfit_right = lax.ppermute(misfit, 'mx', backward_x)]
    all_to_all x1, blocking collectives: 15 us -> 13.6 us  [shards(): lax.all_to_all(products, 'my', split_axis=0, concat_axis=0, tiled=True)]
    unnamed x8, local copies, waits for them, and re-layouts: 0.71 us -> 2.04 us
    ppermute x1, waiting for transfers between devices: 2.57 us -> 1.24 us  [shards(): right = lax.ppermute(own, 'mx', backward_x)]
  transfers between devices with their start and end apart: 8 -> 8, of which waited for: 6 -> 5; matrix products, arithmetic and copies ran while one was open for 0% -> 0% of each run, Pallas kernels for 1% -> 5%
where the time goes in v6:
time: 102 us
  blocking collectives  38.7 us (38%)
  Pallas kernels  36.3 us (36%)
  starting transfers between devices  14 us (14%)
  waiting for transfers between devices  9.78 us (10%)
  local copies, waits for them, and re-layouts  2.06 us (2%)
    all_to_all x1, blocking collectives, shards(): lax.all_to_all(message, AXES, split_axis=0, concat_axis=0, tiled=True)  16.6 us
    pallas_call x1, Pallas kernels, shards(): pl.pallas_call(functools.partial(adjoint_kernel, vectors), out_shape=(nea...  13.7 us
    all_to_all x1, blocking collectives, shards(): lax.all_to_all(products, 'my', split_axis=0, concat_axis=0, tiled=True)  13.6 us
    pallas_call x1, Pallas kernels, shards(): pl.pallas_call(functools.partial(velocity_kernel, vectors), out_shape=(ne...  10.6 us
    ppermute x2, starting transfers between devices, shards(): from_high = lax.ppermute(low, 'my', backward_y)  9.17 us
    all_to_all x1, blocking collectives, shards(): lax.all_to_all(products, 'mx', split_axis=0, concat_axis=0, tiled=True)  8.52 us
    pallas_call x1, Pallas kernels, shards(): pl.pallas_call(functools.partial(finish_kernel, float(cells)), out_shape=...  3.36 us
    ppermute x1, waiting for transfers between devices, shards(): misfit_left = lax.ppermute(misfit, 'mx', forward_x)  3.12 us
  transfers between devices with their start and end apart: 8, of which 5 were waited for; matrix products, arithmetic and copies ran while one was open for 0% of the time, Pallas kernels for 5%

profile of v6, /device:TPU:0, one launch (start us, length us, event | category | flops | bytes accessed | tf_op | source)
XLA Modules:
  0.0 101.7 jit_solution(14490561624515033506)
XLA Ops:
  0.6 1.2 %pack.1 = (f32[4,128,128]{2,1,0:T(8,128)S(1)}, f32[128,128]{1,0:T(8,128)S(1)}, f32[4,8,128]{2,1,0:T(8,128)S(1)}, f32[4,8,128]{2,1,0:T(8,128)S(1)}) custom-call(f32[16,8,128]{2,1,0:T(8,128)} %block.1, f32[16,8,128]{2,1,0:T(8,128)} %previous.1, f32[8,128]{1,0:T(8,128)} %reaction.1, f32[15,8,128]{2,1,0:T(8,128)} %vert.1, f32[16,8,128]{2,1,0:T(8,128)} %horiz.1, ...), custom_call_target="tpu_custom_call" | custom-call | tf_op jit(solution)/shard_map/pack/pallas_call | solution.py:733
  1.9 2.1 %collective-permute-start = (f32[4,8,128]{2,1,0:T(8,128)S(1)}, f32[4,8,128]{2,1,0:T(8,128)S(1)}, u32[]{:S(2)}, u32[]{:S(2)}) collective-permute-start(f32[4,8,128]{2,1,0:T(8,128)S(1)} %get-tuple-element.24), channel_id=1, source_target_pairs={{0,1},{1,2},{2,3},{3,4},{4,5},{5,6},{6,7},{7,8},{8,9},{9,10},{10,1... | collective-permute-start | bytes 49160 | tf_op jit(solution)/shard_map/ppermute | solution.py:754
  3.9 4.7 %collective-permute-start.1 = (f32[4,8,128]{2,1,0:T(8,128)S(1)}, f32[4,8,128]{2,1,0:T(8,128)S(1)}, u32[]{:S(2)}, u32[]{:S(2)}) collective-permute-start(f32[4,8,128]{2,1,0:T(8,128)S(1)} %get-tuple-element.26), channel_id=1, source_target_pairs={{0,15},{1,0},{2,1},{3,2},{4,3},{5,4},{6,5},{7,6},{8,7},{9,8},{10,9... | collective-permute-start | bytes 49160 | tf_op jit(solution)/shard_map/ppermute | solution.py:755
  8.6 1.6 %collective-permute-done = f32[4,8,128]{2,1,0:T(8,128)S(1)} collective-permute-done((f32[4,8,128]{2,1,0:T(8,128)S(1)}, f32[4,8,128]{2,1,0:T(8,128)S(1)}, u32[]{:S(2)}, u32[]{:S(2)}) %collective-permute-start) | collective-permute-done | bytes 16416 | tf_op jit(solution)/shard_map/ppermute | solution.py:754
  10.2 0.0 collective-permute-done.1
  10.3 1.3 %collective-permute-start.3 = (f32[4,144,128]{2,1,0:T(8,128)S(1)}, f32[4,144,128]{2,1,0:T(8,128)S(1)}, u32[]{:S(2)}, u32[]{:S(2)}) collective-permute-start(f32[4,144,128]{2,1,0:T(8,128)S(1)} %pad_maximum_fusion.own), channel_id=1, source_target_pairs={{0,112},{16,0},{32,16},{48,32},{64,48},{80,64},{96,80},{112,96},{1... | collective-permute-start | bytes 884744 | tf_op jit(solution)/shard_map/ppermute | solution.py:758
  11.6 0.0 collective-permute-start.2
  11.6 0.7 copy-done.1
  12.3 0.7 copy-done.2
  13.0 0.7 copy-done.3
  13.7 0.9 table.1
  14.5 0.1 add_convert_fusion.flags.after
  14.6 1.2 %collective-permute-done.3.right = f32[4,144,128]{2,1,0:T(8,128)S(1)} collective-permute-done((f32[4,144,128]{2,1,0:T(8,128)S(1)}, f32[4,144,128]{2,1,0:T(8,128)S(1)}, u32[]{:S(2)}, u32[]{:S(2)}) %collective-permute-start.3) | collective-permute-done | bytes 294944 | tf_op jit(solution)/shard_map/ppermute | solution.py:758
  15.8 3.1 %collective-permute-done.2.left = f32[4,144,128]{2,1,0:T(8,128)S(1)} collective-permute-done((f32[4,144,128]{2,1,0:T(8,128)S(1)}, f32[4,144,128]{2,1,0:T(8,128)S(1)}, u32[]{:S(2)}, u32[]{:S(2)}) %collective-permute-start.2) | collective-permute-done | bytes 294944 | tf_op jit(solution)/shard_map/ppermute | solution.py:757
  19.0 2.1 %moments.1 = (f32[128,128]{1,0:T(8,128)S(1)}, f32[3,18,3,8,128]{4,3,2,1,0:T(8,128)S(1)}, f32[10,18,8,128]{3,2,1,0:T(8,128)S(1)}) custom-call(f32[2]{0:T(128)S(1)} %add_convert_fusion.flags.after, f32[4,144,128]{2,1,0:T(8,128)S(1)} %pad_maximum_fusion.own, f32[4,144,128]{2,1,0:T(8,128)S(1)} %collective-permute-done.2.left, ...), custom_call_target="tpu_custom_call" | custom-call | tf_op jit(solution)/shard_map/moments/pallas_call | solution.py:766
  21.1 16.6 %all_to_all.21 = f32[128,1,128]{2,1,0:T(1,128)S(1)} all-to-all(f32[128,1,128]{2,1,0:T(1,128)S(1)} %bitcast.10), channel_id=1, replica_groups=mesh['mx'=8,'my'=16] {'mx','my'}, dimensions={0} | all-to-all | bytes 131072 | tf_op jit(solution)/shard_map/all_to_all | solution.py:777
  37.7 10.6 %velocity.3 = (f32[2,128,128]{2,1,0:T(8,128)S(1)}, f32[2,8,128]{2,1,0:T(8,128)S(1)}, f32[2,8,128]{2,1,0:T(8,128)S(1)}) custom-call(f32[2]{0:T(128)S(1)} %add_convert_fusion.flags.after, f32[128,128]{1,0:T(8,128)S(1)} %bitcast.9, f32[3,18,3,8,128]{4,3,2,1,0:T(8,128)S(1)} %get-tuple-element.28.basis, f32[10,18,8,128]{3,2,1,0:T(8,128)S(1)} %get-tuple-element.29.fields), custom_call_target="tpu_custom_call" | custom-call | tf_op jit(solution)/shard_map/velocity/pallas_call | solution.py:787
  48.2 0.9 collective-permute-start.4
  49.1 4.5 %collective-permute-start.5 = (f32[2,8,128]{2,1,0:T(8,128)S(1)}, f32[2,8,128]{2,1,0:T(8,128)S(1)}, u32[]{:S(2)}, u32[]{:S(2)}) collective-permute-start(f32[2,8,128]{2,1,0:T(8,128)S(1)} %get-tuple-element.37), channel_id=1, source_target_pairs={{0,15},{1,0},{2,1},{3,2},{4,3},{5,4},{6,5},{7,6},{8,7},{9,8},{10,9... | collective-permute-start | bytes 24584 | tf_op jit(solution)/shard_map/ppermute | solution.py:798
  53.6 3.0 %spread.1 = (f32[10,18,8,1536]{3,2,1,0:T(8,128)S(1)}, f32[8,128]{1,0:T(8,128)S(1)}) custom-call(f32[2]{0:T(128)S(1)} %add_convert_fusion.flags.after, f32[10,18,8,128]{3,2,1,0:T(8,128)S(1)} %get-tuple-element.29.fields), custom_call_target="tpu_custom_call" | custom-call | tf_op jit(solution)/shard_map/spread/pallas_call | solution.py:799
  56.7 0.0 collective-permute-done.4
  56.7 0.0 collective-permute-done.5
  56.8 0.0 collective-permute-start.7
  56.8 0.5 collective-permute-start.6
  57.3 1.5 %columns.1 = (f32[16,18,3,8,128]{4,3,2,1,0:T(8,128)S(1)}, f32[16,18,3,8,128]{4,3,2,1,0:T(8,128)S(1)}) custom-call(f32[2]{0:T(128)S(1)} %add_convert_fusion.flags.after, f32[10,18,8,1536]{3,2,1,0:T(8,128)S(1)} %get-tuple-element.33.wide), custom_call_target="tpu_custom_call" | custom-call | tf_op jit(solution)/shard_map/columns/pallas_call | solution.py:813
  58.8 0.7 collective-permute-done.7.misfit_right
  59.5 3.1 %collective-permute-done.6.misfit_left = f32[2,144,128]{2,1,0:T(8,128)S(1)} collective-permute-done((f32[2,144,128]{2,1,0:T(8,128)S(1)}, f32[2,144,128]{2,1,0:T(8,128)S(1)}, u32[]{:S(2)}, u32[]{:S(2)}) %collective-permute-start.6) | collective-permute-done | bytes 147488 | tf_op jit(solution)/shard_map/ppermute | solution.py:810
  62.6 13.7 %adjoint.1 = (f32[8,16,256]{2,1,0:T(8,128)S(1)}, f32[8,80,128]{2,1,0:T(8,128)S(1)}) custom-call(f32[2]{0:T(128)S(1)} %add_convert_fusion.flags.after, f32[10,18,8,1536]{3,2,1,0:T(8,128)S(1)} %get-tuple-element.33.wide, f32[16,18,3,8,128]{4,3,2,1,0:T(8,128)S(1)} %get-tuple-element.39.bed_col, f32[16,18,3,8,128]{4,3,2,1,0:T(8,128)S(1)} %get-tuple-element.40.top_col, ...), custom_call_target="tpu_custom_call" | custom-call | tf_op jit(solution)/shard_map/adjoint/pallas_call | solution.py:821
  76.2 8.5 %all_to_all.22 = f32[8,16,256]{2,1,0:T(8,128)S(1)} all-to-all(f32[8,16,256]{2,1,0:T(8,128)S(1)} %get-tuple-element.43), channel_id=1, replica_groups=mesh['mx'=8,'my'=16] {'mx'}, dimensions={0} | all-to-all | bytes 262144 | tf_op jit(solution)/shard_map/all_to_all | solution.py:833
  84.8 13.6 %all_to_all.23.received = f32[16,16,256]{2,1,0:T(8,128)S(1)} all-to-all(f32[16,16,256]{2,1,0:T(8,128)S(1)} %broadcast_in_dim.2), channel_id=1, replica_groups=mesh['mx'=8,'my'=16] {'my'}, dimensions={0} | all-to-all | bytes 524288 | tf_op jit(solution)/shard_map/all_to_all | solution.py:835
  98.4 0.0 copy-done
  98.4 3.4 %finish.1 = (f32[16,8,128]{2,1,0:T(8,128)}, f32[16,16]{1,0:T(8,128)}, f32[16,16]{1,0:T(8,128)}) custom-call(f32[16,16,256]{2,1,0:T(8,128)S(1)} %all_to_all.23.received, f32[8,80,128]{2,1,0:T(8,128)S(1)} %get-tuple-element.44.stacked, f32[16,16]{1,0:T(8,128)S(1)} %copy-done), custom_call_target="tpu_custom_call" | custom-call | tf_op jit(solution)/shard_map/finish/pallas_call | solution.py:836
  (13 shorter events, 0.1 us)
Async XLA Ops:
  1.9 8.4 %collective-permute-start = (f32[4,8,128]{2,1,0:T(8,128)S(1)}, f32[4,8,128]{2,1,0:T(8,128)S(1)}, u32[]{:S(2)}, u32[]{:S(2)}) collective-permute-start(f32[4,8,128]{2,1,0:T(8,128)S(1)} %get-tuple-element.24), channel_id=1, source_target_pairs={{0,1},{1,2},{2,3},{3,4},{4,5},{5,6},{6,7},{7,8},{8,9},{9,10},{10,1... | collective-permute-start | bytes 49160 | tf_op jit(solution)/shard_map/ppermute | solution.py:754
  3.9 6.3 %collective-permute-start.1 = (f32[4,8,128]{2,1,0:T(8,128)S(1)}, f32[4,8,128]{2,1,0:T(8,128)S(1)}, u32[]{:S(2)}, u32[]{:S(2)}) collective-permute-start(f32[4,8,128]{2,1,0:T(8,128)S(1)} %get-tuple-element.26), channel_id=1, source_target_pairs={{0,15},{1,0},{2,1},{3,2},{4,3},{5,4},{6,5},{7,6},{8,7},{9,8},{10,9... | collective-permute-start | bytes 49160 | tf_op jit(solution)/shard_map/ppermute | solution.py:755
  10.3 5.6 %collective-permute-start.3 = (f32[4,144,128]{2,1,0:T(8,128)S(1)}, f32[4,144,128]{2,1,0:T(8,128)S(1)}, u32[]{:S(2)}, u32[]{:S(2)}) collective-permute-start(f32[4,144,128]{2,1,0:T(8,128)S(1)} %pad_maximum_fusion.own), channel_id=1, source_target_pairs={{0,112},{16,0},{32,16},{48,32},{64,48},{80,64},{96,80},{112,96},{1... | collective-permute-start | bytes 884744 | tf_op jit(solution)/shard_map/ppermute | solution.py:758
  11.6 7.4 %collective-permute-start.2 = (f32[4,144,128]{2,1,0:T(8,128)S(1)}, f32[4,144,128]{2,1,0:T(8,128)S(1)}, u32[]{:S(2)}, u32[]{:S(2)}) collective-permute-start(f32[4,144,128]{2,1,0:T(8,128)S(1)} %pad_maximum_fusion.own), channel_id=1, source_target_pairs={{0,16},{16,32},{32,48},{48,64},{64,80},{80,96},{96,112},{112,0},{1... | collective-permute-start | bytes 884744 | tf_op jit(solution)/shard_map/ppermute | solution.py:757
  11.6 0.7 copy-start.1
  12.3 0.7 copy-start.2
  13.0 0.7 copy-start.3
  48.2 8.5 %collective-permute-start.4 = (f32[2,8,128]{2,1,0:T(8,128)S(1)}, f32[2,8,128]{2,1,0:T(8,128)S(1)}, u32[]{:S(2)}, u32[]{:S(2)}) collective-permute-start(f32[2,8,128]{2,1,0:T(8,128)S(1)} %get-tuple-element.34), channel_id=1, source_target_pairs={{0,1},{1,2},{2,3},{3,4},{4,5},{5,6},{6,7},{7,8},{8,9},{9,10},{10,1... | collective-permute-start | bytes 24584 | tf_op jit(solution)/shard_map/ppermute | solution.py:797
  49.1 7.6 %collective-permute-start.5 = (f32[2,8,128]{2,1,0:T(8,128)S(1)}, f32[2,8,128]{2,1,0:T(8,128)S(1)}, u32[]{:S(2)}, u32[]{:S(2)}) collective-permute-start(f32[2,8,128]{2,1,0:T(8,128)S(1)} %get-tuple-element.37), channel_id=1, source_target_pairs={{0,15},{1,0},{2,1},{3,2},{4,3},{5,4},{6,5},{7,6},{8,7},{9,8},{10,9... | collective-permute-start | bytes 24584 | tf_op jit(solution)/shard_map/ppermute | solution.py:798
  56.8 2.7 %collective-permute-start.7 = (f32[2,144,128]{2,1,0:T(8,128)S(1)}, f32[2,144,128]{2,1,0:T(8,128)S(1)}, u32[]{:S(2)}, u32[]{:S(2)}) collective-permute-start(f32[2,144,128]{2,1,0:T(8,128)S(1)} %pad_maximum_fusion.1.misfit), channel_id=1, source_target_pairs={{0,112},{16,0},{32,16},{48,32},{64,48},{80,64},{96,80},{112,96},{1... | collective-permute-start | bytes 442376 | tf_op jit(solution)/shard_map/ppermute | solution.py:811
  56.8 5.8 %collective-permute-start.6 = (f32[2,144,128]{2,1,0:T(8,128)S(1)}, f32[2,144,128]{2,1,0:T(8,128)S(1)}, u32[]{:S(2)}, u32[]{:S(2)}) collective-permute-start(f32[2,144,128]{2,1,0:T(8,128)S(1)} %pad_maximum_fusion.1.misfit), channel_id=1, source_target_pairs={{0,16},{16,32},{32,48},{48,64},{64,80},{80,96},{96,112},{112,0},{1... | collective-permute-start | bytes 442376 | tf_op jit(solution)/shard_map/ppermute | solution.py:810
  62.6 35.8 %copy-start = (f32[16,16]{1,0:T(8,128)S(1)}, f32[16,16]{1,0:T(8,128)}, u32[]{:S(2)}) copy-start(f32[16,16]{1,0:T(8,128)} %beta_ref.1) | copy-start | bytes 3076

commit v7 on v6

--- a/solution.py
+++ b/solution.py
@@ -680,8 +680,10 @@
     mix = jnp.concatenate(
         [inverse * v for v in along] + [-dot(inverse, beta), -dot(inverse, alpha, last)], axis=1
     )
+    lanes = stacked.shape[2]
+    whole = dot(mix, jnp.concatenate([stacked[at] for at in range(stacked.shape[0])], axis=1))
     for at in range(stacked.shape[0]):
-        next_out[:, at, :] = dot(mix, stacked[at])
+        next_out[:, at, :] = whole[:, at * lanes : (at + 1) * lanes]
 
 
 def shards(

time: 102 us -> 102 us (level)
  no operation moved by 1% of the time
where the time goes in v7:
time: 102 us
  blocking collectives  38.7 us (38%)
  Pallas kernels  36.2 us (35%)
  starting transfers between devices  14 us (14%)
  waiting for transfers between devices  9.78 us (10%)
  local copies, waits for them, and re-layouts  2.06 us (2%)
    all_to_all x1, blocking collectives, shards(): lax.all_to_all(message, AXES, split_axis=0, concat_axis=0, tiled=True)  16.6 us
    pallas_call x1, Pallas kernels, shards(): pl.pallas_call(functools.partial(adjoint_kernel, vectors), out_shape=(nea...  13.7 us
    all_to_all x1, blocking collectives, shards(): lax.all_to_all(products, 'my', split_axis=0, concat_axis=0, tiled=True)  13.6 us
    pallas_call x1, Pallas kernels, shards(): pl.pallas_call(functools.partial(velocity_kernel, vectors), out_shape=(ne...  10.6 us
    ppermute x2, starting transfers between devices, shards(): from_high = lax.ppermute(low, 'my', backward_y)  9.17 us
    all_to_all x1, blocking collectives, shards(): lax.all_to_all(products, 'mx', split_axis=0, concat_axis=0, tiled=True)  8.52 us
    pallas_call x1, Pallas kernels, shards(): pl.pallas_call(functools.partial(finish_kernel, float(cells)), out_shape=...  3.25 us
    ppermute x1, waiting for transfers between devices, shards(): misfit_left = lax.ppermute(misfit, 'mx', forward_x)  3.12 us
  transfers between devices with their start and end apart: 8, of which 5 were waited for; matrix products, arithmetic and copies ran while one was open for 0% of the time, Pallas kernels for 5%

profile of v7, /device:TPU:0, one launch (start us, length us, event | category | flops | bytes accessed | tf_op | source)
XLA Modules:
  0.0 101.6 jit_solution(17540664612092614295)
XLA Ops:
  0.6 1.2 %pack.1 = (f32[4,128,128]{2,1,0:T(8,128)S(1)}, f32[128,128]{1,0:T(8,128)S(1)}, f32[4,8,128]{2,1,0:T(8,128)S(1)}, f32[4,8,128]{2,1,0:T(8,128)S(1)}) custom-call(f32[16,8,128]{2,1,0:T(8,128)} %block.1, f32[16,8,128]{2,1,0:T(8,128)} %previous.1, f32[8,128]{1,0:T(8,128)} %reaction.1, f32[15,8,128]{2,1,0:T(8,128)} %vert.1, f32[16,8,128]{2,1,0:T(8,128)} %horiz.1, ...), custom_call_target="tpu_custom_call" | custom-call | tf_op jit(solution)/shard_map/pack/pallas_call | solution.py:735
  1.9 2.1 %collective-permute-start = (f32[4,8,128]{2,1,0:T(8,128)S(1)}, f32[4,8,128]{2,1,0:T(8,128)S(1)}, u32[]{:S(2)}, u32[]{:S(2)}) collective-permute-start(f32[4,8,128]{2,1,0:T(8,128)S(1)} %get-tuple-element.24), channel_id=1, source_target_pairs={{0,1},{1,2},{2,3},{3,4},{4,5},{5,6},{6,7},{7,8},{8,9},{9,10},{10,1... | collective-permute-start | bytes 49160 | tf_op jit(solution)/shard_map/ppermute | solution.py:756
  3.9 4.7 %collective-permute-start.1 = (f32[4,8,128]{2,1,0:T(8,128)S(1)}, f32[4,8,128]{2,1,0:T(8,128)S(1)}, u32[]{:S(2)}, u32[]{:S(2)}) collective-permute-start(f32[4,8,128]{2,1,0:T(8,128)S(1)} %get-tuple-element.26), channel_id=1, source_target_pairs={{0,15},{1,0},{2,1},{3,2},{4,3},{5,4},{6,5},{7,6},{8,7},{9,8},{10,9... | collective-permute-start | bytes 49160 | tf_op jit(solution)/shard_map/ppermute | solution.py:757
  8.6 1.6 %collective-permute-done = f32[4,8,128]{2,1,0:T(8,128)S(1)} collective-permute-done((f32[4,8,128]{2,1,0:T(8,128)S(1)}, f32[4,8,128]{2,1,0:T(8,128)S(1)}, u32[]{:S(2)}, u32[]{:S(2)}) %collective-permute-start) | collective-permute-done | bytes 16416 | tf_op jit(solution)/shard_map/ppermute | solution.py:756
  10.2 0.0 collective-permute-done.1
  10.3 1.3 %collective-permute-start.3 = (f32[4,144,128]{2,1,0:T(8,128)S(1)}, f32[4,144,128]{2,1,0:T(8,128)S(1)}, u32[]{:S(2)}, u32[]{:S(2)}) collective-permute-start(f32[4,144,128]{2,1,0:T(8,128)S(1)} %pad_maximum_fusion.own), channel_id=1, source_target_pairs={{0,112},{16,0},{32,16},{48,32},{64,48},{80,64},{96,80},{112,96},{1... | collective-permute-start | bytes 884744 | tf_op jit(solution)/shard_map/ppermute | solution.py:760
  11.6 0.0 collective-permute-start.2
  11.6 0.7 copy-done.1
  12.3 0.7 copy-done.2
  13.0 0.7 copy-done.3
  13.7 0.9 table.1
  14.5 0.1 add_convert_fusion.flags.after
  14.6 1.2 %collective-permute-done.3.right = f32[4,144,128]{2,1,0:T(8,128)S(1)} collective-permute-done((f32[4,144,128]{2,1,0:T(8,128)S(1)}, f32[4,144,128]{2,1,0:T(8,128)S(1)}, u32[]{:S(2)}, u32[]{:S(2)}) %collective-permute-start.3) | collective-permute-done | bytes 294944 | tf_op jit(solution)/shard_map/ppermute | solution.py:760
  15.8 3.1 %collective-permute-done.2.left = f32[4,144,128]{2,1,0:T(8,128)S(1)} collective-permute-done((f32[4,144,128]{2,1,0:T(8,128)S(1)}, f32[4,144,128]{2,1,0:T(8,128)S(1)}, u32[]{:S(2)}, u32[]{:S(2)}) %collective-permute-start.2) | collective-permute-done | bytes 294944 | tf_op jit(solution)/shard_map/ppermute | solution.py:759
  19.0 2.1 %moments.1 = (f32[128,128]{1,0:T(8,128)S(1)}, f32[3,18,3,8,128]{4,3,2,1,0:T(8,128)S(1)}, f32[10,18,8,128]{3,2,1,0:T(8,128)S(1)}) custom-call(f32[2]{0:T(128)S(1)} %add_convert_fusion.flags.after, f32[4,144,128]{2,1,0:T(8,128)S(1)} %pad_maximum_fusion.own, f32[4,144,128]{2,1,0:T(8,128)S(1)} %collective-permute-done.2.left, ...), custom_call_target="tpu_custom_call" | custom-call | tf_op jit(solution)/shard_map/moments/pallas_call | solution.py:768
  21.1 16.6 %all_to_all.21 = f32[128,1,128]{2,1,0:T(1,128)S(1)} all-to-all(f32[128,1,128]{2,1,0:T(1,128)S(1)} %bitcast.10), channel_id=1, replica_groups=mesh['mx'=8,'my'=16] {'mx','my'}, dimensions={0} | all-to-all | bytes 131072 | tf_op jit(solution)/shard_map/all_to_all | solution.py:779
  37.7 10.6 %velocity.3 = (f32[2,128,128]{2,1,0:T(8,128)S(1)}, f32[2,8,128]{2,1,0:T(8,128)S(1)}, f32[2,8,128]{2,1,0:T(8,128)S(1)}) custom-call(f32[2]{0:T(128)S(1)} %add_convert_fusion.flags.after, f32[128,128]{1,0:T(8,128)S(1)} %bitcast.9, f32[3,18,3,8,128]{4,3,2,1,0:T(8,128)S(1)} %get-tuple-element.28.basis, f32[10,18,8,128]{3,2,1,0:T(8,128)S(1)} %get-tuple-element.29.fields), custom_call_target="tpu_custom_call" | custom-call | tf_op jit(solution)/shard_map/velocity/pallas_call | solution.py:789
  48.2 0.9 collective-permute-start.4
  49.1 4.5 %collective-permute-start.5 = (f32[2,8,128]{2,1,0:T(8,128)S(1)}, f32[2,8,128]{2,1,0:T(8,128)S(1)}, u32[]{:S(2)}, u32[]{:S(2)}) collective-permute-start(f32[2,8,128]{2,1,0:T(8,128)S(1)} %get-tuple-element.37), channel_id=1, source_target_pairs={{0,15},{1,0},{2,1},{3,2},{4,3},{5,4},{6,5},{7,6},{8,7},{9,8},{10,9... | collective-permute-start | bytes 24584 | tf_op jit(solution)/shard_map/ppermute | solution.py:800
  53.6 3.0 %spread.1 = (f32[10,18,8,1536]{3,2,1,0:T(8,128)S(1)}, f32[8,128]{1,0:T(8,128)S(1)}) custom-call(f32[2]{0:T(128)S(1)} %add_convert_fusion.flags.after, f32[10,18,8,128]{3,2,1,0:T(8,128)S(1)} %get-tuple-element.29.fields), custom_call_target="tpu_custom_call" | custom-call | tf_op jit(solution)/shard_map/spread/pallas_call | solution.py:801
  56.7 0.0 collective-permute-done.4
  56.7 0.0 collective-permute-done.5
  56.8 0.0 collective-permute-start.7
  56.8 0.5 collective-permute-start.6
  57.3 1.5 %columns.1 = (f32[16,18,3,8,128]{4,3,2,1,0:T(8,128)S(1)}, f32[16,18,3,8,128]{4,3,2,1,0:T(8,128)S(1)}) custom-call(f32[2]{0:T(128)S(1)} %add_convert_fusion.flags.after, f32[10,18,8,1536]{3,2,1,0:T(8,128)S(1)} %get-tuple-element.33.wide), custom_call_target="tpu_custom_call" | custom-call | tf_op jit(solution)/shard_map/columns/pallas_call | solution.py:815
  58.8 0.7 collective-permute-done.7.misfit_right
  59.5 3.1 %collective-permute-done.6.misfit_left = f32[2,144,128]{2,1,0:T(8,128)S(1)} collective-permute-done((f32[2,144,128]{2,1,0:T(8,128)S(1)}, f32[2,144,128]{2,1,0:T(8,128)S(1)}, u32[]{:S(2)}, u32[]{:S(2)}) %collective-permute-start.6) | collective-permute-done | bytes 147488 | tf_op jit(solution)/shard_map/ppermute | solution.py:812
  62.6 13.7 %adjoint.1 = (f32[8,16,256]{2,1,0:T(8,128)S(1)}, f32[8,80,128]{2,1,0:T(8,128)S(1)}) custom-call(f32[2]{0:T(128)S(1)} %add_convert_fusion.flags.after, f32[10,18,8,1536]{3,2,1,0:T(8,128)S(1)} %get-tuple-element.33.wide, f32[16,18,3,8,128]{4,3,2,1,0:T(8,128)S(1)} %get-tuple-element.39.bed_col, f32[16,18,3,8,128]{4,3,2,1,0:T(8,128)S(1)} %get-tuple-element.40.top_col, ...), custom_call_target="tpu_custom_call" | custom-call | tf_op jit(solution)/shard_map/adjoint/pallas_call | solution.py:823
  76.2 8.5 %all_to_all.22 = f32[8,16,256]{2,1,0:T(8,128)S(1)} all-to-all(f32[8,16,256]{2,1,0:T(8,128)S(1)} %get-tuple-element.43), channel_id=1, replica_groups=mesh['mx'=8,'my'=16] {'mx'}, dimensions={0} | all-to-all | bytes 262144 | tf_op jit(solution)/shard_map/all_to_all | solution.py:835
  84.8 13.6 %all_to_all.23.received = f32[16,16,256]{2,1,0:T(8,128)S(1)} all-to-all(f32[16,16,256]{2,1,0:T(8,128)S(1)} %broadcast_in_dim.2), channel_id=1, replica_groups=mesh['mx'=8,'my'=16] {'my'}, dimensions={0} | all-to-all | bytes 524288 | tf_op jit(solution)/shard_map/all_to_all | solution.py:837
  98.4 0.0 copy-done
  98.4 3.3 %finish.1 = (f32[16,8,128]{2,1,0:T(8,128)}, f32[16,16]{1,0:T(8,128)}, f32[16,16]{1,0:T(8,128)}) custom-call(f32[16,16,256]{2,1,0:T(8,128)S(1)} %all_to_all.23.received, f32[8,80,128]{2,1,0:T(8,128)S(1)} %get-tuple-element.44.stacked, f32[16,16]{1,0:T(8,128)S(1)} %copy-done), custom_call_target="tpu_custom_call" | custom-call | tf_op jit(solution)/shard_map/finish/pallas_call | solution.py:838
  (13 shorter events, 0.1 us)
Async XLA Ops:
  1.9 8.4 %collective-permute-start = (f32[4,8,128]{2,1,0:T(8,128)S(1)}, f32[4,8,128]{2,1,0:T(8,128)S(1)}, u32[]{:S(2)}, u32[]{:S(2)}) collective-permute-start(f32[4,8,128]{2,1,0:T(8,128)S(1)} %get-tuple-element.24), channel_id=1, source_target_pairs={{0,1},{1,2},{2,3},{3,4},{4,5},{5,6},{6,7},{7,8},{8,9},{9,10},{10,1... | collective-permute-start | bytes 49160 | tf_op jit(solution)/shard_map/ppermute | solution.py:756
  3.9 6.3 %collective-permute-start.1 = (f32[4,8,128]{2,1,0:T(8,128)S(1)}, f32[4,8,128]{2,1,0:T(8,128)S(1)}, u32[]{:S(2)}, u32[]{:S(2)}) collective-permute-start(f32[4,8,128]{2,1,0:T(8,128)S(1)} %get-tuple-element.26), channel_id=1, source_target_pairs={{0,15},{1,0},{2,1},{3,2},{4,3},{5,4},{6,5},{7,6},{8,7},{9,8},{10,9... | collective-permute-start | bytes 49160 | tf_op jit(solution)/shard_map/ppermute | solution.py:757
  10.3 5.6 %collective-permute-start.3 = (f32[4,144,128]{2,1,0:T(8,128)S(1)}, f32[4,144,128]{2,1,0:T(8,128)S(1)}, u32[]{:S(2)}, u32[]{:S(2)}) collective-permute-start(f32[4,144,128]{2,1,0:T(8,128)S(1)} %pad_maximum_fusion.own), channel_id=1, source_target_pairs={{0,112},{16,0},{32,16},{48,32},{64,48},{80,64},{96,80},{112,96},{1... | collective-permute-start | bytes 884744 | tf_op jit(solution)/shard_map/ppermute | solution.py:760
  11.6 7.4 %collective-permute-start.2 = (f32[4,144,128]{2,1,0:T(8,128)S(1)}, f32[4,144,128]{2,1,0:T(8,128)S(1)}, u32[]{:S(2)}, u32[]{:S(2)}) collective-permute-start(f32[4,144,128]{2,1,0:T(8,128)S(1)} %pad_maximum_fusion.own), channel_id=1, source_target_pairs={{0,16},{16,32},{32,48},{48,64},{64,80},{80,96},{96,112},{112,0},{1... | collective-permute-start | bytes 884744 | tf_op jit(solution)/shard_map/ppermute | solution.py:759
  11.6 0.7 copy-start.1
  12.3 0.7 copy-start.2
  13.0 0.7 copy-start.3
  48.2 8.5 %collective-permute-start.4 = (f32[2,8,128]{2,1,0:T(8,128)S(1)}, f32[2,8,128]{2,1,0:T(8,128)S(1)}, u32[]{:S(2)}, u32[]{:S(2)}) collective-permute-start(f32[2,8,128]{2,1,0:T(8,128)S(1)} %get-tuple-element.34), channel_id=1, source_target_pairs={{0,1},{1,2},{2,3},{3,4},{4,5},{5,6},{6,7},{7,8},{8,9},{9,10},{10,1... | collective-permute-start | bytes 24584 | tf_op jit(solution)/shard_map/ppermute | solution.py:799
  49.1 7.6 %collective-permute-start.5 = (f32[2,8,128]{2,1,0:T(8,128)S(1)}, f32[2,8,128]{2,1,0:T(8,128)S(1)}, u32[]{:S(2)}, u32[]{:S(2)}) collective-permute-start(f32[2,8,128]{2,1,0:T(8,128)S(1)} %get-tuple-element.37), channel_id=1, source_target_pairs={{0,15},{1,0},{2,1},{3,2},{4,3},{5,4},{6,5},{7,6},{8,7},{9,8},{10,9... | collective-permute-start | bytes 24584 | tf_op jit(solution)/shard_map/ppermute | solution.py:800
  56.8 2.7 %collective-permute-start.7 = (f32[2,144,128]{2,1,0:T(8,128)S(1)}, f32[2,144,128]{2,1,0:T(8,128)S(1)}, u32[]{:S(2)}, u32[]{:S(2)}) collective-permute-start(f32[2,144,128]{2,1,0:T(8,128)S(1)} %pad_maximum_fusion.1.misfit), channel_id=1, source_target_pairs={{0,112},{16,0},{32,16},{48,32},{64,48},{80,64},{96,80},{112,96},{1... | collective-permute-start | bytes 442376 | tf_op jit(solution)/shard_map/ppermute | solution.py:813
  56.8 5.8 %collective-permute-start.6 = (f32[2,144,128]{2,1,0:T(8,128)S(1)}, f32[2,144,128]{2,1,0:T(8,128)S(1)}, u32[]{:S(2)}, u32[]{:S(2)}) collective-permute-start(f32[2,144,128]{2,1,0:T(8,128)S(1)} %pad_maximum_fusion.1.misfit), channel_id=1, source_target_pairs={{0,16},{16,32},{32,48},{48,64},{64,80},{80,96},{96,112},{112,0},{1... | collective-permute-start | bytes 442376 | tf_op jit(solution)/shard_map/ppermute | solution.py:812
  62.6 35.8 %copy-start = (f32[16,16]{1,0:T(8,128)S(1)}, f32[16,16]{1,0:T(8,128)}, u32[]{:S(2)}) copy-start(f32[16,16]{1,0:T(8,128)} %beta_ref.1) | copy-start | bytes 3076
